TPU v7x, 1024 devices: a whole 4x4x32 slice. The times are simulated.
1024 devices in a mesh: grp: 64 (over z, core), rep: 16 (over y, x).
Axes of the slice: x: 4, y: 4, z: 32, core: 2. Of those that a mesh axis runs over, the one named last changes fastest.
Arguments:
- user_factors: float32 [131072, 256], P(('grp', 'rep'))
- item_factors: float32 [524288, 256], P(('grp', 'rep')), may hold values from -3 to 3
- tile_users: int32 [65536], P(('grp', 'rep')), may hold values from 0 to 2047, as said below
- tile_counts: int32 [65536, 64, 128], P(('grp', 'rep')), may hold values from 0 to 5
Outputs:
- item_solution: float32 [524288, 256], P(('grp', 'rep'))
Inputs may be any that keep to these rules, and one draw needn't show every extreme that they name: `tile_users`: users and items are laid out in 64 x 16 equal shards in the order of the mesh (grp slowest). Every tile names a row block of the shard with the same rep index as its own shard, and all tiles of one shard that name blocks of one user shard name the same block. The first tile of every shard names a block of the shard whose grp index is 32 away, counted round.
All inputs are finite; a program needn't handle non-finite values.
Results may differ from a plain program's by a relative error of at most 0.0026.
Values may be sent and summed in bfloat16 or wider, within the bound.
No kernel may reach another device: no remote copies, remote signals or barrier semaphores. Data moves between devices by JAX's collectives and lax.ppermute only.
A program may use at most 32 MiB of HBM per device.

v0:
```python
import jax
import jax.numpy as jnp
from jax import lax
from jax.sharding import PartitionSpec as P

UROWS = 64
IBLK = 128
ITERS = 3


ALPHA = 8.0
LAMBDA = 1.0
EPSILON = 1e-06


def on_device(user_factors, item_factors, tile_users, tile_counts):
    highest = lax.Precision.HIGHEST
    replicas = lax.axis_size("rep")
    features = user_factors.shape[1]
    owned_blocks = user_factors.shape[0] // UROWS
    user_half = user_factors.astype(jnp.bfloat16).reshape(owned_blocks, UROWS, features)
    partial_gram = jnp.dot(
        user_factors.T, user_factors, precision=highest, preferred_element_type=jnp.float32
    )
    gram_total = lax.psum(partial_gram, ("grp", "rep"))
    holder = tile_users // owned_blocks // replicas
    within = tile_users % owned_blocks
    group_rows = lax.all_gather(user_half, "grp", axis=0, tiled=True)
    tile_rows = group_rows[holder * owned_blocks + within]
    tile_total = tile_users.shape[0]
    item_blocks = item_factors.shape[0] // IBLK
    per_block = tile_total // item_blocks
    block_rows = tile_rows.reshape(item_blocks, per_block, UROWS, features)
    counts = tile_counts.reshape(item_blocks, per_block, UROWS, IBLK)
    confidence = jnp.where(counts > 0, 1.0 + ALPHA * counts.astype(jnp.float32), 0.0).astype(
        jnp.bfloat16
    )
    target = jnp.einsum(
        "bsui,bsuk->bik", confidence, block_rows, preferred_element_type=jnp.float32
    ).reshape(-1, features)

    def operate(direction):
        rounded = direction.astype(jnp.bfloat16).reshape(item_blocks, IBLK, features)
        scores = jnp.einsum(
            "bsuk,bik->bsui", block_rows, rounded, preferred_element_type=jnp.float32
        )
        mixed_terms = (ALPHA * counts.astype(jnp.float32) * scores).astype(jnp.bfloat16)
        tile_part = jnp.einsum(
            "bsui,bsuk->bik", mixed_terms, block_rows, preferred_element_type=jnp.float32
        )
        gram_part = jnp.dot(
            direction, gram_total, precision=highest, preferred_element_type=jnp.float32
        )
        return gram_part + LAMBDA * direction + tile_part.reshape(-1, features)

    solution = item_factors
    residue = target - operate(solution)
    direction = residue
    current = jnp.sum(residue * residue, axis=1, keepdims=True)
    for iteration in range(ITERS):
        applied = operate(direction)
        step_size = current / (jnp.sum(direction * applied, axis=1, keepdims=True) + EPSILON)
        solution = solution + step_size * direction
        residue = residue - step_size * applied
        following = jnp.sum(residue * residue, axis=1, keepdims=True)
        direction = residue + following / (current + EPSILON) * direction
        current = following
    return solution


def solution(mesh):
    in_specs = (
        P(("grp", "rep"), None),
        P(("grp", "rep"), None),
        P(("grp", "rep")),
        P(("grp", "rep"), None, None),
    )
    out_specs = P(("grp", "rep"), None)
    return jax.shard_map(
        on_device, mesh=mesh, in_specs=in_specs, out_specs=out_specs, check_vma=False
    )
```

profile of v0, /device:TPU:1, one launch (start us, length us, event | category | flops | bytes accessed | tf_op | source)
XLA Modules:
  0.0 929.4 jit_solution(38162177743685819)
XLA Ops:
  7.4 0.0 copy-start
  7.4 0.0 all-gather.2.cloned.1.call-start
  7.4 1.7 convert_element_type.40
  9.1 0.0 all-gather.2.cloned.1.call-update
  9.1 0.0 all-reduce.2.cloned.1.call-start
  9.1 2.1 fusion.27
  11.2 0.0 all-reduce.2.cloned.1.call-update
  11.3 1.1 convert_element_type.41
  12.3 0.0 copy-done.3
  12.4 1.0 copy.20
  13.4 0.0 copy-done
  13.4 0.3 broadcast_compare_fusion
  13.7 0.0 copy-start.7
  13.7 1.6 convert_multiply_fusion
  15.2 0.0 copy-done.7
  15.3 143.9 %all-gather.2.cloned.1.call-done = bf16[128,64,256]{2,1,0:T(8,128)(2,1)} async-done(((bf16[2,64,256]{2,1,0:T(8,128)(2,1)}), bf16[128,64,256]{2,1,0:T(8,128)(2,1)}) %all-gather.2.cloned.1.call-update) | async-done | bytes 4194320 | tf_op jit(solution)/shard_map/all_gather | solution.py:28
  159.2 2.9 gather_fusion
  162.0 3.4 fusion
  165.4 3.0 fusion.12
  168.4 2.0 copy.17
  170.5 2.0 copy.36
  172.5 721.1 %all-reduce.2.cloned.1.call-done = f32[256,256]{1,0:T(8,128)} async-done(((f32[256,256]{1,0:T(8,128)}), f32[256,256]{1,0:T(8,128)}) %all-reduce.2.cloned.1.call-update) | async-done | bytes 262160 | tf_op jit(solution)/shard_map/psum | solution.py:25
  893.6 2.5 fusion.26
  896.1 0.1 reshape.102
  896.2 0.0 copy-start.6
  896.2 3.4 fusion.1
  899.6 1.2 copy.37
  900.9 0.0 copy-done.6
  900.9 0.7 multiply_reduce_fusion.3
  901.7 0.1 multiply_reduce_fusion.2
  901.8 1.0 fusion.25
  902.8 1.7 reshape.104
  904.5 3.5 fusion.2
  908.0 2.1 copy.38
  910.0 0.0 copy-start.1
  910.0 2.1 multiply_reduce_fusion.1
  912.2 0.1 multiply_reduce_fusion
  912.3 0.0 copy-done.1
  912.3 1.1 fusion.24
  913.4 1.7 reshape.106
  915.1 3.5 fusion.3
  918.7 1.3 copy.39
  920.0 0.0 copy-done.4
  920.0 0.7 fusion.11
  920.7 0.0 copy-done.2
  920.7 0.0 copy-done.5
  920.7 0.2 multiply_add_fusion
  921.0 1.0 copy.24
  (11 shorter events, 0.1 us)
Async XLA Ops:
  7.4 5.0 copy-start.3
  7.4 6.0 copy-start
  7.4 151.8 %all-gather.2.cloned.1.call-start = ((), (), s32[]{:S(2)}) async-start(), calls=%async_computation | async-start | bytes 4259840 | tf_op jit(solution)/shard_map/all_gather | solution.py:28
  9.1 884.5 %all-reduce.2.cloned.1.call-start = ((), (), s32[]{:S(2)}) async-start(), calls=%async_computation.1 | async-start | bytes 524288 | tf_op jit(solution)/shard_map/psum | solution.py:25
  13.7 1.6 copy-start.7
  896.2 4.7 copy-start.6
  910.0 2.3 copy-start.1
  915.1 4.9 copy-start.4
  918.6 2.1 copy-start.2
  918.7 2.1 copy-start.5
Sparse Core Ops, SparseCore 0:
  10.9 148.2 all-gather.1
Sparse Core Ops, SparseCore 1:
  15.0 878.6 all-reduce.1
where the time goes:
time: 931 us; the launch traced here: 929 us
  waiting for transfers between devices  865 us (93%)
  matrix products  25 us (3%)
  local copies, waits for them, and re-layouts  17.1 us (2%)
  between operations  15 us (2%)
    psum x1, waiting for transfers between devices, on_device(): gram_total = lax.psum(partial_gram, ('grp', 'rep'))  721 us
    all_gather x1, waiting for transfers between devices, on_device(): group_rows = lax.all_gather(user_half, 'grp', axis=0, tiled=True)  144 us
  transfers between devices with their start and end apart: 2, of which 2 were waited for; matrix products, arithmetic and copies ran while one was open for 2% of the time, Pallas kernels for 0%

commit v1 on v0

v1 whole, which is shorter than its diff:
```python
import functools

import jax
import jax.numpy as jnp
import numpy as np
from jax import lax
from jax.experimental import pallas as pl
from jax.experimental.pallas import tpu as pltpu
from jax.sharding import PartitionSpec as P

UROWS = 64
IBLK = 128
ITERS = 3
CORES = 2
STRIDE = 8
CHUNK = 256

ALPHA = 8.0
LAMBDA = 1.0
EPSILON = 1e-06


def chip_shift(value, chips, distance):
    pairs = [
        (CORES * chip + core, CORES * ((chip + distance) % chips) + core)
        for chip in range(chips)
        for core in range(CORES)
    ]
    return lax.ppermute(value, "grp", pairs)


def core_swap(value, chips):
    pairs = [(CORES * chip + core, CORES * chip + 1 - core) for chip in range(chips) for core in range(CORES)]
    return lax.ppermute(value, "grp", pairs)


def slot_table(chips):
    pack_slot = {0: 0, chips - STRIDE: 1, STRIDE: 2, 2 * STRIDE: 3}
    table = np.full((chips,), -1, np.int32)
    for pack, offset in enumerate([0, -1, -2, -3, 1, 2, 3]):
        for ahead, slot in pack_slot.items():
            table[(offset + ahead) % chips] = 4 * pack + slot
    for slot, ahead in enumerate([-4 - STRIDE, -4 + STRIDE, 4 - STRIDE, 4 + STRIDE]):
        table[ahead % chips] = 28 + slot
    assert (table >= 0).all()
    return table


def gram_kernel(users_ref, gram_ref):
    users = users_ref[...]
    high = users.astype(jnp.bfloat16)
    low = (users - high.astype(jnp.float32)).astype(jnp.bfloat16)
    dims = (((0,), (0,)), ((), ()))
    product = functools.partial(lax.dot_general, dimension_numbers=dims, preferred_element_type=jnp.float32)
    gram_ref[...] = product(high, high) + (product(high, low) + product(low, high))


def local_gram(users):
    features = users.shape[1]
    return pl.pallas_call(
        gram_kernel,
        out_shape=jax.ShapeDtypeStruct((features, features), jnp.float32),
        in_specs=[pl.BlockSpec(memory_space=pltpu.VMEM)],
        out_specs=pl.BlockSpec(memory_space=pltpu.VMEM),
    )(users)


def solve_kernel(
    tiles_ref, slots_ref, place_ref, near_ref, other_ref, near_last_ref, other_last_ref, counts_ref, items_ref,
    gram_ref, out_ref, rows_ref, turned_ref, weight_ref, high_ref, low_ref, guess_ref, residue_ref, direction_ref,
    applied_ref,
):
    tile_total = counts_ref.shape[0]
    features, items = guess_ref.shape
    blocks = items // IBLK
    depth = rows_ref.shape[0] // blocks
    chips = slots_ref.shape[0]
    replicas, owned = place_ref[2], place_ref[3]
    near_blocks = near_ref.shape[0] // UROWS

    def fetch(tile, carry):
        block = tiles_ref[tile]
        within = lax.rem(block, owned)
        member = lax.div(lax.div(block, owned), replicas)
        chip, core = lax.div(member, CORES), lax.rem(member, CORES)
        ahead = lax.rem(chip - place_ref[0] + chips, chips)
        place = slots_ref[ahead] * owned + within
        last = place >= near_blocks
        mine = core == place_ref[1]
        to = pl.ds(pl.multiple_of(tile * UROWS, UROWS), UROWS)
        at = pl.ds(pl.multiple_of(place * UROWS, UROWS), UROWS)
        at_last = pl.ds(pl.multiple_of((place - near_blocks) * UROWS, UROWS), UROWS)

        @pl.when(mine & ~last)
        def _():
            rows_ref[to, :] = near_ref[at, :]

        @pl.when(~mine & ~last)
        def _():
            rows_ref[to, :] = other_ref[at, :]

        @pl.when(mine & last)
        def _():
            rows_ref[to, :] = near_last_ref[at_last, :]

        @pl.when(~mine & last)
        def _():
            rows_ref[to, :] = other_last_ref[at_last, :]

        return carry

    lax.fori_loop(0, tile_total, fetch, 0)

    gram = gram_ref[...]
    gram_high = gram.astype(jnp.bfloat16)
    high_ref[...] = gram_high
    low_ref[...] = (gram - gram_high.astype(jnp.float32)).astype(jnp.bfloat16)

    def dot(left, right):
        return jnp.dot(left, right, preferred_element_type=jnp.float32)

    def columns(block):
        return slice(block * IBLK, (block + 1) * IBLK)

    def operate(vector, block):
        high = vector.astype(jnp.bfloat16)
        low = (vector - high.astype(jnp.float32)).astype(jnp.bfloat16)
        total = vector * LAMBDA + dot(high_ref[...], high) + (dot(low_ref[...], high) + dot(high_ref[...], low))
        for start in range(0, depth, CHUNK):
            span = slice(block * depth + start, block * depth + start + CHUNK)
            scores = dot(rows_ref[span, :], high)
            mixed = (weight_ref[span, :] * scores).astype(jnp.bfloat16)
            total = total + dot(turned_ref[block, :, start : start + CHUNK], mixed)
        return total

    per_block = tile_total // blocks
    squares = []
    for block in range(blocks):
        turned_ref[block] = rows_ref[block * depth : (block + 1) * depth, :].T
        target = jnp.zeros((features, IBLK), jnp.float32)
        for start in range(0, depth, CHUNK):
            span = slice(block * depth + start, block * depth + start + CHUNK)
            first = block * per_block + start // UROWS
            counts = counts_ref[first : first + CHUNK // UROWS].reshape(CHUNK, IBLK).astype(jnp.float32)
            weight = ALPHA * counts
            weight_ref[span, :] = weight
            confidence = jnp.where(counts > 0, 1.0 + weight, 0.0).astype(jnp.bfloat16)
            target = target + dot(turned_ref[block, :, start : start + CHUNK], confidence)
        guess = items_ref[columns(block), :].T
        guess_ref[:, columns(block)] = guess
        residue = target - operate(guess, block)
        residue_ref[:, columns(block)] = residue
        direction_ref[:, columns(block)] = residue
        squares.append(jnp.sum(residue * residue, axis=0, keepdims=True))

    def step(iteration, squares):
        nexts = []
        for block in range(blocks):
            applied_ref[:, columns(block)] = operate(direction_ref[:, columns(block)], block)
        for block in range(blocks):
            current = squares[block]
            direction = direction_ref[:, columns(block)]
            applied = applied_ref[:, columns(block)]
            size = current / (jnp.sum(direction * applied, axis=0, keepdims=True) + EPSILON)
            guess_ref[:, columns(block)] += size * direction
            residue = residue_ref[:, columns(block)] - size * applied
            residue_ref[:, columns(block)] = residue
            following = jnp.sum(residue * residue, axis=0, keepdims=True)
            direction_ref[:, columns(block)] = residue + (following / (current + EPSILON)) * direction
            nexts.append(following)
        return tuple(nexts)

    lax.fori_loop(0, ITERS, step, tuple(squares))
    for block in range(blocks):
        out_ref[columns(block), :] = guess_ref[:, columns(block)].T


def solve(tile_users, slots, place, near, other, near_last, other_last, counts, items, gram):
    item_total, features = items.shape
    tile_total = counts.shape[0]
    depth = tile_total * UROWS
    blocks = item_total // IBLK
    state = pltpu.VMEM((features, item_total), jnp.float32)
    scalar, vector = pl.BlockSpec(memory_space=pltpu.SMEM), pl.BlockSpec(memory_space=pltpu.VMEM)
    return pl.pallas_call(
        solve_kernel,
        out_shape=jax.ShapeDtypeStruct(items.shape, jnp.float32),
        in_specs=[scalar] * 3 + [vector] * 7,
        out_specs=vector,
        scratch_shapes=[
            pltpu.VMEM((depth, features), jnp.bfloat16),
            pltpu.VMEM((blocks, features, depth // blocks), jnp.bfloat16),
            pltpu.VMEM((depth, IBLK), jnp.float32),
            pltpu.VMEM((features, features), jnp.bfloat16),
            pltpu.VMEM((features, features), jnp.bfloat16),
            state,
            state,
            state,
            state,
        ],
        compiler_params=pltpu.CompilerParams(vmem_limit_bytes=40 * 1024 * 1024),
    )(tile_users, slots, place, near, other, near_last, other_last, counts, items, gram)


def on_device(user_factors, item_factors, tile_users, tile_counts):
    chips = lax.axis_size("grp") // CORES
    replicas = lax.axis_size("rep")
    owned_rows, features = user_factors.shape
    share = features // replicas
    half = owned_rows // 2
    shift = functools.partial(chip_shift, chips=chips)
    bar = lax.optimization_barrier

    own = user_factors.astype(jnp.bfloat16)
    below, above = shift(own, distance=STRIDE), shift(own, distance=-STRIDE)
    pieces = lax.all_to_all(local_gram(user_factors), "rep", 0, 0, tiled=True)
    gram = jnp.sum(pieces.reshape(replicas, share, features), axis=0)
    below, above, gram = bar((below, above, gram))

    far_first, far_last = shift(below[:half], distance=STRIDE), shift(above[half:], distance=-STRIDE)
    gram = gram + core_swap(gram, chips)
    gram = gram + shift(gram, distance=STRIDE)
    far_first, far_last, gram = bar((far_first, far_last, gram))

    pack = jnp.concatenate([own, below, above, far_first, far_last])
    ups, downs = [pack], [pack]
    for hop in range(3):
        up, down = shift(ups[-1], distance=1), shift(downs[-1], distance=-1)
        if hop == 0:
            gram = gram + shift(gram, distance=2 * STRIDE)
        elif hop == 1:
            gram = gram + shift(gram, distance=1) + (shift(gram, distance=2) + shift(gram, distance=3))
        else:
            gram = gram + shift(gram, distance=4)
        up, down, gram = bar((up, down, gram))
        ups.append(up)
        downs.append(down)

    middle = slice(owned_rows, 3 * owned_rows)
    up, down = shift(ups[-1][middle], distance=1), shift(downs[-1][middle], distance=-1)
    near = jnp.concatenate(ups + downs[1:])
    other = core_swap(near, chips)
    gram = lax.all_to_all(jnp.concatenate([gram] * replicas), "rep", 0, 0, tiled=True)
    up, down, other, gram = bar((up, down, other, gram))
    near_last = jnp.concatenate([up, down])
    other_last = core_swap(near_last, chips)

    member = lax.axis_index("grp")
    place = jnp.stack([member // CORES, member % CORES, replicas, owned_rows // UROWS]).astype(jnp.int32)
    slots = jnp.asarray(slot_table(chips))
    return solve(
        tile_users, slots, place, near, other, near_last, other_last, tile_counts, item_factors, gram
    )


def solution(mesh):
    in_specs = (
        P(("grp", "rep"), None),
        P(("grp", "rep"), None),
        P(("grp", "rep")),
        P(("grp", "rep"), None, None),
    )
    out_specs = P(("grp", "rep"), None)
    return jax.shard_map(
        on_device, mesh=mesh, in_specs=in_specs, out_specs=out_specs, check_vma=False
    )
```

time: 931 us -> 204 us (0.22)
  waiting for transfers between devices: 865 us -> 53.9 us
  starting transfers between devices: 0.05 us -> 120 us
  matrix products: 25 us -> 0 us
  Pallas kernels: 0 us -> 19.2 us
  between operations: 15 us -> 0.47 us
    psum x1 -> x0, waiting for transfers between devices: 721 us -> none  [on_device(): gram_total = lax.psum(partial_gram, ('grp', 'rep'))]
    all_gather x1 -> x0, waiting for transfers between devices: 144 us -> none  [on_device(): group_rows = lax.all_gather(user_half, 'grp', axis=0, tiled=True)]
    ppermute x0 -> x21, starting transfers between devices: none -> 106 us  [the longest x18 82.1 us: chip_shift(): return lax.ppermute(value, 'grp', pairs)]
    ppermute x0 -> x21, waiting for transfers between devices: none -> 53.8 us  [the longest x18 52.8 us: chip_shift(): return lax.ppermute(value, 'grp', pairs)]
    dot_general x10 -> x0, matrix products: 25 us -> none  [the longest x4 13.8 us: operate(): jnp.einsum('bsui,bsuk->bik', mixed_terms, block_rows, preferred_element_t...]
    pallas_call x0 -> x2, Pallas kernels: none -> 19.2 us  [the longest x1 17.3 us: solve(): pl.pallas_call(solve_kernel, out_shape=jax.ShapeDtypeStruct(items.shape,...]
    all_to_all x0 -> x2, starting transfers between devices: none -> 13.3 us  [the longest x1 7.58 us: on_device(): pieces = lax.all_to_all(local_gram(user_factors), 'rep', 0, 0, tiled=True)]
    reshape x8 -> x0, local copies, waits for them, and re-layouts: 12.2 us -> none  [the longest x4 6.65 us: operate(): return gram_part + LAMBDA * direction + tile_part.reshape(-1, features)]
  transfers between devices with their start and end apart: 2 -> 23, of which waited for: 2 -> 9; matrix products, arithmetic and copies ran while one was open for 2% -> 2% of each run, Pallas kernels for 0% -> 0%
where the time goes in v1:
time: 204 us; the launch traced here: 203 us
  starting transfers between devices  120 us (59%)
  waiting for transfers between devices  53.9 us (26%)
  Pallas kernels  19.2 us (9%)
  local copies, waits for them, and re-layouts  8.31 us (4%)
    ppermute x18, starting transfers between devices, chip_shift(): return lax.ppermute(value, 'grp', pairs)  82.1 us
    ppermute x18, waiting for transfers between devices, chip_shift(): return lax.ppermute(value, 'grp', pairs)  52.8 us
    ppermute x3, starting transfers between devices, core_swap(): return lax.ppermute(value, 'grp', pairs)  24.3 us
    pallas_call x1, Pallas kernels, solve(): pl.pallas_call(solve_kernel, out_shape=jax.ShapeDtypeStruct(items.shape,...  17.3 us
    all_to_all x1, starting transfers between devices, on_device(): pieces = lax.all_to_all(local_gram(user_factors), 'rep', 0, 0, tiled=True)  7.58 us
    unnamed x35, local copies, waits for them, and re-layouts  6.94 us
    all_to_all x1, starting transfers between devices, on_device(): lax.all_to_all(jnp.concatenate([gram] * replicas), 'rep', 0, 0, tiled=True)  5.74 us
  transfers between devices with their start and end apart: 23, of which 9 were waited for; matrix products, arithmetic and copies ran while one was open for 2% of the time, Pallas kernels for 0%

profile of v1, /device:TPU:1, one launch (start us, length us, event | category | flops | bytes accessed | tf_op | source)
XLA Modules:
  0.0 202.6 jit_solution(3850636005041872935)
XLA Ops:
  0.0 1.9 shard_map.55
  1.9 7.6 %all-to-all-start = ((f32[16,16,256]{2,1,0:T(8,128)}), f32[16,16,256]{2,1,0:T(8,128)S(1)}, u32[]{:S(2)}, u32[]{:S(2)}) async-start(f32[16,16,256]{2,1,0:T(8,128)} %bitcast.6), calls=%async_computation | async-start | bytes 524288 | tf_op jit(solution)/shard_map/all_to_all | solution.py:216
  9.5 0.9 constant_dynamic-update-slice_fusion.4
  10.4 22.7 %collective-permute-start.1 = (bf16[128,256]{1,0:T(8,128)(2,1)S(1)}, bf16[128,256]{1,0:T(8,128)(2,1)S(1)}, u32[]{:S(2)}, u32[]{:S(2)}) collective-permute-start(bf16[128,256]{1,0:T(8,128)(2,1)S(1)} %get-tuple-element.44), channel_id=1, source_target_pairs={{0,768},{16,784},{32,800},{48,816},{64,832},{80,848},{96,864},{112... | collective-permute-start | bytes 196616 | tf_op jit(solution)/shard_map/ppermute | solution.py:29
  33.1 1.9 collective-permute-start
  35.1 0.6 constant_dynamic-update-slice_fusion.15
  35.7 11.7 %collective-permute-done = bf16[128,256]{1,0:T(8,128)(2,1)S(1)} collective-permute-done((bf16[128,256]{1,0:T(8,128)(2,1)S(1)}, bf16[128,256]{1,0:T(8,128)(2,1)S(1)}, u32[]{:S(2)}, u32[]{:S(2)}) %collective-permute-start) | collective-permute-done | bytes 65568 | tf_op jit(solution)/shard_map/ppermute | solution.py:29
  47.4 12.1 %collective-permute-start.4 = (f32[16,256]{1,0:T(8,128)S(1)}, f32[16,256]{1,0:T(8,128)S(1)}, u32[]{:S(2)}, u32[]{:S(2)}) collective-permute-start(f32[16,256]{1,0:T(8,128)S(1)} %reduce_sum.9), channel_id=1, source_target_pairs={{0,16},{16,0},{32,48},{48,32},{64,80},{80,64},{96,112},{112,96},{1... | collective-permute-start | bytes 49160 | tf_op jit(solution)/shard_map/ppermute | solution.py:34
  59.5 4.0 %collective-permute-start.3 = (bf16[64,256]{1,0:T(8,128)(2,1)S(1)}, bf16[64,256]{1,0:T(8,128)(2,1)S(1)}, u32[]{:S(2)}, u32[]{:S(2)}) collective-permute-start(bf16[64,256]{1,0:T(8,128)(2,1)S(1)} %slice.13), channel_id=1, source_target_pairs={{0,768},{16,784},{32,800},{48,816},{64,832},{80,848},{96,864},{112... | collective-permute-start | bytes 98312 | tf_op jit(solution)/shard_map/ppermute | solution.py:29
  63.5 10.0 %collective-permute-start.2 = (bf16[64,256]{1,0:T(8,128)(2,1)S(1)}, bf16[64,256]{1,0:T(8,128)(2,1)S(1)}, u32[]{:S(2)}, u32[]{:S(2)}) collective-permute-start(bf16[64,256]{1,0:T(8,128)(2,1)S(1)} %slice.12), channel_id=1, source_target_pairs={{0,256},{16,272},{32,288},{48,304},{64,320},{80,336},{96,352},{112... | collective-permute-start | bytes 98312 | tf_op jit(solution)/shard_map/ppermute | solution.py:29
  73.5 0.6 constant_dynamic-update-slice_fusion.3
  74.2 1.9 collective-permute-start.5
  76.1 0.6 constant_dynamic-update-slice_fusion.2
  76.7 10.7 %collective-permute-done.5 = f32[16,256]{1,0:T(8,128)S(1)} collective-permute-done((f32[16,256]{1,0:T(8,128)S(1)}, f32[16,256]{1,0:T(8,128)S(1)}, u32[]{:S(2)}, u32[]{:S(2)}) %collective-permute-start.5) | collective-permute-done | bytes 16416 | tf_op jit(solution)/shard_map/ppermute | solution.py:29
  87.5 0.6 constant_dynamic-update-slice_fusion.1
  88.1 0.6 constant_dynamic-update-slice_fusion
  88.7 1.9 collective-permute-start.7
  90.6 3.4 %collective-permute-start.6 = (bf16[512,256]{1,0:T(8,128)(2,1)S(1)}, bf16[512,256]{1,0:T(8,128)(2,1)S(1)}, u32[]{:S(2)}, u32[]{:S(2)}) collective-permute-start(bf16[512,256]{1,0:T(8,128)(2,1)S(1)} %get-tuple-element.49), channel_id=1, source_target_pairs={{0,32},{16,48},{32,64},{48,80},{64,96},{80,112},{96,128},{112,144}... | collective-permute-start | bytes 786440 | tf_op jit(solution)/shard_map/ppermute | solution.py:29
  94.0 6.9 %collective-permute-start.8 = (f32[16,256]{1,0:T(8,128)S(1)}, f32[16,256]{1,0:T(8,128)S(1)}, u32[]{:S(2)}, u32[]{:S(2)}) collective-permute-start(f32[16,256]{1,0:T(8,128)S(1)} %add.28), channel_id=1, source_target_pairs={{0,512},{16,528},{32,544},{48,560},{64,576},{80,592},{96,608},{112... | collective-permute-start | bytes 49160 | tf_op jit(solution)/shard_map/ppermute | solution.py:29
  100.9 15.9 %collective-permute-done.8 = f32[16,256]{1,0:T(8,128)S(1)} collective-permute-done((f32[16,256]{1,0:T(8,128)S(1)}, f32[16,256]{1,0:T(8,128)S(1)}, u32[]{:S(2)}, u32[]{:S(2)}) %collective-permute-start.8) | collective-permute-done | bytes 16416 | tf_op jit(solution)/shard_map/ppermute | solution.py:29
  116.8 2.4 %collective-permute-start.9 = (bf16[512,256]{1,0:T(8,128)(2,1)S(1)}, bf16[512,256]{1,0:T(8,128)(2,1)S(1)}, u32[]{:S(2)}, u32[]{:S(2)}) collective-permute-start(bf16[512,256]{1,0:T(8,128)(2,1)S(1)} %collective-permute-done.6), channel_id=1, source_target_pairs={{0,32},{16,48},{32,64},{48,80},{64,96},{80,112},{96,128},{112,144}... | collective-permute-start | bytes 786440 | tf_op jit(solution)/shard_map/ppermute | solution.py:29
  119.2 4.1 %collective-permute-start.10 = (bf16[512,256]{1,0:T(8,128)(2,1)S(1)}, bf16[512,256]{1,0:T(8,128)(2,1)S(1)}, u32[]{:S(2)}, u32[]{:S(2)}) collective-permute-start(bf16[512,256]{1,0:T(8,128)(2,1)S(1)} %collective-permute-done.7), channel_id=1, source_target_pairs={{0,992},{16,1008},{32,0},{48,16},{64,32},{80,48},{96,64},{112,80},... | collective-permute-start | bytes 786440 | tf_op jit(solution)/shard_map/ppermute | solution.py:29
  123.3 4.2 %collective-permute-start.13 = (f32[16,256]{1,0:T(8,128)S(1)}, f32[16,256]{1,0:T(8,128)S(1)}, u32[]{:S(2)}, u32[]{:S(2)}) collective-permute-start(f32[16,256]{1,0:T(8,128)S(1)} %add.29), channel_id=1, source_target_pairs={{0,96},{16,112},{32,128},{48,144},{64,160},{80,176},{96,192},{112,... | collective-permute-start | bytes 49160 | tf_op jit(solution)/shard_map/ppermute | solution.py:29
  127.5 1.9 collective-permute-start.12
  129.5 3.1 %collective-permute-start.11 = (f32[16,256]{1,0:T(8,128)S(1)}, f32[16,256]{1,0:T(8,128)S(1)}, u32[]{:S(2)}, u32[]{:S(2)}) collective-permute-start(f32[16,256]{1,0:T(8,128)S(1)} %add.29), channel_id=1, source_target_pairs={{0,32},{16,48},{32,64},{48,80},{64,96},{80,112},{96,128},{112,144}... | collective-permute-start | bytes 49160 | tf_op jit(solution)/shard_map/ppermute | solution.py:29
  132.6 1.5 collective-permute-done.12
  134.1 2.0 collective-permute-done.11
  136.1 1.9 collective-permute-start.14
  138.1 4.6 %collective-permute-start.15 = (bf16[512,256]{1,0:T(8,128)(2,1)S(1)}, bf16[512,256]{1,0:T(8,128)(2,1)S(1)}, u32[]{:S(2)}, u32[]{:S(2)}) collective-permute-start(bf16[512,256]{1,0:T(8,128)(2,1)S(1)} %collective-permute-done.10), channel_id=1, source_target_pairs={{0,992},{16,1008},{32,0},{48,16},{64,32},{80,48},{96,64},{112,80},... | collective-permute-start | bytes 786440 | tf_op jit(solution)/shard_map/ppermute | solution.py:29
  142.6 0.7 constant_dynamic-update-slice_fusion.10
  143.4 1.9 collective-permute-start.16
  145.3 0.7 constant_dynamic-update-slice_fusion.9
  146.0 6.0 %collective-permute-done.16 = f32[16,256]{1,0:T(8,128)S(1)} collective-permute-done((f32[16,256]{1,0:T(8,128)S(1)}, f32[16,256]{1,0:T(8,128)S(1)}, u32[]{:S(2)}, u32[]{:S(2)}) %collective-permute-start.16) | collective-permute-done | bytes 16416 | tf_op jit(solution)/shard_map/ppermute | solution.py:29
  152.1 0.7 constant_dynamic-update-slice_fusion.8
  152.9 0.7 constant_dynamic-update-slice_fusion.7
  153.6 0.7 constant_dynamic-update-slice_fusion.6
  154.3 0.7 constant_dynamic-update-slice_fusion.5.near_ref
  155.0 8.9 %collective-permute-start.19 = (bf16[3584,256]{1,0:T(8,128)(2,1)}, bf16[3584,256]{1,0:T(8,128)(2,1)}, u32[]{:S(2)}, u32[]{:S(2)}) collective-permute-start(bf16[3584,256]{1,0:T(8,128)(2,1)} %constant_dynamic-update-slice_fusion.5.near_ref), channel_id=1, source_target_pairs={{0,16},{16,0},{32,48},{48,32},{64,80},{80,64},{96,112},{112,96},{1... | collective-permute-start | bytes 5505032 | tf_op jit(solution)/shard_map/ppermute | solution.py:34
  164.1 0.7 copy-done.4
  164.8 5.7 %all-to-all-start.1 = ((f32[16,16,256]{2,1,0:T(8,128)}), f32[16,16,256]{2,1,0:T(8,128)S(1)}, u32[]{:S(2)}, u32[]{:S(2)}) async-start(f32[16,16,256]{2,1,0:T(8,128)} %bitcast.7), calls=%async_computation.1 | async-start | bytes 524288 | tf_op jit(solution)/shard_map/all_to_all | solution.py:243
  170.6 2.6 %collective-permute-start.18 = (bf16[256,256]{1,0:T(8,128)(2,1)S(1)}, bf16[256,256]{1,0:T(8,128)(2,1)S(1)}, u32[]{:S(2)}, u32[]{:S(2)}) collective-permute-start(bf16[256,256]{1,0:T(8,128)(2,1)S(1)} %slice.15), channel_id=1, source_target_pairs={{0,992},{16,1008},{32,0},{48,16},{64,32},{80,48},{96,64},{112,80},... | collective-permute-start | bytes 393224 | tf_op jit(solution)/shard_map/ppermute | solution.py:29
  173.2 2.7 %collective-permute-start.17 = (bf16[256,256]{1,0:T(8,128)(2,1)S(1)}, bf16[256,256]{1,0:T(8,128)(2,1)S(1)}, u32[]{:S(2)}, u32[]{:S(2)}) collective-permute-start(bf16[256,256]{1,0:T(8,128)(2,1)S(1)} %slice.14), channel_id=1, source_target_pairs={{0,32},{16,48},{32,64},{48,80},{64,96},{80,112},{96,128},{112,144}... | collective-permute-start | bytes 393224 | tf_op jit(solution)/shard_map/ppermute | solution.py:29
  175.9 1.4 collective-permute-done.18
  177.3 3.5 %collective-permute-done.17 = bf16[256,256]{1,0:T(8,128)(2,1)S(1)} collective-permute-done((bf16[256,256]{1,0:T(8,128)(2,1)S(1)}, bf16[256,256]{1,0:T(8,128)(2,1)S(1)}, u32[]{:S(2)}, u32[]{:S(2)}) %collective-permute-start.17) | collective-permute-done | bytes 131104 | tf_op jit(solution)/shard_map/ppermute | solution.py:29
  180.8 3.3 %collective-permute-start.20 = (bf16[512,256]{1,0:T(8,128)(2,1)S(1)}, bf16[512,256]{1,0:T(8,128)(2,1)S(1)}, u32[]{:S(2)}, u32[]{:S(2)}) collective-permute-start(bf16[512,256]{1,0:T(8,128)(2,1)S(1)} %constant_dynamic-update-slice_fusion.32.near_last_ref), channel_id=1, source_target_pairs={{0,16},{16,0},{32,48},{48,32},{64,80},{80,64},{96,112},{112,96},{1... | collective-permute-start | bytes 786440 | tf_op jit(solution)/shard_map/ppermute | solution.py:34
  184.2 0.1 pad_add_fusion.place_ref
  184.3 1.0 collective-permute-done.20.other_last_ref
  185.3 17.3 %shard_map.56 = f32[512,256]{1,0:T(8,128)} custom-call(s32[64]{0:T(128)S(1)} %copy-done.2, s32[32]{0:T(128)S(1)} %copy-done.3, s32[4]{0:T(128)S(1)} %pad_add_fusion.place_ref, bf16[3584,256]{1,0:T(8,128)(2,1)} %constant_dynamic-update-slice_fusion.5.near_ref, bf16[3584,256]{1,0:T(8,128)(2,1)} %collective-permute-done.19.other_ref, ...), custom_call_target="tpu_custom_call" | custom-call | tf_op jit(solution)/shard_map/pallas_call | solution.py:185
  (51 shorter events, 0.2 us)
Async XLA Ops:
  1.9 33.8 %all-to-all-start = ((f32[16,16,256]{2,1,0:T(8,128)}), f32[16,16,256]{2,1,0:T(8,128)S(1)}, u32[]{:S(2)}, u32[]{:S(2)}) async-start(f32[16,16,256]{2,1,0:T(8,128)} %bitcast.6), calls=%async_computation | async-start | bytes 524288 | tf_op jit(solution)/shard_map/all_to_all | solution.py:216
  10.4 25.3 %collective-permute-start.1 = (bf16[128,256]{1,0:T(8,128)(2,1)S(1)}, bf16[128,256]{1,0:T(8,128)(2,1)S(1)}, u32[]{:S(2)}, u32[]{:S(2)}) collective-permute-start(bf16[128,256]{1,0:T(8,128)(2,1)S(1)} %get-tuple-element.44), channel_id=1, source_target_pairs={{0,768},{16,784},{32,800},{48,816},{64,832},{80,848},{96,864},{112... | collective-permute-start | bytes 196616 | tf_op jit(solution)/shard_map/ppermute | solution.py:29
  33.1 14.3 %collective-permute-start = (bf16[128,256]{1,0:T(8,128)(2,1)S(1)}, bf16[128,256]{1,0:T(8,128)(2,1)S(1)}, u32[]{:S(2)}, u32[]{:S(2)}) collective-permute-start(bf16[128,256]{1,0:T(8,128)(2,1)S(1)} %get-tuple-element.44), channel_id=1, source_target_pairs={{0,256},{16,272},{32,288},{48,304},{64,320},{80,336},{96,352},{112... | collective-permute-start | bytes 196616 | tf_op jit(solution)/shard_map/ppermute | solution.py:29
  47.4 26.7 %collective-permute-start.4 = (f32[16,256]{1,0:T(8,128)S(1)}, f32[16,256]{1,0:T(8,128)S(1)}, u32[]{:S(2)}, u32[]{:S(2)}) collective-permute-start(f32[16,256]{1,0:T(8,128)S(1)} %reduce_sum.9), channel_id=1, source_target_pairs={{0,16},{16,0},{32,48},{48,32},{64,80},{80,64},{96,112},{112,96},{1... | collective-permute-start | bytes 49160 | tf_op jit(solution)/shard_map/ppermute | solution.py:34
  59.5 27.9 %collective-permute-start.3 = (bf16[64,256]{1,0:T(8,128)(2,1)S(1)}, bf16[64,256]{1,0:T(8,128)(2,1)S(1)}, u32[]{:S(2)}, u32[]{:S(2)}) collective-permute-start(bf16[64,256]{1,0:T(8,128)(2,1)S(1)} %slice.13), channel_id=1, source_target_pairs={{0,768},{16,784},{32,800},{48,816},{64,832},{80,848},{96,864},{112... | collective-permute-start | bytes 98312 | tf_op jit(solution)/shard_map/ppermute | solution.py:29
  63.5 24.0 %collective-permute-start.2 = (bf16[64,256]{1,0:T(8,128)(2,1)S(1)}, bf16[64,256]{1,0:T(8,128)(2,1)S(1)}, u32[]{:S(2)}, u32[]{:S(2)}) collective-permute-start(bf16[64,256]{1,0:T(8,128)(2,1)S(1)} %slice.12), channel_id=1, source_target_pairs={{0,256},{16,272},{32,288},{48,304},{64,320},{80,336},{96,352},{112... | collective-permute-start | bytes 98312 | tf_op jit(solution)/shard_map/ppermute | solution.py:29
  74.2 13.3 %collective-permute-start.5 = (f32[16,256]{1,0:T(8,128)S(1)}, f32[16,256]{1,0:T(8,128)S(1)}, u32[]{:S(2)}, u32[]{:S(2)}) collective-permute-start(f32[16,256]{1,0:T(8,128)S(1)} %add.27), channel_id=1, source_target_pairs={{0,256},{16,272},{32,288},{48,304},{64,320},{80,336},{96,352},{112... | collective-permute-start | bytes 49160 | tf_op jit(solution)/shard_map/ppermute | solution.py:29
  88.7 28.1 %collective-permute-start.7 = (bf16[512,256]{1,0:T(8,128)(2,1)S(1)}, bf16[512,256]{1,0:T(8,128)(2,1)S(1)}, u32[]{:S(2)}, u32[]{:S(2)}) collective-permute-start(bf16[512,256]{1,0:T(8,128)(2,1)S(1)} %get-tuple-element.49), channel_id=1, source_target_pairs={{0,992},{16,1008},{32,0},{48,16},{64,32},{80,48},{96,64},{112,80},... | collective-permute-start | bytes 786440 | tf_op jit(solution)/shard_map/ppermute | solution.py:29
  90.6 26.2 %collective-permute-start.6 = (bf16[512,256]{1,0:T(8,128)(2,1)S(1)}, bf16[512,256]{1,0:T(8,128)(2,1)S(1)}, u32[]{:S(2)}, u32[]{:S(2)}) collective-permute-start(bf16[512,256]{1,0:T(8,128)(2,1)S(1)} %get-tuple-element.49), channel_id=1, source_target_pairs={{0,32},{16,48},{32,64},{48,80},{64,96},{80,112},{96,128},{112,144}... | collective-permute-start | bytes 786440 | tf_op jit(solution)/shard_map/ppermute | solution.py:29
  94.0 22.8 %collective-permute-start.8 = (f32[16,256]{1,0:T(8,128)S(1)}, f32[16,256]{1,0:T(8,128)S(1)}, u32[]{:S(2)}, u32[]{:S(2)}) collective-permute-start(f32[16,256]{1,0:T(8,128)S(1)} %add.28), channel_id=1, source_target_pairs={{0,512},{16,528},{32,544},{48,560},{64,576},{80,592},{96,608},{112... | collective-permute-start | bytes 49160 | tf_op jit(solution)/shard_map/ppermute | solution.py:29
  116.8 19.3 %collective-permute-start.9 = (bf16[512,256]{1,0:T(8,128)(2,1)S(1)}, bf16[512,256]{1,0:T(8,128)(2,1)S(1)}, u32[]{:S(2)}, u32[]{:S(2)}) collective-permute-start(bf16[512,256]{1,0:T(8,128)(2,1)S(1)} %collective-permute-done.6), channel_id=1, source_target_pairs={{0,32},{16,48},{32,64},{48,80},{64,96},{80,112},{96,128},{112,144}... | collective-permute-start | bytes 786440 | tf_op jit(solution)/shard_map/ppermute | solution.py:29
  119.2 16.9 %collective-permute-start.10 = (bf16[512,256]{1,0:T(8,128)(2,1)S(1)}, bf16[512,256]{1,0:T(8,128)(2,1)S(1)}, u32[]{:S(2)}, u32[]{:S(2)}) collective-permute-start(bf16[512,256]{1,0:T(8,128)(2,1)S(1)} %collective-permute-done.7), channel_id=1, source_target_pairs={{0,992},{16,1008},{32,0},{48,16},{64,32},{80,48},{96,64},{112,80},... | collective-permute-start | bytes 786440 | tf_op jit(solution)/shard_map/ppermute | solution.py:29
  123.3 9.3 %collective-permute-start.13 = (f32[16,256]{1,0:T(8,128)S(1)}, f32[16,256]{1,0:T(8,128)S(1)}, u32[]{:S(2)}, u32[]{:S(2)}) collective-permute-start(f32[16,256]{1,0:T(8,128)S(1)} %add.29), channel_id=1, source_target_pairs={{0,96},{16,112},{32,128},{48,144},{64,160},{80,176},{96,192},{112,... | collective-permute-start | bytes 49160 | tf_op jit(solution)/shard_map/ppermute | solution.py:29
  127.5 6.6 %collective-permute-start.12 = (f32[16,256]{1,0:T(8,128)S(1)}, f32[16,256]{1,0:T(8,128)S(1)}, u32[]{:S(2)}, u32[]{:S(2)}) collective-permute-start(f32[16,256]{1,0:T(8,128)S(1)} %add.29), channel_id=1, source_target_pairs={{0,64},{16,80},{32,96},{48,112},{64,128},{80,144},{96,160},{112,17... | collective-permute-start | bytes 49160 | tf_op jit(solution)/shard_map/ppermute | solution.py:29
  129.5 6.6 %collective-permute-start.11 = (f32[16,256]{1,0:T(8,128)S(1)}, f32[16,256]{1,0:T(8,128)S(1)}, u32[]{:S(2)}, u32[]{:S(2)}) collective-permute-start(f32[16,256]{1,0:T(8,128)S(1)} %add.29), channel_id=1, source_target_pairs={{0,32},{16,48},{32,64},{48,80},{64,96},{80,112},{96,128},{112,144}... | collective-permute-start | bytes 49160 | tf_op jit(solution)/shard_map/ppermute | solution.py:29
  136.1 16.0 %collective-permute-start.14 = (bf16[512,256]{1,0:T(8,128)(2,1)S(1)}, bf16[512,256]{1,0:T(8,128)(2,1)S(1)}, u32[]{:S(2)}, u32[]{:S(2)}) collective-permute-start(bf16[512,256]{1,0:T(8,128)(2,1)S(1)} %collective-permute-done.9), channel_id=1, source_target_pairs={{0,32},{16,48},{32,64},{48,80},{64,96},{80,112},{96,128},{112,144}... | collective-permute-start | bytes 786440 | tf_op jit(solution)/shard_map/ppermute | solution.py:29
  138.1 14.0 %collective-permute-start.15 = (bf16[512,256]{1,0:T(8,128)(2,1)S(1)}, bf16[512,256]{1,0:T(8,128)(2,1)S(1)}, u32[]{:S(2)}, u32[]{:S(2)}) collective-permute-start(bf16[512,256]{1,0:T(8,128)(2,1)S(1)} %collective-permute-done.10), channel_id=1, source_target_pairs={{0,992},{16,1008},{32,0},{48,16},{64,32},{80,48},{96,64},{112,80},... | collective-permute-start | bytes 786440 | tf_op jit(solution)/shard_map/ppermute | solution.py:29
  143.4 8.7 %collective-permute-start.16 = (f32[16,256]{1,0:T(8,128)S(1)}, f32[16,256]{1,0:T(8,128)S(1)}, u32[]{:S(2)}, u32[]{:S(2)}) collective-permute-start(f32[16,256]{1,0:T(8,128)S(1)} %add_add_fusion), channel_id=1, source_target_pairs={{0,128},{16,144},{32,160},{48,176},{64,192},{80,208},{96,224},{112... | collective-permute-start | bytes 49160 | tf_op jit(solution)/shard_map/ppermute | solution.py:29
  152.8 32.5 %copy-start = (s32[64,64,128]{2,1,0:T(8,128)S(1)}, s32[64,64,128]{2,1,0:T(8,128)}, u32[]{:S(2)}) copy-start(s32[64,64,128]{2,1,0:T(8,128)} %counts_ref.1) | copy-start | bytes 6291460
  152.8 32.5 %copy-start.1 = (f32[512,256]{1,0:T(8,128)S(1)}, f32[512,256]{1,0:T(8,128)}, u32[]{:S(2)}) copy-start(f32[512,256]{1,0:T(8,128)} %items_ref.1) | copy-start | bytes 1572868
  152.8 32.5 %copy-start.2 = (s32[64]{0:T(128)S(1)}, s32[64]{0:T(128)}, u32[]{:S(2)}) copy-start(s32[64]{0:T(128)} %tiles_ref.1) | copy-start | bytes 772
  152.8 32.5 %copy-start.3 = (s32[32]{0:T(128)S(1)}, s32[32]{0:T(128)}, u32[]{:S(2)}) copy-start(s32[32]{0:T(128)} %constant.38.clone.slots_ref) | copy-start | bytes 388
  155.0 25.8 %collective-permute-start.19 = (bf16[3584,256]{1,0:T(8,128)(2,1)}, bf16[3584,256]{1,0:T(8,128)(2,1)}, u32[]{:S(2)}, u32[]{:S(2)}) collective-permute-start(bf16[3584,256]{1,0:T(8,128)(2,1)} %constant_dynamic-update-slice_fusion.5.near_ref), channel_id=1, source_target_pairs={{0,16},{16,0},{32,48},{48,32},{64,80},{80,64},{96,112},{112,96},{1... | collective-permute-start | bytes 5505032 | tf_op jit(solution)/shard_map/ppermute | solution.py:34
  164.1 0.7 copy-start.4
  164.8 16.0 %all-to-all-start.1 = ((f32[16,16,256]{2,1,0:T(8,128)}), f32[16,16,256]{2,1,0:T(8,128)S(1)}, u32[]{:S(2)}, u32[]{:S(2)}) async-start(f32[16,16,256]{2,1,0:T(8,128)} %bitcast.7), calls=%async_computation.1 | async-start | bytes 524288 | tf_op jit(solution)/shard_map/all_to_all | solution.py:243
  170.6 6.7 %collective-permute-start.18 = (bf16[256,256]{1,0:T(8,128)(2,1)S(1)}, bf16[256,256]{1,0:T(8,128)(2,1)S(1)}, u32[]{:S(2)}, u32[]{:S(2)}) collective-permute-start(bf16[256,256]{1,0:T(8,128)(2,1)S(1)} %slice.15), channel_id=1, source_target_pairs={{0,992},{16,1008},{32,0},{48,16},{64,32},{80,48},{96,64},{112,80},... | collective-permute-start | bytes 393224 | tf_op jit(solution)/shard_map/ppermute | solution.py:29
  173.2 7.6 %collective-permute-start.17 = (bf16[256,256]{1,0:T(8,128)(2,1)S(1)}, bf16[256,256]{1,0:T(8,128)(2,1)S(1)}, u32[]{:S(2)}, u32[]{:S(2)}) collective-permute-start(bf16[256,256]{1,0:T(8,128)(2,1)S(1)} %slice.14), channel_id=1, source_target_pairs={{0,32},{16,48},{32,64},{48,80},{64,96},{80,112},{96,128},{112,144}... | collective-permute-start | bytes 393224 | tf_op jit(solution)/shard_map/ppermute | solution.py:29
  180.8 4.5 %collective-permute-start.20 = (bf16[512,256]{1,0:T(8,128)(2,1)S(1)}, bf16[512,256]{1,0:T(8,128)(2,1)S(1)}, u32[]{:S(2)}, u32[]{:S(2)}) collective-permute-start(bf16[512,256]{1,0:T(8,128)(2,1)S(1)} %constant_dynamic-update-slice_fusion.32.near_last_ref), channel_id=1, source_target_pairs={{0,16},{16,0},{32,48},{48,32},{64,80},{80,64},{96,112},{112,96},{1... | collective-permute-start | bytes 786440 | tf_op jit(solution)/shard_map/ppermute | solution.py:34

commit v2 on v0

v2 whole, which is shorter than its diff:
```python
import functools

import jax
import jax.numpy as jnp
import numpy as np
from jax import lax
from jax.experimental import pallas as pl
from jax.experimental.pallas import tpu as pltpu
from jax.sharding import PartitionSpec as P

UROWS = 64
IBLK = 128
ITERS = 3
CORES = 2
STRIDE = 8
CHUNK = 256
PACK = 4
HOPS = 3

ALPHA = 8.0
LAMBDA = 1.0
EPSILON = 1e-06


def chip_shift(value, chips, distance):
    pairs = [
        (CORES * chip + core, CORES * ((chip + distance) % chips) + core)
        for chip in range(chips)
        for core in range(CORES)
    ]
    return lax.ppermute(value, "grp", pairs)


def core_swap(value, chips):
    pairs = [(CORES * chip + core, CORES * chip + 1 - core) for chip in range(chips) for core in range(CORES)]
    return lax.ppermute(value, "grp", pairs)


def slot_table(chips):
    pack_slot = {0: 0, 2 * STRIDE: 1, chips - STRIDE: 2, STRIDE: 3}
    table = np.full((chips,), -1, np.int32)
    for pack, offset in enumerate([0, -1, 1, -2, 2, -3, 3]):
        for ahead, slot in pack_slot.items():
            table[(offset + ahead) % chips] = PACK * pack + slot
    for slot, ahead in enumerate([-4 - STRIDE, -4 + STRIDE, 4 - STRIDE, 4 + STRIDE]):
        table[ahead % chips] = PACK * (2 * HOPS + 1) + slot
    assert (table >= 0).all()
    return table


def pool_places(tile_users, chips, replicas, owned):
    member = tile_users // (owned * replicas)
    here = lax.axis_index("grp")
    ahead = (member // CORES - here // CORES + chips) % chips
    distances = np.arange(chips, dtype=np.int32)
    slot = jnp.sum(jnp.where(ahead[:, None] == distances, slot_table(chips), 0), axis=1)
    other_core = (member % CORES != here % CORES).astype(jnp.int32)
    return ((other_core * chips + slot) * owned + tile_users % owned).astype(jnp.int32)


def merge(parts):
    half = parts.shape[0] // 2
    return parts[:half].astype(jnp.float32) + parts[half:].astype(jnp.float32)


def dot(left, right):
    return jnp.dot(left, right, preferred_element_type=jnp.float32)


def dot_turned(left, right):
    return lax.dot_general(left, right, (((1,), (1,)), ((), ())), preferred_element_type=jnp.float32)


def high_low(value):
    high = value.astype(jnp.bfloat16)
    return high, (value - high.astype(jnp.float32)).astype(jnp.bfloat16)


def item_rows(block):
    return slice(block * IBLK, (block + 1) * IBLK)


SCALAR = pl.BlockSpec(memory_space=pltpu.SMEM)
VECTOR = pl.BlockSpec(memory_space=pltpu.VMEM)
PARAMS = pltpu.CompilerParams(vmem_limit_bytes=40 * 1024 * 1024)


def gram_kernel(users_ref, gram_ref):
    high, low = high_low(users_ref[...])
    dims = (((0,), (0,)), ((), ()))
    product = functools.partial(lax.dot_general, dimension_numbers=dims, preferred_element_type=jnp.float32)
    gram_ref[...] = product(high, high) + (product(high, low) + product(low, high))


def local_gram(users):
    features = users.shape[1]
    return pl.pallas_call(
        gram_kernel,
        out_shape=jax.ShapeDtypeStruct((features, features), jnp.float32),
        in_specs=[VECTOR],
        out_specs=VECTOR,
        cost_estimate=pl.CostEstimate(flops=10**10, bytes_accessed=10**7, transcendentals=0),
        name="local_gram",
    )(users)


def weight_kernel(counts_ref, weight_ref):
    blocks, _, depth = weight_ref.shape
    tiles = IBLK // UROWS
    for block in range(blocks):
        for start in range(0, depth, IBLK):
            first = (block * depth + start) // UROWS
            counts = counts_ref[first : first + tiles].reshape(IBLK, IBLK).astype(jnp.float32)
            weight_ref[block, :, start : start + IBLK] = (ALPHA * counts).T.astype(jnp.bfloat16)


def item_weights(counts, blocks):
    depth = counts.shape[0] * counts.shape[1] // blocks
    return pl.pallas_call(
        weight_kernel,
        out_shape=jax.ShapeDtypeStruct((blocks, IBLK, depth), jnp.bfloat16),
        in_specs=[VECTOR],
        out_specs=VECTOR,
        compiler_params=PARAMS,
        name="item_weights",
    )(counts)


def tile_part(total, high, block, rows_ref, weight_ref):
    depth = weight_ref.shape[2]
    for start in range(0, depth, CHUNK):
        rows = rows_ref[block * depth + start : block * depth + start + CHUNK, :]
        scores = dot_turned(high, rows)
        weight = weight_ref[block, :, start : start + CHUNK].astype(jnp.float32)
        total = total + dot((weight * scores).astype(jnp.bfloat16), rows)
    return total


def first_kernel(places_ref, *refs):
    gathered, (weight_ref, items_ref, rows_ref, residue_ref, pool_ref) = refs[:-5], refs[-5:]
    filled = 0
    for part in gathered:
        pool_ref[filled : filled + part.shape[0], :] = part[...]
        filled += part.shape[0]

    def fetch(tile, carry):
        to = pl.ds(pl.multiple_of(tile * UROWS, UROWS), UROWS)
        at = pl.ds(pl.multiple_of(places_ref[tile] * UROWS, UROWS), UROWS)
        rows_ref[to, :] = pool_ref[at, :]
        return carry

    lax.fori_loop(0, places_ref.shape[0], fetch, 0, unroll=4)
    blocks, _, depth = weight_ref.shape
    for block in range(blocks):
        guess = items_ref[item_rows(block), :]
        target = -LAMBDA * guess
        for start in range(0, depth, CHUNK):
            weight = weight_ref[block, :, start : start + CHUNK]
            confidence = weight + jnp.where(weight > 0, 1.0, 0.0).astype(jnp.bfloat16)
            target = target + dot(confidence, rows_ref[block * depth + start : block * depth + start + CHUNK, :])
        part = tile_part(jnp.zeros_like(guess), guess.astype(jnp.bfloat16), block, rows_ref, weight_ref)
        residue_ref[item_rows(block), :] = target - part


def first_residue(places, gathered, weight, items):
    blocks, _, depth = weight.shape
    features = items.shape[1]
    pool_rows = sum(part.shape[0] for part in gathered)
    return pl.pallas_call(
        first_kernel,
        out_shape=(
            jax.ShapeDtypeStruct((blocks * depth, features), jnp.bfloat16),
            jax.ShapeDtypeStruct(items.shape, jnp.float32),
        ),
        in_specs=[SCALAR] + [VECTOR] * (len(gathered) + 2),
        out_specs=(VECTOR, VECTOR),
        scratch_shapes=[pltpu.VMEM((pool_rows, features), jnp.bfloat16)],
        compiler_params=PARAMS,
        name="first_residue",
    )(places, *gathered, weight, items)


def steps_kernel(
    rows_ref, weight_ref, items_ref, started_ref, gram_ref, guess_ref, high_ref, low_ref, residue_ref, direction_ref,
    applied_ref,
):
    blocks = weight_ref.shape[0]
    high_ref[...], low_ref[...] = high_low(gram_ref[...])

    def gram_part(vector):
        high, low = high_low(vector)
        return dot(high, high_ref[...]) + (dot(high, low_ref[...]) + dot(low, high_ref[...]))

    guess = items_ref[...]
    guess_ref[...] = guess
    residue = started_ref[...] - gram_part(guess)
    residue_ref[...] = residue
    direction_ref[...] = residue

    def step(iteration, current):
        vector = direction_ref[...]
        applied_ref[...] = vector * LAMBDA + gram_part(vector)
        for block in range(blocks):
            span = item_rows(block)
            high = direction_ref[span, :].astype(jnp.bfloat16)
            applied_ref[span, :] = tile_part(applied_ref[span, :], high, block, rows_ref, weight_ref)
        direction = direction_ref[...]
        applied = applied_ref[...]
        size = current / (jnp.sum(direction * applied, axis=1, keepdims=True) + EPSILON)
        guess_ref[...] += size * direction
        residue = residue_ref[...] - size * applied
        residue_ref[...] = residue
        following = jnp.sum(residue * residue, axis=1, keepdims=True)
        direction_ref[...] = residue + (following / (current + EPSILON)) * direction
        return following

    lax.fori_loop(0, ITERS, step, jnp.sum(residue * residue, axis=1, keepdims=True))


def solve_steps(rows, weight, items, started, gram):
    features = items.shape[1]
    state = pltpu.VMEM(items.shape, jnp.float32)
    square = pltpu.VMEM((features, features), jnp.bfloat16)
    return pl.pallas_call(
        steps_kernel,
        out_shape=jax.ShapeDtypeStruct(items.shape, jnp.float32),
        in_specs=[VECTOR] * 5,
        out_specs=VECTOR,
        scratch_shapes=[square, square, state, state, state],
        compiler_params=PARAMS,
        name="solve_steps",
    )(rows, weight, items, started, gram)


def small_call(kernel, outs, name, *args):
    return pl.pallas_call(
        kernel,
        out_shape=outs,
        in_specs=[VECTOR] * len(args),
        out_specs=jax.tree.map(lambda _: VECTOR, outs),
        compiler_params=PARAMS,
        name=name,
    )(*args)


def put_parts(ref, start, value):
    count = value.shape[0]
    ref[start : start + count, :], ref[start + count : start + 2 * count, :] = high_low(value)


def far_kernel(below_ref, above_ref, mine_ref, other_ref, up_ref, down_ref, total_ref):
    half = below_ref.shape[0] // 2
    total = mine_ref[...] + other_ref[...]
    total_ref[...] = total
    up_ref[:half, :] = below_ref[:half, :]
    down_ref[:half, :] = above_ref[half:, :]
    put_parts(up_ref, half, total)
    put_parts(down_ref, half, total)


def pack_kernel(own_ref, below_ref, above_ref, up_ref, down_ref, total_ref, farthest_ref, pack_ref):
    rows = own_ref.shape[0]
    half = rows // 2
    pack_ref[:rows, :] = own_ref[...]
    pack_ref[rows : rows + half, :] = up_ref[:half, :]
    pack_ref[rows + half : 2 * rows, :] = down_ref[:half, :]
    pack_ref[2 * rows : 3 * rows, :] = below_ref[...]
    pack_ref[3 * rows : 4 * rows, :] = above_ref[...]
    total = total_ref[...] + (merge(up_ref[half:, :]) + merge(down_ref[half:, :])) + merge(farthest_ref[...])
    put_parts(pack_ref, PACK * rows, total)


def join_kernel(counts, *refs):
    filled = 0
    for count, part in zip(counts, refs[:-1]):
        refs[-1][filled : filled + count, :] = part[:count, :]
        filled += count


def join(parts, counts):
    out = jax.ShapeDtypeStruct((sum(counts), parts[0].shape[1]), parts[0].dtype)
    return small_call(functools.partial(join_kernel, counts), out, "join", *parts)


def spread_kernel(*refs):
    parts, out_ref = refs[:-1], refs[-1]
    copies, share, _ = out_ref.shape
    total = functools.reduce(jnp.add, [merge(part[-2 * share :, :]) for part in parts])
    for copy in range(copies):
        out_ref[copy] = total


def on_device(user_factors, item_factors, tile_users, tile_counts):
    chips = lax.axis_size("grp") // CORES
    replicas = lax.axis_size("rep")
    owned_rows, features = user_factors.shape
    share = features // replicas
    half = owned_rows // 2
    pack_rows = PACK * owned_rows
    shift = functools.partial(chip_shift, chips=chips)
    bar = lax.optimization_barrier

    def half_rows(count):
        return jax.ShapeDtypeStruct((count, features), jnp.bfloat16)

    piece = jax.ShapeDtypeStruct((share, features), jnp.float32)

    own = user_factors.astype(jnp.bfloat16)
    below, above = shift(own, distance=STRIDE), shift(own, distance=-STRIDE)
    pieces = lax.all_to_all(local_gram(user_factors), "rep", 0, 0, tiled=True)
    gram = jnp.sum(pieces.reshape(replicas, share, features), axis=0)
    gram_other = core_swap(gram, chips)
    below, above, gram, gram_other = bar((below, above, gram, gram_other))

    sent = half_rows(half + 2 * share)
    to_up, to_down, total = small_call(far_kernel, (sent, sent, piece), "far_parts", below, above, gram, gram_other)
    far_up, far_down = bar((shift(to_up, distance=STRIDE), shift(to_down, distance=-STRIDE)))
    farthest = shift(far_up[half:], distance=STRIDE)
    pack = small_call(
        pack_kernel, half_rows(pack_rows + 2 * share), "pack", own, below, above, far_up, far_down, total, farthest
    )

    gathered = [pack]
    up, down = pack, pack
    for hop in range(HOPS + 1):
        last = hop == HOPS
        up = shift(up[pack_rows // 2 :] if last else up, distance=1)
        down = shift(down[pack_rows // 2 : pack_rows] if last else down, distance=-1)
        up, down = bar((up, down))
        gathered += [up, down]
    near = join(gathered, [pack_rows] * (2 * HOPS + 1) + [pack_rows // 2] * 2)
    other = core_swap(near, chips)

    spread = small_call(
        spread_kernel, jax.ShapeDtypeStruct((replicas, share, features), jnp.float32), "spread", *gathered[:-1]
    )
    gram = lax.all_to_all(spread.reshape(features, features), "rep", 0, 0, tiled=True)

    owned = owned_rows // UROWS
    places = pool_places(tile_users, chips, replicas, owned)
    weight = item_weights(tile_counts, item_factors.shape[0] // IBLK)
    rows, started = first_residue(places, [near, other], weight, item_factors)
    return solve_steps(rows, weight, item_factors, started, gram)


def solution(mesh):
    in_specs = (
        P(("grp", "rep"), None),
        P(("grp", "rep"), None),
        P(("grp", "rep")),
        P(("grp", "rep"), None, None),
    )
    out_specs = P(("grp", "rep"), None)
    return jax.shard_map(
        on_device, mesh=mesh, in_specs=in_specs, out_specs=out_specs, check_vma=False
    )
```

time: 931 us -> 174 us (0.19)
  waiting for transfers between devices: 865 us -> 35.2 us
  starting transfers between devices: 0.05 us -> 113 us
  matrix products: 25 us -> 0 us
  between operations: 15 us -> 0.37 us
  Pallas kernels: 0 us -> 12.1 us
    psum x1 -> x0, waiting for transfers between devices: 721 us -> none  [on_device(): gram_total = lax.psum(partial_gram, ('grp', 'rep'))]
    all_gather x1 -> x0, waiting for transfers between devices: 144 us -> none  [on_device(): group_rows = lax.all_gather(user_half, 'grp', axis=0, tiled=True)]
    ppermute x0 -> x15, starting transfers between devices: none -> 99 us  [the longest x13 81.8 us: chip_shift(): return lax.ppermute(value, 'grp', pairs)]
    ppermute x0 -> x15, waiting for transfers between devices: none -> 35.2 us  [the longest x13 35.2 us: chip_shift(): return lax.ppermute(value, 'grp', pairs)]
    dot_general x10 -> x0, matrix products: 25 us -> none  [the longest x4 13.8 us: operate(): jnp.einsum('bsui,bsuk->bik', mixed_terms, block_rows, preferred_element_t...]
    all_to_all x0 -> x2, starting transfers between devices: none -> 13.7 us  [the longest x1 7.58 us: on_device(): pieces = lax.all_to_all(local_gram(user_factors), 'rep', 0, 0, tiled=True)]
    reshape x8 -> x0, local copies, waits for them, and re-layouts: 12.2 us -> none  [the longest x4 6.65 us: operate(): return gram_part + LAMBDA * direction + tile_part.reshape(-1, features)]
    pallas_call x0 -> x8, Pallas kernels: none -> 12.1 us  [the longest x1 6.06 us: solve_steps(): pl.pallas_call(steps_kernel, out_shape=jax.ShapeDtypeStruct(items.shape,...]
  transfers between devices with their start and end apart: 2 -> 17, of which waited for: 2 -> 10; matrix products, arithmetic and copies ran while one was open for 2% -> 0% of each run, Pallas kernels for 0% -> 2%
where the time goes in v2:
time: 174 us; the launch traced here: 173 us
  starting transfers between devices  113 us (65%)
  waiting for transfers between devices  35.2 us (20%)
  local copies, waits for them, and re-layouts  12.1 us (7%)
  Pallas kernels  12.1 us (7%)
    ppermute x13, starting transfers between devices, chip_shift(): return lax.ppermute(value, 'grp', pairs)  81.8 us
    ppermute x13, waiting for transfers between devices, chip_shift(): return lax.ppermute(value, 'grp', pairs)  35.2 us
    ppermute x2, starting transfers between devices, core_swap(): return lax.ppermute(value, 'grp', pairs)  17.2 us
    unnamed x34, local copies, waits for them, and re-layouts  12 us
    all_to_all x1, starting transfers between devices, on_device(): pieces = lax.all_to_all(local_gram(user_factors), 'rep', 0, 0, tiled=True)  7.58 us
    all_to_all x1, starting transfers between devices, on_device(): lax.all_to_all(spread.reshape(features, features), 'rep', 0, 0, tiled=True)  6.13 us
    pallas_call x1, Pallas kernels, solve_steps(): pl.pallas_call(steps_kernel, out_shape=jax.ShapeDtypeStruct(items.shape,...  6.06 us
    pallas_call x1, Pallas kernels, first_residue(): pl.pallas_call(first_kernel, out_shape=(jax.ShapeDtypeStruct((blocks * de...  3.55 us
  transfers between devices with their start and end apart: 17, of which 10 were waited for; matrix products, arithmetic and copies ran while one was open for 0% of the time, Pallas kernels for 2%

profile of v2, /device:TPU:1, one launch (start us, length us, event | category | flops | bytes accessed | tf_op | source)
XLA Modules:
  0.0 172.6 jit_solution(9774873164060591435)
XLA Ops:
  0.0 2.0 %local_gram.1 = f32[256,256]{1,0:T(8,128)} custom-call(f32[128,256]{1,0:T(8,128)} %users_ref.1), custom_call_target="tpu_custom_call" | custom-call | flops 10000000000 | bytes 10000000 | tf_op jit(solution)/shard_map/local_gram/pallas_call | solution.py:97
  2.0 7.6 %all-to-all-start = ((f32[16,16,256]{2,1,0:T(8,128)}), f32[16,16,256]{2,1,0:T(8,128)S(1)}, u32[]{:S(2)}, u32[]{:S(2)}) async-start(f32[16,16,256]{2,1,0:T(8,128)} %bitcast.3), calls=%async_computation | async-start | bytes 524288 | tf_op jit(solution)/shard_map/all_to_all | solution.py:310
  9.6 22.7 %collective-permute-start.1 = (bf16[128,256]{1,0:T(8,128)(2,1)S(1)}, bf16[128,256]{1,0:T(8,128)(2,1)S(1)}, u32[]{:S(2)}, u32[]{:S(2)}) collective-permute-start(bf16[128,256]{1,0:T(8,128)(2,1)S(1)} %convert_element_type.4.own_ref), channel_id=1, source_target_pairs={{0,768},{16,784},{32,800},{48,816},{64,832},{80,848},{96,864},{112... | collective-permute-start | bytes 196616 | tf_op jit(solution)/shard_map/ppermute | solution.py:31
  32.3 1.9 %collective-permute-start = (bf16[128,256]{1,0:T(8,128)(2,1)S(1)}, bf16[128,256]{1,0:T(8,128)(2,1)S(1)}, u32[]{:S(2)}, u32[]{:S(2)}) collective-permute-start(bf16[128,256]{1,0:T(8,128)(2,1)S(1)} %convert_element_type.4.own_ref), channel_id=1, source_target_pairs={{0,256},{16,272},{32,288},{48,304},{64,320},{80,336},{96,352},{112... | collective-permute-start | bytes 196616 | tf_op jit(solution)/shard_map/ppermute | solution.py:31
  34.3 3.1 %collective-permute-start.2 = (f32[16,256]{1,0:T(8,128)S(1)}, f32[16,256]{1,0:T(8,128)S(1)}, u32[]{:S(2)}, u32[]{:S(2)}) collective-permute-start(f32[16,256]{1,0:T(8,128)S(1)} %reduce_sum.19.mine_ref), channel_id=1, source_target_pairs={{0,16},{16,0},{32,48},{48,32},{64,80},{80,64},{96,112},{112,96},{1... | collective-permute-start | bytes 49160 | tf_op jit(solution)/shard_map/ppermute | solution.py:36
  37.4 9.2 %collective-permute-done.below_ref = bf16[128,256]{1,0:T(8,128)(2,1)S(1)} collective-permute-done((bf16[128,256]{1,0:T(8,128)(2,1)S(1)}, bf16[128,256]{1,0:T(8,128)(2,1)S(1)}, u32[]{:S(2)}, u32[]{:S(2)}) %collective-permute-start) | collective-permute-done | bytes 65568 | tf_op jit(solution)/shard_map/ppermute | solution.py:31
  46.6 5.4 %collective-permute-start.3 = (bf16[96,256]{1,0:T(8,128)(2,1)S(1)}, bf16[96,256]{1,0:T(8,128)(2,1)S(1)}, u32[]{:S(2)}, u32[]{:S(2)}) collective-permute-start(bf16[96,256]{1,0:T(8,128)(2,1)S(1)} %get-tuple-element.28), channel_id=1, source_target_pairs={{0,256},{16,272},{32,288},{48,304},{64,320},{80,336},{96,352},{112... | collective-permute-start | bytes 147464 | tf_op jit(solution)/shard_map/ppermute | solution.py:31
  52.0 10.1 %collective-permute-start.4 = (bf16[96,256]{1,0:T(8,128)(2,1)S(1)}, bf16[96,256]{1,0:T(8,128)(2,1)S(1)}, u32[]{:S(2)}, u32[]{:S(2)}) collective-permute-start(bf16[96,256]{1,0:T(8,128)(2,1)S(1)} %get-tuple-element.29), channel_id=1, source_target_pairs={{0,768},{16,784},{32,800},{48,816},{64,832},{80,848},{96,864},{112... | collective-permute-start | bytes 147464 | tf_op jit(solution)/shard_map/ppermute | solution.py:31
  62.1 4.2 %collective-permute-done.4.down_ref = bf16[96,256]{1,0:T(8,128)(2,1)S(1)} collective-permute-done((bf16[96,256]{1,0:T(8,128)(2,1)S(1)}, bf16[96,256]{1,0:T(8,128)(2,1)S(1)}, u32[]{:S(2)}, u32[]{:S(2)}) %collective-permute-start.4) | collective-permute-done | bytes 49184 | tf_op jit(solution)/shard_map/ppermute | solution.py:31
  66.3 10.0 %collective-permute-start.5 = (bf16[32,256]{1,0:T(8,128)(2,1)S(1)}, bf16[32,256]{1,0:T(8,128)(2,1)S(1)}, u32[]{:S(2)}, u32[]{:S(2)}) collective-permute-start(bf16[32,256]{1,0:T(8,128)(2,1)S(1)} %slice.9), channel_id=1, source_target_pairs={{0,256},{16,272},{32,288},{48,304},{64,320},{80,336},{96,352},{112... | collective-permute-start | bytes 49160 | tf_op jit(solution)/shard_map/ppermute | solution.py:31
  76.4 3.1 %collective-permute-done.5.farthest_ref = bf16[32,256]{1,0:T(8,128)(2,1)S(1)} collective-permute-done((bf16[32,256]{1,0:T(8,128)(2,1)S(1)}, bf16[32,256]{1,0:T(8,128)(2,1)S(1)}, u32[]{:S(2)}, u32[]{:S(2)}) %collective-permute-start.5) | collective-permute-done | bytes 16416 | tf_op jit(solution)/shard_map/ppermute | solution.py:31
  79.5 9.4 %collective-permute-start.7 = (bf16[544,256]{1,0:T(8,128)(2,1)S(1)}, bf16[544,256]{1,0:T(8,128)(2,1)S(1)}, u32[]{:S(2)}, u32[]{:S(2)}) collective-permute-start(bf16[544,256]{1,0:T(8,128)(2,1)S(1)} %pack.1.refs_0_), channel_id=1, source_target_pairs={{0,992},{16,1008},{32,0},{48,16},{64,32},{80,48},{96,64},{112,80},... | collective-permute-start | bytes 835592 | tf_op jit(solution)/shard_map/ppermute | solution.py:31
  88.9 1.9 %collective-permute-start.6 = (bf16[544,256]{1,0:T(8,128)(2,1)S(1)}, bf16[544,256]{1,0:T(8,128)(2,1)S(1)}, u32[]{:S(2)}, u32[]{:S(2)}) collective-permute-start(bf16[544,256]{1,0:T(8,128)(2,1)S(1)} %pack.1.refs_0_), channel_id=1, source_target_pairs={{0,32},{16,48},{32,64},{48,80},{64,96},{80,112},{96,128},{112,144}... | collective-permute-start | bytes 835592 | tf_op jit(solution)/shard_map/ppermute | solution.py:31
  90.8 1.5 collective-permute-done.7.refs_2_
  92.4 5.0 %collective-permute-done.6.refs_1_ = bf16[544,256]{1,0:T(8,128)(2,1)S(1)} collective-permute-done((bf16[544,256]{1,0:T(8,128)(2,1)S(1)}, bf16[544,256]{1,0:T(8,128)(2,1)S(1)}, u32[]{:S(2)}, u32[]{:S(2)}) %collective-permute-start.6) | collective-permute-done | bytes 278560 | tf_op jit(solution)/shard_map/ppermute | solution.py:31
  97.4 1.9 %collective-permute-start.8 = (bf16[544,256]{1,0:T(8,128)(2,1)S(1)}, bf16[544,256]{1,0:T(8,128)(2,1)S(1)}, u32[]{:S(2)}, u32[]{:S(2)}) collective-permute-start(bf16[544,256]{1,0:T(8,128)(2,1)S(1)} %collective-permute-done.6.refs_1_), channel_id=1, source_target_pairs={{0,32},{16,48},{32,64},{48,80},{64,96},{80,112},{96,128},{112,144}... | collective-permute-start | bytes 835592 | tf_op jit(solution)/shard_map/ppermute | solution.py:31
  99.3 4.6 %collective-permute-start.9 = (bf16[544,256]{1,0:T(8,128)(2,1)S(1)}, bf16[544,256]{1,0:T(8,128)(2,1)S(1)}, u32[]{:S(2)}, u32[]{:S(2)}) collective-permute-start(bf16[544,256]{1,0:T(8,128)(2,1)S(1)} %collective-permute-done.7.refs_2_), channel_id=1, source_target_pairs={{0,992},{16,1008},{32,0},{48,16},{64,32},{80,48},{96,64},{112,80},... | collective-permute-start | bytes 835592 | tf_op jit(solution)/shard_map/ppermute | solution.py:31
  103.9 3.3 %collective-permute-done.8.refs_3_ = bf16[544,256]{1,0:T(8,128)(2,1)S(1)} collective-permute-done((bf16[544,256]{1,0:T(8,128)(2,1)S(1)}, bf16[544,256]{1,0:T(8,128)(2,1)S(1)}, u32[]{:S(2)}, u32[]{:S(2)}) %collective-permute-start.8) | collective-permute-done | bytes 278560 | tf_op jit(solution)/shard_map/ppermute | solution.py:31
  107.2 0.2 collective-permute-done.9.refs_4_
  107.4 1.9 %collective-permute-start.10 = (bf16[544,256]{1,0:T(8,128)(2,1)S(1)}, bf16[544,256]{1,0:T(8,128)(2,1)S(1)}, u32[]{:S(2)}, u32[]{:S(2)}) collective-permute-start(bf16[544,256]{1,0:T(8,128)(2,1)S(1)} %collective-permute-done.8.refs_3_), channel_id=1, source_target_pairs={{0,32},{16,48},{32,64},{48,80},{64,96},{80,112},{96,128},{112,144}... | collective-permute-start | bytes 835592 | tf_op jit(solution)/shard_map/ppermute | solution.py:31
  109.3 5.0 %collective-permute-start.11 = (bf16[544,256]{1,0:T(8,128)(2,1)S(1)}, bf16[544,256]{1,0:T(8,128)(2,1)S(1)}, u32[]{:S(2)}, u32[]{:S(2)}) collective-permute-start(bf16[544,256]{1,0:T(8,128)(2,1)S(1)} %collective-permute-done.9.refs_4_), channel_id=1, source_target_pairs={{0,992},{16,1008},{32,0},{48,16},{64,32},{80,48},{96,64},{112,80},... | collective-permute-start | bytes 835592 | tf_op jit(solution)/shard_map/ppermute | solution.py:31
  114.3 3.7 %collective-permute-done.10.refs_5_ = bf16[544,256]{1,0:T(8,128)(2,1)S(1)} collective-permute-done((bf16[544,256]{1,0:T(8,128)(2,1)S(1)}, bf16[544,256]{1,0:T(8,128)(2,1)S(1)}, u32[]{:S(2)}, u32[]{:S(2)}) %collective-permute-start.10) | collective-permute-done | bytes 278560 | tf_op jit(solution)/shard_map/ppermute | solution.py:31
  118.0 1.8 %collective-permute-done.11.refs_6_ = bf16[544,256]{1,0:T(8,128)(2,1)S(1)} collective-permute-done((bf16[544,256]{1,0:T(8,128)(2,1)S(1)}, bf16[544,256]{1,0:T(8,128)(2,1)S(1)}, u32[]{:S(2)}, u32[]{:S(2)}) %collective-permute-start.11) | collective-permute-done | bytes 278560 | tf_op jit(solution)/shard_map/ppermute | solution.py:31
  119.8 1.9 %collective-permute-start.12 = (bf16[288,256]{1,0:T(8,128)(2,1)S(1)}, bf16[288,256]{1,0:T(8,128)(2,1)S(1)}, u32[]{:S(2)}, u32[]{:S(2)}) collective-permute-start(bf16[288,256]{1,0:T(8,128)(2,1)S(1)} %slice.10), channel_id=1, source_target_pairs={{0,32},{16,48},{32,64},{48,80},{64,96},{80,112},{96,128},{112,144}... | collective-permute-start | bytes 442376 | tf_op jit(solution)/shard_map/ppermute | solution.py:31
  121.7 0.0 copy-start.15
  121.7 5.0 %collective-permute-start.13 = (bf16[256,256]{1,0:T(8,128)(2,1)S(1)}, bf16[256,256]{1,0:T(8,128)(2,1)S(1)}, u32[]{:S(2)}, u32[]{:S(2)}) collective-permute-start(bf16[256,256]{1,0:T(8,128)(2,1)S(1)} %slice.11), channel_id=1, source_target_pairs={{0,992},{16,1008},{32,0},{48,16},{64,32},{80,48},{96,64},{112,80},... | collective-permute-start | bytes 393224 | tf_op jit(solution)/shard_map/ppermute | solution.py:31
  126.8 3.2 %collective-permute-done.13.refs_8_ = bf16[256,256]{1,0:T(8,128)(2,1)S(1)} collective-permute-done((bf16[256,256]{1,0:T(8,128)(2,1)S(1)}, bf16[256,256]{1,0:T(8,128)(2,1)S(1)}, u32[]{:S(2)}, u32[]{:S(2)}) %collective-permute-start.13) | collective-permute-done | bytes 131104 | tf_op jit(solution)/shard_map/ppermute | solution.py:31
  130.0 0.1 join.1.refs_0_
  130.2 0.0 copy-start.16
  130.2 14.0 %collective-permute-start.14 = (bf16[4096,256]{1,0:T(8,128)(2,1)S(1)}, bf16[4096,256]{1,0:T(8,128)(2,1)}, u32[]{:S(2)}, u32[]{:S(2)}) collective-permute-start(bf16[4096,256]{1,0:T(8,128)(2,1)S(1)} %join.1.refs_0_), channel_id=1, source_target_pairs={{0,16},{16,0},{32,48},{48,32},{64,80},{80,64},{96,112},{112,96},{1... | collective-permute-start | bytes 6291464 | tf_op jit(solution)/shard_map/ppermute | solution.py:36
  144.3 0.0 copy-start.6
  144.3 0.9 copy-done.6
  145.2 1.0 copy-done.8
  146.2 1.0 copy-done.10
  147.2 0.7 copy-done.11
  147.9 6.1 %all-to-all-start.1 = ((f32[16,16,256]{2,1,0:T(8,128)}), f32[16,16,256]{2,1,0:T(8,128)S(1)}, u32[]{:S(2)}, u32[]{:S(2)}) async-start(f32[16,16,256]{2,1,0:T(8,128)} %copy-done.11), calls=%async_computation.1 | async-start | bytes 524288 | tf_op jit(solution)/shard_map/all_to_all | solution.py:337
  154.0 0.1 select_reduce_fusion
  154.1 1.6 copy-done.2
  155.7 0.4 item_weights.1.refs_2_.weight_ref
  156.1 0.0 copy-start
  156.1 1.0 copy-done
  157.2 3.5 %first_residue.1 = (bf16[4096,256]{1,0:T(8,128)(2,1)S(1)}, f32[512,256]{1,0:T(8,128)S(1)}) custom-call(s32[64]{0:T(128)S(1)} %fusion.places_ref, bf16[4096,256]{1,0:T(8,128)(2,1)S(1)} %join.1.refs_0_, bf16[4096,256]{1,0:T(8,128)(2,1)} %collective-permute-done.14.refs_1_, bf16[4,128,1024]{2,1,0:T(8,128)(2,1)S(1)} %item_weights.1.refs_2_.weight_ref, ...), custom_call_target="tpu_custom_call" | custom-call | tf_op jit(solution)/shard_map/first_residue/pallas_call | solution.py:169
  160.7 1.3 copy-done.3
  162.1 0.8 copy-done.12
  162.9 1.0 copy-done.1
  163.9 1.6 copy-done.4
  165.5 1.0 copy-done.13
  166.5 6.1 %solve_steps.1 = f32[512,256]{1,0:T(8,128)} custom-call(bf16[4096,256]{1,0:T(8,128)(2,1)S(1)} %copy-done.4, bf16[4,128,1024]{2,1,0:T(8,128)(2,1)S(1)} %item_weights.1.refs_2_.weight_ref, f32[512,256]{1,0:T(8,128)S(1)} %copy-done.1, f32[512,256]{1,0:T(8,128)S(1)} %copy-done.13, f32[256,256]{1,0:T(8,128)S(1)} %bitcast.2), custom_call_target="tpu_custom_call" | custom-call | tf_op jit(solution)/shard_map/solve_steps/pallas_call | solution.py:224
  (36 shorter events, 0.2 us)
Async XLA Ops:
  0.0 9.6 %copy-start.14 = (f32[128,256]{1,0:T(8,128)S(1)}, f32[128,256]{1,0:T(8,128)}, u32[]{:S(2)}) copy-start(f32[128,256]{1,0:T(8,128)} %users_ref.1) | copy-start | bytes 393220
  2.0 32.3 %all-to-all-start = ((f32[16,16,256]{2,1,0:T(8,128)}), f32[16,16,256]{2,1,0:T(8,128)S(1)}, u32[]{:S(2)}, u32[]{:S(2)}) async-start(f32[16,16,256]{2,1,0:T(8,128)} %bitcast.3), calls=%async_computation | async-start | bytes 524288 | tf_op jit(solution)/shard_map/all_to_all | solution.py:310
  9.6 27.8 %collective-permute-start.1 = (bf16[128,256]{1,0:T(8,128)(2,1)S(1)}, bf16[128,256]{1,0:T(8,128)(2,1)S(1)}, u32[]{:S(2)}, u32[]{:S(2)}) collective-permute-start(bf16[128,256]{1,0:T(8,128)(2,1)S(1)} %convert_element_type.4.own_ref), channel_id=1, source_target_pairs={{0,768},{16,784},{32,800},{48,816},{64,832},{80,848},{96,864},{112... | collective-permute-start | bytes 196616 | tf_op jit(solution)/shard_map/ppermute | solution.py:31
  32.3 14.3 %collective-permute-start = (bf16[128,256]{1,0:T(8,128)(2,1)S(1)}, bf16[128,256]{1,0:T(8,128)(2,1)S(1)}, u32[]{:S(2)}, u32[]{:S(2)}) collective-permute-start(bf16[128,256]{1,0:T(8,128)(2,1)S(1)} %convert_element_type.4.own_ref), channel_id=1, source_target_pairs={{0,256},{16,272},{32,288},{48,304},{64,320},{80,336},{96,352},{112... | collective-permute-start | bytes 196616 | tf_op jit(solution)/shard_map/ppermute | solution.py:31
  34.3 12.3 %collective-permute-start.2 = (f32[16,256]{1,0:T(8,128)S(1)}, f32[16,256]{1,0:T(8,128)S(1)}, u32[]{:S(2)}, u32[]{:S(2)}) collective-permute-start(f32[16,256]{1,0:T(8,128)S(1)} %reduce_sum.19.mine_ref), channel_id=1, source_target_pairs={{0,16},{16,0},{32,48},{48,32},{64,80},{80,64},{96,112},{112,96},{1... | collective-permute-start | bytes 49160 | tf_op jit(solution)/shard_map/ppermute | solution.py:36
  46.6 15.5 %collective-permute-start.3 = (bf16[96,256]{1,0:T(8,128)(2,1)S(1)}, bf16[96,256]{1,0:T(8,128)(2,1)S(1)}, u32[]{:S(2)}, u32[]{:S(2)}) collective-permute-start(bf16[96,256]{1,0:T(8,128)(2,1)S(1)} %get-tuple-element.28), channel_id=1, source_target_pairs={{0,256},{16,272},{32,288},{48,304},{64,320},{80,336},{96,352},{112... | collective-permute-start | bytes 147464 | tf_op jit(solution)/shard_map/ppermute | solution.py:31
  52.0 14.3 %collective-permute-start.4 = (bf16[96,256]{1,0:T(8,128)(2,1)S(1)}, bf16[96,256]{1,0:T(8,128)(2,1)S(1)}, u32[]{:S(2)}, u32[]{:S(2)}) collective-permute-start(bf16[96,256]{1,0:T(8,128)(2,1)S(1)} %get-tuple-element.29), channel_id=1, source_target_pairs={{0,768},{16,784},{32,800},{48,816},{64,832},{80,848},{96,864},{112... | collective-permute-start | bytes 147464 | tf_op jit(solution)/shard_map/ppermute | solution.py:31
  66.3 13.2 %collective-permute-start.5 = (bf16[32,256]{1,0:T(8,128)(2,1)S(1)}, bf16[32,256]{1,0:T(8,128)(2,1)S(1)}, u32[]{:S(2)}, u32[]{:S(2)}) collective-permute-start(bf16[32,256]{1,0:T(8,128)(2,1)S(1)} %slice.9), channel_id=1, source_target_pairs={{0,256},{16,272},{32,288},{48,304},{64,320},{80,336},{96,352},{112... | collective-permute-start | bytes 49160 | tf_op jit(solution)/shard_map/ppermute | solution.py:31
  79.5 12.8 %collective-permute-start.7 = (bf16[544,256]{1,0:T(8,128)(2,1)S(1)}, bf16[544,256]{1,0:T(8,128)(2,1)S(1)}, u32[]{:S(2)}, u32[]{:S(2)}) collective-permute-start(bf16[544,256]{1,0:T(8,128)(2,1)S(1)} %pack.1.refs_0_), channel_id=1, source_target_pairs={{0,992},{16,1008},{32,0},{48,16},{64,32},{80,48},{96,64},{112,80},... | collective-permute-start | bytes 835592 | tf_op jit(solution)/shard_map/ppermute | solution.py:31
  88.9 8.5 %collective-permute-start.6 = (bf16[544,256]{1,0:T(8,128)(2,1)S(1)}, bf16[544,256]{1,0:T(8,128)(2,1)S(1)}, u32[]{:S(2)}, u32[]{:S(2)}) collective-permute-start(bf16[544,256]{1,0:T(8,128)(2,1)S(1)} %pack.1.refs_0_), channel_id=1, source_target_pairs={{0,32},{16,48},{32,64},{48,80},{64,96},{80,112},{96,128},{112,144}... | collective-permute-start | bytes 835592 | tf_op jit(solution)/shard_map/ppermute | solution.py:31
  97.4 32.7 %copy-start.5 = (bf16[544,256]{1,0:T(8,128)(2,1)}, bf16[544,256]{1,0:T(8,128)(2,1)S(1)}, u32[]{:S(2)}) copy-start(bf16[544,256]{1,0:T(8,128)(2,1)S(1)} %collective-permute-done.6.refs_1_) | copy-start | bytes 835588
  97.4 9.8 %collective-permute-start.8 = (bf16[544,256]{1,0:T(8,128)(2,1)S(1)}, bf16[544,256]{1,0:T(8,128)(2,1)S(1)}, u32[]{:S(2)}, u32[]{:S(2)}) collective-permute-start(bf16[544,256]{1,0:T(8,128)(2,1)S(1)} %collective-permute-done.6.refs_1_), channel_id=1, source_target_pairs={{0,32},{16,48},{32,64},{48,80},{64,96},{80,112},{96,128},{112,144}... | collective-permute-start | bytes 835592 | tf_op jit(solution)/shard_map/ppermute | solution.py:31
  99.3 8.1 %collective-permute-start.9 = (bf16[544,256]{1,0:T(8,128)(2,1)S(1)}, bf16[544,256]{1,0:T(8,128)(2,1)S(1)}, u32[]{:S(2)}, u32[]{:S(2)}) collective-permute-start(bf16[544,256]{1,0:T(8,128)(2,1)S(1)} %collective-permute-done.7.refs_2_), channel_id=1, source_target_pairs={{0,992},{16,1008},{32,0},{48,16},{64,32},{80,48},{96,64},{112,80},... | collective-permute-start | bytes 835592 | tf_op jit(solution)/shard_map/ppermute | solution.py:31
  107.2 23.0 %copy-start.7 = (bf16[544,256]{1,0:T(8,128)(2,1)}, bf16[544,256]{1,0:T(8,128)(2,1)S(1)}, u32[]{:S(2)}) copy-start(bf16[544,256]{1,0:T(8,128)(2,1)S(1)} %collective-permute-done.8.refs_3_) | copy-start | bytes 835588
  107.4 22.8 %copy-start.9 = (bf16[544,256]{1,0:T(8,128)(2,1)}, bf16[544,256]{1,0:T(8,128)(2,1)S(1)}, u32[]{:S(2)}) copy-start(bf16[544,256]{1,0:T(8,128)(2,1)S(1)} %collective-permute-done.9.refs_4_) | copy-start | bytes 835588
  107.4 10.6 %collective-permute-start.10 = (bf16[544,256]{1,0:T(8,128)(2,1)S(1)}, bf16[544,256]{1,0:T(8,128)(2,1)S(1)}, u32[]{:S(2)}, u32[]{:S(2)}) collective-permute-start(bf16[544,256]{1,0:T(8,128)(2,1)S(1)} %collective-permute-done.8.refs_3_), channel_id=1, source_target_pairs={{0,32},{16,48},{32,64},{48,80},{64,96},{80,112},{96,128},{112,144}... | collective-permute-start | bytes 835592 | tf_op jit(solution)/shard_map/ppermute | solution.py:31
  109.3 10.5 %collective-permute-start.11 = (bf16[544,256]{1,0:T(8,128)(2,1)S(1)}, bf16[544,256]{1,0:T(8,128)(2,1)S(1)}, u32[]{:S(2)}, u32[]{:S(2)}) collective-permute-start(bf16[544,256]{1,0:T(8,128)(2,1)S(1)} %collective-permute-done.9.refs_4_), channel_id=1, source_target_pairs={{0,992},{16,1008},{32,0},{48,16},{64,32},{80,48},{96,64},{112,80},... | collective-permute-start | bytes 835592 | tf_op jit(solution)/shard_map/ppermute | solution.py:31
  119.8 10.2 %collective-permute-start.12 = (bf16[288,256]{1,0:T(8,128)(2,1)S(1)}, bf16[288,256]{1,0:T(8,128)(2,1)S(1)}, u32[]{:S(2)}, u32[]{:S(2)}) collective-permute-start(bf16[288,256]{1,0:T(8,128)(2,1)S(1)} %slice.10), channel_id=1, source_target_pairs={{0,32},{16,48},{32,64},{48,80},{64,96},{80,112},{96,128},{112,144}... | collective-permute-start | bytes 442376 | tf_op jit(solution)/shard_map/ppermute | solution.py:31
  121.7 22.5 %copy-start.15 = (s32[64]{0:T(128)S(1)}, s32[64]{0:T(128)}, u32[]{:S(2)}) copy-start(s32[64]{0:T(128)} %param.8) | copy-start | bytes 772
  121.7 8.3 %collective-permute-start.13 = (bf16[256,256]{1,0:T(8,128)(2,1)S(1)}, bf16[256,256]{1,0:T(8,128)(2,1)S(1)}, u32[]{:S(2)}, u32[]{:S(2)}) collective-permute-start(bf16[256,256]{1,0:T(8,128)(2,1)S(1)} %slice.11), channel_id=1, source_target_pairs={{0,992},{16,1008},{32,0},{48,16},{64,32},{80,48},{96,64},{112,80},... | collective-permute-start | bytes 393224 | tf_op jit(solution)/shard_map/ppermute | solution.py:31
  130.2 23.9 %copy-start.16 = (s32[32]{0:T(128)S(1)}, s32[32]{0:T(128)}, u32[]{:S(2)}) copy-start(s32[32]{0:T(128)} %constant.82.clone) | copy-start | bytes 388
  130.2 25.9 %collective-permute-start.14 = (bf16[4096,256]{1,0:T(8,128)(2,1)S(1)}, bf16[4096,256]{1,0:T(8,128)(2,1)}, u32[]{:S(2)}, u32[]{:S(2)}) collective-permute-start(bf16[4096,256]{1,0:T(8,128)(2,1)S(1)} %join.1.refs_0_), channel_id=1, source_target_pairs={{0,16},{16,0},{32,48},{48,32},{64,80},{80,64},{96,112},{112,96},{1... | collective-permute-start | bytes 6291464 | tf_op jit(solution)/shard_map/ppermute | solution.py:36
  144.3 1.0 copy-start.6
  145.2 1.0 copy-start.8
  146.2 1.0 copy-start.10
  147.2 0.7 copy-start.11
  147.9 15.0 %all-to-all-start.1 = ((f32[16,16,256]{2,1,0:T(8,128)}), f32[16,16,256]{2,1,0:T(8,128)S(1)}, u32[]{:S(2)}, u32[]{:S(2)}) async-start(f32[16,16,256]{2,1,0:T(8,128)} %copy-done.11), calls=%async_computation.1 | async-start | bytes 524288 | tf_op jit(solution)/shard_map/all_to_all | solution.py:337
  154.1 1.6 copy-start.2
  156.1 1.0 copy-start
  160.7 1.4 copy-start.3
  162.1 0.8 copy-start.12
  162.9 1.0 copy-start.1
  163.9 1.6 copy-start.4
  165.5 1.0 copy-start.13

commit v3 on v2

--- a/solution.py
+++ b/solution.py
@@ -12,10 +12,10 @@
 IBLK = 128
 ITERS = 3
 CORES = 2
-STRIDE = 8
+HOPS = 3
+STRIDE = 2 * HOPS + 1
 CHUNK = 256
-PACK = 4
-HOPS = 3
+MIB = 1024 * 1024
 
 ALPHA = 8.0
 LAMBDA = 1.0
@@ -24,7 +24,7 @@
 
 def chip_shift(value, chips, distance):
     pairs = [
-        (CORES * chip + core, CORES * ((chip + distance) % chips) + core)
+        (CORES * chip + core, CORES * ((chip + (1 - 2 * core) * distance) % chips) + core)
         for chip in range(chips)
         for core in range(CORES)
     ]
@@ -37,24 +37,24 @@
 
 
 def slot_table(chips):
-    pack_slot = {0: 0, 2 * STRIDE: 1, chips - STRIDE: 2, STRIDE: 3}
+    slots = [0, -STRIDE, STRIDE, -2 * STRIDE, 2 * STRIDE]
+    order = [slot - hop for hop in range(HOPS + 1) for slot in slots]
+    order += [slot + hop for hop in range(1, HOPS + 1) for slot in slots[:-1]]
     table = np.full((chips,), -1, np.int32)
-    for pack, offset in enumerate([0, -1, 1, -2, 2, -3, 3]):
-        for ahead, slot in pack_slot.items():
-            table[(offset + ahead) % chips] = PACK * pack + slot
-    for slot, ahead in enumerate([-4 - STRIDE, -4 + STRIDE, 4 - STRIDE, 4 + STRIDE]):
-        table[ahead % chips] = PACK * (2 * HOPS + 1) + slot
-    assert (table >= 0).all()
+    for place, distance in enumerate(order):
+        table[distance % chips] = place
+    assert len(order) == chips and (table >= 0).all()
     return table
 
 
 def pool_places(tile_users, chips, replicas, owned):
     member = tile_users // (owned * replicas)
+    core = member % CORES
     here = lax.axis_index("grp")
-    ahead = (member // CORES - here // CORES + chips) % chips
+    ahead = ((1 - 2 * core) * (member // CORES - here // CORES) + chips) % chips
     distances = np.arange(chips, dtype=np.int32)
     slot = jnp.sum(jnp.where(ahead[:, None] == distances, slot_table(chips), 0), axis=1)
-    other_core = (member % CORES != here % CORES).astype(jnp.int32)
+    other_core = (core != here % CORES).astype(jnp.int32)
     return ((other_core * chips + slot) * owned + tile_users % owned).astype(jnp.int32)
 
 
@@ -82,26 +82,25 @@
 
 SCALAR = pl.BlockSpec(memory_space=pltpu.SMEM)
 VECTOR = pl.BlockSpec(memory_space=pltpu.VMEM)
-PARAMS = pltpu.CompilerParams(vmem_limit_bytes=40 * 1024 * 1024)
-
-
-def gram_kernel(users_ref, gram_ref):
+
+
+def small_call(kernel, outs, name, *args):
+    return pl.pallas_call(
+        kernel,
+        out_shape=outs,
+        in_specs=[VECTOR] * len(args),
+        out_specs=jax.tree.map(lambda _: VECTOR, outs),
+        compiler_params=pltpu.CompilerParams(vmem_limit_bytes=8 * MIB),
+        name=name,
+    )(*args)
+
+
+def gram_kernel(users_ref, gram_ref, own_ref):
     high, low = high_low(users_ref[...])
+    own_ref[...] = high
     dims = (((0,), (0,)), ((), ()))
     product = functools.partial(lax.dot_general, dimension_numbers=dims, preferred_element_type=jnp.float32)
     gram_ref[...] = product(high, high) + (product(high, low) + product(low, high))
-
-
-def local_gram(users):
-    features = users.shape[1]
-    return pl.pallas_call(
-        gram_kernel,
-        out_shape=jax.ShapeDtypeStruct((features, features), jnp.float32),
-        in_specs=[VECTOR],
-        out_specs=VECTOR,
-        cost_estimate=pl.CostEstimate(flops=10**10, bytes_accessed=10**7, transcendentals=0),
-        name="local_gram",
-    )(users)
 
 
 def weight_kernel(counts_ref, weight_ref):
@@ -112,18 +111,6 @@
             first = (block * depth + start) // UROWS
             counts = counts_ref[first : first + tiles].reshape(IBLK, IBLK).astype(jnp.float32)
             weight_ref[block, :, start : start + IBLK] = (ALPHA * counts).T.astype(jnp.bfloat16)
-
-
-def item_weights(counts, blocks):
-    depth = counts.shape[0] * counts.shape[1] // blocks
-    return pl.pallas_call(
-        weight_kernel,
-        out_shape=jax.ShapeDtypeStruct((blocks, IBLK, depth), jnp.bfloat16),
-        in_specs=[VECTOR],
-        out_specs=VECTOR,
-        compiler_params=PARAMS,
-        name="item_weights",
-    )(counts)
 
 
 def tile_part(total, high, block, rows_ref, weight_ref):
@@ -175,7 +162,7 @@
         in_specs=[SCALAR] + [VECTOR] * (len(gathered) + 2),
         out_specs=(VECTOR, VECTOR),
         scratch_shapes=[pltpu.VMEM((pool_rows, features), jnp.bfloat16)],
-        compiler_params=PARAMS,
+        compiler_params=pltpu.CompilerParams(vmem_limit_bytes=20 * MIB),
         name="first_residue",
     )(places, *gathered, weight, items)
 
@@ -227,20 +214,9 @@
         in_specs=[VECTOR] * 5,
         out_specs=VECTOR,
         scratch_shapes=[square, square, state, state, state],
-        compiler_params=PARAMS,
+        compiler_params=pltpu.CompilerParams(vmem_limit_bytes=16 * MIB),
         name="solve_steps",
     )(rows, weight, items, started, gram)
-
-
-def small_call(kernel, outs, name, *args):
-    return pl.pallas_call(
-        kernel,
-        out_shape=outs,
-        in_specs=[VECTOR] * len(args),
-        out_specs=jax.tree.map(lambda _: VECTOR, outs),
-        compiler_params=PARAMS,
-        name=name,
-    )(*args)
 
 
 def put_parts(ref, start, value):
@@ -248,26 +224,24 @@
     ref[start : start + count, :], ref[start + count : start + 2 * count, :] = high_low(value)
 
 
-def far_kernel(below_ref, above_ref, mine_ref, other_ref, up_ref, down_ref, total_ref):
-    half = below_ref.shape[0] // 2
-    total = mine_ref[...] + other_ref[...]
-    total_ref[...] = total
-    up_ref[:half, :] = below_ref[:half, :]
-    down_ref[:half, :] = above_ref[half:, :]
-    put_parts(up_ref, half, total)
-    put_parts(down_ref, half, total)
-
-
-def pack_kernel(own_ref, below_ref, above_ref, up_ref, down_ref, total_ref, farthest_ref, pack_ref):
+def own_kernel(own_ref, mine_ref, other_ref, out_ref):
     rows = own_ref.shape[0]
-    half = rows // 2
-    pack_ref[:rows, :] = own_ref[...]
-    pack_ref[rows : rows + half, :] = up_ref[:half, :]
-    pack_ref[rows + half : 2 * rows, :] = down_ref[:half, :]
-    pack_ref[2 * rows : 3 * rows, :] = below_ref[...]
-    pack_ref[3 * rows : 4 * rows, :] = above_ref[...]
-    total = total_ref[...] + (merge(up_ref[half:, :]) + merge(down_ref[half:, :])) + merge(farthest_ref[...])
-    put_parts(pack_ref, PACK * rows, total)
+    out_ref[:rows, :] = own_ref[...]
+    put_parts(out_ref, rows, mine_ref[...] + other_ref[...])
+
+
+def pack_kernel(rows, *refs):
+    parts, (up_ref, down_ref) = refs[:-2], refs[-2:]
+    total = None
+    for place, part in enumerate(parts):
+        up_ref[place * rows : (place + 1) * rows, :] = part[:rows, :]
+        if place < len(parts) - 1:
+            down_ref[place * rows : (place + 1) * rows, :] = part[:rows, :]
+        else:
+            put_parts(down_ref, place * rows, total)
+        piece = merge(part[rows:, :])
+        total = piece if total is None else total + piece
+    put_parts(up_ref, len(parts) * rows, total)
 
 
 def join_kernel(counts, *refs):
@@ -294,51 +268,56 @@
     chips = lax.axis_size("grp") // CORES
     replicas = lax.axis_size("rep")
     owned_rows, features = user_factors.shape
+    blocks = item_factors.shape[0] // IBLK
     share = features // replicas
-    half = owned_rows // 2
-    pack_rows = PACK * owned_rows
+    parts = 2 * share
     shift = functools.partial(chip_shift, chips=chips)
     bar = lax.optimization_barrier
 
     def half_rows(count):
         return jax.ShapeDtypeStruct((count, features), jnp.bfloat16)
 
-    piece = jax.ShapeDtypeStruct((share, features), jnp.float32)
-
-    own = user_factors.astype(jnp.bfloat16)
-    below, above = shift(own, distance=STRIDE), shift(own, distance=-STRIDE)
-    pieces = lax.all_to_all(local_gram(user_factors), "rep", 0, 0, tiled=True)
+    square = jax.ShapeDtypeStruct((features, features), jnp.float32)
+    gram, own = small_call(gram_kernel, (square, half_rows(owned_rows)), "local_gram", user_factors)
+    pieces = lax.all_to_all(gram, "rep", 0, 0, tiled=True)
     gram = jnp.sum(pieces.reshape(replicas, share, features), axis=0)
-    gram_other = core_swap(gram, chips)
-    below, above, gram, gram_other = bar((below, above, gram, gram_other))
-
-    sent = half_rows(half + 2 * share)
-    to_up, to_down, total = small_call(far_kernel, (sent, sent, piece), "far_parts", below, above, gram, gram_other)
-    far_up, far_down = bar((shift(to_up, distance=STRIDE), shift(to_down, distance=-STRIDE)))
-    farthest = shift(far_up[half:], distance=STRIDE)
-    pack = small_call(
-        pack_kernel, half_rows(pack_rows + 2 * share), "pack", own, below, above, far_up, far_down, total, farthest
-    )
-
-    gathered = [pack]
-    up, down = pack, pack
-    for hop in range(HOPS + 1):
-        last = hop == HOPS
-        up = shift(up[pack_rows // 2 :] if last else up, distance=1)
-        down = shift(down[pack_rows // 2 : pack_rows] if last else down, distance=-1)
-        up, down = bar((up, down))
-        gathered += [up, down]
-    near = join(gathered, [pack_rows] * (2 * HOPS + 1) + [pack_rows // 2] * 2)
+    own = small_call(own_kernel, half_rows(owned_rows + parts), "own", own, gram, core_swap(gram, chips))
+
+    below, above = bar((shift(own, distance=STRIDE), shift(own, distance=-STRIDE)))
+    far_below, far_above = bar((shift(below, distance=STRIDE), shift(above, distance=-STRIDE)))
+    up, down = small_call(
+        functools.partial(pack_kernel, owned_rows),
+        (half_rows(5 * owned_rows + parts), half_rows(4 * owned_rows + parts)),
+        "pack",
+        own,
+        below,
+        above,
+        far_below,
+        far_above,
+    )
+    ups, downs = [up], []
+    weight = small_call(
+        weight_kernel,
+        jax.ShapeDtypeStruct((blocks, IBLK, tile_counts.shape[0] * UROWS // blocks), jnp.bfloat16),
+        "item_weights",
+        tile_counts,
+    )
+    places = pool_places(tile_users, chips, replicas, owned_rows // UROWS)
+    for hop in range(HOPS):
+        up, down = shift(up, distance=1), shift(down, distance=-1)
+        if hop == 0:
+            up, down, weight, places = bar((up, down, weight, places))
+        else:
+            up, down = bar((up, down))
+        ups.append(up)
+        downs.append(down)
+
+    near = join(ups + downs, [5 * owned_rows] * (HOPS + 1) + [4 * owned_rows] * HOPS)
     other = core_swap(near, chips)
-
     spread = small_call(
-        spread_kernel, jax.ShapeDtypeStruct((replicas, share, features), jnp.float32), "spread", *gathered[:-1]
+        spread_kernel, jax.ShapeDtypeStruct((replicas, share, features), jnp.float32), "spread", *ups, *downs
     )
     gram = lax.all_to_all(spread.reshape(features, features), "rep", 0, 0, tiled=True)
-
-    owned = owned_rows // UROWS
-    places = pool_places(tile_users, chips, replicas, owned)
-    weight = item_weights(tile_counts, item_factors.shape[0] // IBLK)
     rows, started = first_residue(places, [near, other], weight, item_factors)
     return solve_steps(rows, weight, item_factors, started, gram)
 

time: 174 us -> 146 us (0.84)
  starting transfers between devices: 113 us -> 64.5 us
  blocking collectives: 0 us -> 14.9 us
  waiting for transfers between devices: 35.2 us -> 40.6 us
    ppermute x13 -> x10, starting transfers between devices: 81.8 us -> 46.4 us  [chip_shift(): return lax.ppermute(value, 'grp', pairs)]
    all_to_all x0 -> x1, blocking collectives: none -> 14.9 us  [on_device(): pieces = lax.all_to_all(gram, 'rep', 0, 0, tiled=True)]
    all_to_all x1 -> x0, starting transfers between devices: 7.58 us -> none  [on_device(): pieces = lax.all_to_all(local_gram(user_factors), 'rep', 0, 0, tiled=True)]
    ppermute x13 -> x10, waiting for transfers between devices: 35.2 us -> 38 us  [chip_shift(): return lax.ppermute(value, 'grp', pairs)]
    ppermute x2, starting transfers between devices: 17.2 us -> 14.6 us  [core_swap(): return lax.ppermute(value, 'grp', pairs)]
    all_to_all x1, starting transfers between devices: 6.13 us -> 3.53 us  [on_device(): lax.all_to_all(spread.reshape(features, features), 'rep', 0, 0, tiled=True)]
    pallas_call x2 -> x0, Pallas kernels: 2.33 us -> none  [the longest x1 1.97 us: local_gram(): pl.pallas_call(gram_kernel, out_shape=jax.ShapeDtypeStruct((features, fea...]
    all_to_all x1, waiting for transfers between devices: 0.01 us -> 1.79 us  [on_device(): lax.all_to_all(spread.reshape(features, features), 'rep', 0, 0, tiled=True)]
  transfers between devices with their start and end apart: 17 -> 13, of which waited for: 10 -> 9; matrix products, arithmetic and copies ran while one was open for 0% -> 1% of each run, Pallas kernels for 2% -> 3%
where the time goes in v3:
time: 146 us
  starting transfers between devices  64.5 us (44%)
  waiting for transfers between devices  40.6 us (28%)
  blocking collectives  14.9 us (10%)
  local copies, waits for them, and re-layouts  13.4 us (9%)
  Pallas kernels  10.4 us (7%)
  other arithmetic  1.47 us (1%)
    ppermute x10, starting transfers between devices, chip_shift(): return lax.ppermute(value, 'grp', pairs)  46.4 us
    ppermute x10, waiting for transfers between devices, chip_shift(): return lax.ppermute(value, 'grp', pairs)  38 us
    all_to_all x1, blocking collectives, on_device(): pieces = lax.all_to_all(gram, 'rep', 0, 0, tiled=True)  14.9 us
    ppermute x2, starting transfers between devices, core_swap(): return lax.ppermute(value, 'grp', pairs)  14.6 us
    unnamed x28, local copies, waits for them, and re-layouts  13.4 us
    pallas_call x1, Pallas kernels, solve_steps(): pl.pallas_call(steps_kernel, out_shape=jax.ShapeDtypeStruct(items.shape,...  6.06 us
    all_to_all x1, starting transfers between devices, on_device(): lax.all_to_all(spread.reshape(features, features), 'rep', 0, 0, tiled=True)  3.53 us
    pallas_call x1, Pallas kernels, first_residue(): pl.pallas_call(first_kernel, out_shape=(jax.ShapeDtypeStruct((blocks * de...  3.52 us
  transfers between devices with their start and end apart: 13, of which 9 were waited for; matrix products, arithmetic and copies ran while one was open for 1% of the time, Pallas kernels for 3%

profile of v3, /device:TPU:1, one launch (start us, length us, event | category | flops | bytes accessed | tf_op | source)
XLA Modules:
  0.0 145.6 jit_solution(13991364273203825120)
XLA Ops:
  0.0 0.9 copy-done.12
  0.9 0.3 local_gram.1
  1.2 14.9 %all_to_all.17 = f32[16,16,256]{2,1,0:T(8,128)S(1)} all-to-all(f32[16,16,256]{2,1,0:T(8,128)S(1)} %bitcast.3), channel_id=1, replica_groups=mesh['grp'=64,'rep'=16] {'rep'}, dimensions={0} | all-to-all | bytes 524288 | tf_op jit(solution)/shard_map/all_to_all | solution.py:282
  16.2 12.4 %collective-permute-start = (f32[16,256]{1,0:T(8,128)S(1)}, f32[16,256]{1,0:T(8,128)S(1)}, u32[]{:S(2)}, u32[]{:S(2)}) collective-permute-start(f32[16,256]{1,0:T(8,128)S(1)} %reduce_sum.18.mine_ref), channel_id=1, source_target_pairs={{0,16},{16,0},{32,48},{48,32},{64,80},{80,64},{96,112},{112,96},{1... | collective-permute-start | bytes 49160 | tf_op jit(solution)/shard_map/ppermute | solution.py:36
  28.6 0.8 collective-permute-done.other_ref
  29.4 4.5 %collective-permute-start.2 = (bf16[160,256]{1,0:T(8,128)(2,1)S(1)}, bf16[160,256]{1,0:T(8,128)(2,1)S(1)}, u32[]{:S(2)}, u32[]{:S(2)}) collective-permute-start(bf16[160,256]{1,0:T(8,128)(2,1)S(1)} %own.1.refs_0_), channel_id=1, source_target_pairs={{0,800},{16,240},{32,832},{48,272},{64,864},{80,304},{96,896},{112... | collective-permute-start | bytes 245768 | tf_op jit(solution)/shard_map/ppermute | solution.py:31
  33.9 11.3 %collective-permute-start.1 = (bf16[160,256]{1,0:T(8,128)(2,1)S(1)}, bf16[160,256]{1,0:T(8,128)(2,1)S(1)}, u32[]{:S(2)}, u32[]{:S(2)}) collective-permute-start(bf16[160,256]{1,0:T(8,128)(2,1)S(1)} %own.1.refs_0_), channel_id=1, source_target_pairs={{0,224},{16,816},{32,256},{48,848},{64,288},{80,880},{96,320},{112... | collective-permute-start | bytes 245768 | tf_op jit(solution)/shard_map/ppermute | solution.py:31
  45.2 0.1 collective-permute-done.2.refs_2_
  45.4 11.5 %collective-permute-done.1.refs_1_ = bf16[160,256]{1,0:T(8,128)(2,1)S(1)} collective-permute-done((bf16[160,256]{1,0:T(8,128)(2,1)S(1)}, bf16[160,256]{1,0:T(8,128)(2,1)S(1)}, u32[]{:S(2)}, u32[]{:S(2)}) %collective-permute-start.1) | collective-permute-done | bytes 81952 | tf_op jit(solution)/shard_map/ppermute | solution.py:31
  56.9 11.9 %collective-permute-start.3 = (bf16[160,256]{1,0:T(8,128)(2,1)S(1)}, bf16[160,256]{1,0:T(8,128)(2,1)S(1)}, u32[]{:S(2)}, u32[]{:S(2)}) collective-permute-start(bf16[160,256]{1,0:T(8,128)(2,1)S(1)} %collective-permute-done.1.refs_1_), channel_id=1, source_target_pairs={{0,224},{16,816},{32,256},{48,848},{64,288},{80,880},{96,320},{112... | collective-permute-start | bytes 245768 | tf_op jit(solution)/shard_map/ppermute | solution.py:31
  68.8 1.9 %collective-permute-start.4 = (bf16[160,256]{1,0:T(8,128)(2,1)S(1)}, bf16[160,256]{1,0:T(8,128)(2,1)S(1)}, u32[]{:S(2)}, u32[]{:S(2)}) collective-permute-start(bf16[160,256]{1,0:T(8,128)(2,1)S(1)} %collective-permute-done.2.refs_2_), channel_id=1, source_target_pairs={{0,800},{16,240},{32,832},{48,272},{64,864},{80,304},{96,896},{112... | collective-permute-start | bytes 245768 | tf_op jit(solution)/shard_map/ppermute | solution.py:31
  70.8 2.2 %collective-permute-done.3.refs_3_ = bf16[160,256]{1,0:T(8,128)(2,1)S(1)} collective-permute-done((bf16[160,256]{1,0:T(8,128)(2,1)S(1)}, bf16[160,256]{1,0:T(8,128)(2,1)S(1)}, u32[]{:S(2)}, u32[]{:S(2)}) %collective-permute-start.3) | collective-permute-done | bytes 81952 | tf_op jit(solution)/shard_map/ppermute | solution.py:31
  72.9 9.9 %collective-permute-done.4.refs_4_ = bf16[160,256]{1,0:T(8,128)(2,1)S(1)} collective-permute-done((bf16[160,256]{1,0:T(8,128)(2,1)S(1)}, bf16[160,256]{1,0:T(8,128)(2,1)S(1)}, u32[]{:S(2)}, u32[]{:S(2)}) %collective-permute-start.4) | collective-permute-done | bytes 81952 | tf_op jit(solution)/shard_map/ppermute | solution.py:31
  82.9 1.9 %collective-permute-start.5 = (bf16[672,256]{1,0:T(8,128)(2,1)S(1)}, bf16[672,256]{1,0:T(8,128)(2,1)S(1)}, u32[]{:S(2)}, u32[]{:S(2)}) collective-permute-start(bf16[672,256]{1,0:T(8,128)(2,1)S(1)} %get-tuple-element.29.refs_0_), channel_id=1, source_target_pairs={{0,32},{16,1008},{32,64},{48,16},{64,96},{80,48},{96,128},{112,80}... | collective-permute-start | bytes 1032200 | tf_op jit(solution)/shard_map/ppermute | solution.py:31
  84.8 0.7 and_select_fusion.1
  85.5 3.5 %collective-permute-start.6 = (bf16[544,256]{1,0:T(8,128)(2,1)S(1)}, bf16[544,256]{1,0:T(8,128)(2,1)S(1)}, u32[]{:S(2)}, u32[]{:S(2)}) collective-permute-start(bf16[544,256]{1,0:T(8,128)(2,1)S(1)} %get-tuple-element.30), channel_id=1, source_target_pairs={{0,992},{16,48},{32,0},{48,80},{64,32},{80,112},{96,64},{112,144},... | collective-permute-start | bytes 835592 | tf_op jit(solution)/shard_map/ppermute | solution.py:31
  89.0 0.7 select_reduce_fusion
  89.7 0.0 copy-start.2
  89.8 1.6 %copy-done.2 = s32[64,64,128]{2,1,0:T(8,128)S(1)} copy-done((s32[64,64,128]{2,1,0:T(8,128)S(1)}, s32[64,64,128]{2,1,0:T(8,128)}, u32[]{:S(2)}) %copy-start.2) | copy-done | bytes 2097176
  91.3 0.4 item_weights.1.refs_2_.weight_ref
  91.7 2.3 %collective-permute-done.6.refs_4_ = bf16[544,256]{1,0:T(8,128)(2,1)S(1)} collective-permute-done((bf16[544,256]{1,0:T(8,128)(2,1)S(1)}, bf16[544,256]{1,0:T(8,128)(2,1)S(1)}, u32[]{:S(2)}, u32[]{:S(2)}) %collective-permute-start.6) | collective-permute-done | bytes 278560 | tf_op jit(solution)/shard_map/ppermute | solution.py:31
  94.0 0.0 collective-permute-done.5.refs_1_
  94.0 4.2 %collective-permute-start.7 = (bf16[672,256]{1,0:T(8,128)(2,1)S(1)}, bf16[672,256]{1,0:T(8,128)(2,1)S(1)}, u32[]{:S(2)}, u32[]{:S(2)}) collective-permute-start(bf16[672,256]{1,0:T(8,128)(2,1)S(1)} %collective-permute-done.5.refs_1_), channel_id=1, source_target_pairs={{0,32},{16,1008},{32,64},{48,16},{64,96},{80,48},{96,128},{112,80}... | collective-permute-start | bytes 1032200 | tf_op jit(solution)/shard_map/ppermute | solution.py:31
  98.2 0.0 copy-start.5
  98.2 0.7 copy-done.5
  98.9 1.9 %collective-permute-start.8 = (bf16[544,256]{1,0:T(8,128)(2,1)S(1)}, bf16[544,256]{1,0:T(8,128)(2,1)S(1)}, u32[]{:S(2)}, u32[]{:S(2)}) collective-permute-start(bf16[544,256]{1,0:T(8,128)(2,1)S(1)} %collective-permute-done.6.refs_4_), channel_id=1, source_target_pairs={{0,992},{16,48},{32,0},{48,80},{64,32},{80,112},{96,64},{112,144},... | collective-permute-start | bytes 835592 | tf_op jit(solution)/shard_map/ppermute | solution.py:31
  100.9 0.7 copy-done.7
  101.5 5.9 %collective-permute-done.8.refs_5_ = bf16[544,256]{1,0:T(8,128)(2,1)S(1)} collective-permute-done((bf16[544,256]{1,0:T(8,128)(2,1)S(1)}, bf16[544,256]{1,0:T(8,128)(2,1)S(1)}, u32[]{:S(2)}, u32[]{:S(2)}) %collective-permute-start.8) | collective-permute-done | bytes 278560 | tf_op jit(solution)/shard_map/ppermute | solution.py:31
  107.4 0.0 collective-permute-done.7.refs_2_
  107.4 2.7 %collective-permute-start.9 = (bf16[672,256]{1,0:T(8,128)(2,1)S(1)}, bf16[672,256]{1,0:T(8,128)(2,1)S(1)}, u32[]{:S(2)}, u32[]{:S(2)}) collective-permute-start(bf16[672,256]{1,0:T(8,128)(2,1)S(1)} %collective-permute-done.7.refs_2_), channel_id=1, source_target_pairs={{0,32},{16,1008},{32,64},{48,16},{64,96},{80,48},{96,128},{112,80}... | collective-permute-start | bytes 1032200 | tf_op jit(solution)/shard_map/ppermute | solution.py:31
  110.1 2.6 %collective-permute-start.10 = (bf16[544,256]{1,0:T(8,128)(2,1)S(1)}, bf16[544,256]{1,0:T(8,128)(2,1)S(1)}, u32[]{:S(2)}, u32[]{:S(2)}) collective-permute-start(bf16[544,256]{1,0:T(8,128)(2,1)S(1)} %collective-permute-done.8.refs_5_), channel_id=1, source_target_pairs={{0,992},{16,48},{32,0},{48,80},{64,32},{80,112},{96,64},{112,144},... | collective-permute-start | bytes 835592 | tf_op jit(solution)/shard_map/ppermute | solution.py:31
  112.7 6.1 %collective-permute-done.10.refs_6_ = bf16[544,256]{1,0:T(8,128)(2,1)S(1)} collective-permute-done((bf16[544,256]{1,0:T(8,128)(2,1)S(1)}, bf16[544,256]{1,0:T(8,128)(2,1)S(1)}, u32[]{:S(2)}, u32[]{:S(2)}) %collective-permute-start.10) | collective-permute-done | bytes 278560 | tf_op jit(solution)/shard_map/ppermute | solution.py:31
  118.9 1.0 copy-done.6
  119.8 1.0 copy-done.8
  120.8 0.1 join.1.refs_0_
  120.9 2.1 %collective-permute-start.11 = (bf16[4096,256]{1,0:T(8,128)(2,1)S(1)}, bf16[4096,256]{1,0:T(8,128)(2,1)}, u32[]{:S(2)}, u32[]{:S(2)}) collective-permute-start(bf16[4096,256]{1,0:T(8,128)(2,1)S(1)} %join.1.refs_0_), channel_id=1, source_target_pairs={{0,16},{16,0},{32,48},{48,32},{64,80},{80,64},{96,112},{112,96},{1... | collective-permute-start | bytes 6291464 | tf_op jit(solution)/shard_map/ppermute | solution.py:36
  123.1 0.7 copy-done.9
  123.8 3.5 %all-to-all-start.1 = ((f32[16,16,256]{2,1,0:T(8,128)}), f32[16,16,256]{2,1,0:T(8,128)S(1)}, u32[]{:S(2)}, u32[]{:S(2)}) async-start(f32[16,16,256]{2,1,0:T(8,128)} %copy-done.9), calls=%async_computation.1 | async-start | bytes 524288 | tf_op jit(solution)/shard_map/all_to_all | solution.py:320
  127.4 0.0 copy-start
  127.4 1.0 copy-done
  128.4 3.5 %first_residue.1 = (bf16[4096,256]{1,0:T(8,128)(2,1)S(1)}, f32[512,256]{1,0:T(8,128)S(1)}) custom-call(s32[64]{0:T(128)S(1)} %fusion.places_ref, bf16[4096,256]{1,0:T(8,128)(2,1)S(1)} %join.1.refs_0_, bf16[4096,256]{1,0:T(8,128)(2,1)} %collective-permute-done.11.refs_1_, bf16[4,128,1024]{2,1,0:T(8,128)(2,1)S(1)} %item_weights.1.refs_2_.weight_ref, ...), custom_call_target="tpu_custom_call" | custom-call | tf_op jit(solution)/shard_map/first_residue/pallas_call | solution.py:156
  131.9 1.3 copy-done.3
  133.3 0.8 copy-done.10
  134.1 1.8 %all-to-all-done.1 = f32[16,16,256]{2,1,0:T(8,128)S(1)} async-done(((f32[16,16,256]{2,1,0:T(8,128)}), f32[16,16,256]{2,1,0:T(8,128)S(1)}, u32[]{:S(2)}, u32[]{:S(2)}) %all-to-all-start.1) | async-done | bytes 262176 | tf_op jit(solution)/shard_map/all_to_all | solution.py:320
  135.9 1.0 copy-done.1
  136.9 1.6 %copy-done.4 = bf16[4096,256]{1,0:T(8,128)(2,1)S(1)} copy-done((bf16[4096,256]{1,0:T(8,128)(2,1)S(1)}, bf16[4096,256]{1,0:T(8,128)(2,1)}, u32[]{:S(2)}) %copy-start.4) | copy-done | bytes 2097176
  138.5 1.0 copy-done.11
  139.5 6.1 %solve_steps.1 = f32[512,256]{1,0:T(8,128)} custom-call(bf16[4096,256]{1,0:T(8,128)(2,1)S(1)} %copy-done.4, bf16[4,128,1024]{2,1,0:T(8,128)(2,1)S(1)} %item_weights.1.refs_2_.weight_ref, f32[512,256]{1,0:T(8,128)S(1)} %copy-done.1, f32[512,256]{1,0:T(8,128)S(1)} %copy-done.11, f32[256,256]{1,0:T(8,128)S(1)} %bitcast.2), custom_call_target="tpu_custom_call" | custom-call | tf_op jit(solution)/shard_map/solve_steps/pallas_call | solution.py:211
  (19 shorter events, 0.2 us)
Async XLA Ops:
  0.0 0.9 copy-start.12
  16.1 75.6 %copy-start.13 = (s32[64]{0:T(128)S(1)}, s32[64]{0:T(128)}, u32[]{:S(2)}) copy-start(s32[64]{0:T(128)} %param.8) | copy-start | bytes 772
  16.2 13.2 %collective-permute-start = (f32[16,256]{1,0:T(8,128)S(1)}, f32[16,256]{1,0:T(8,128)S(1)}, u32[]{:S(2)}, u32[]{:S(2)}) collective-permute-start(f32[16,256]{1,0:T(8,128)S(1)} %reduce_sum.18.mine_ref), channel_id=1, source_target_pairs={{0,16},{16,0},{32,48},{48,32},{64,80},{80,64},{96,112},{112,96},{1... | collective-permute-start | bytes 49160 | tf_op jit(solution)/shard_map/ppermute | solution.py:36
  29.4 15.9 %collective-permute-start.2 = (bf16[160,256]{1,0:T(8,128)(2,1)S(1)}, bf16[160,256]{1,0:T(8,128)(2,1)S(1)}, u32[]{:S(2)}, u32[]{:S(2)}) collective-permute-start(bf16[160,256]{1,0:T(8,128)(2,1)S(1)} %own.1.refs_0_), channel_id=1, source_target_pairs={{0,800},{16,240},{32,832},{48,272},{64,864},{80,304},{96,896},{112... | collective-permute-start | bytes 245768 | tf_op jit(solution)/shard_map/ppermute | solution.py:31
  33.9 23.0 %collective-permute-start.1 = (bf16[160,256]{1,0:T(8,128)(2,1)S(1)}, bf16[160,256]{1,0:T(8,128)(2,1)S(1)}, u32[]{:S(2)}, u32[]{:S(2)}) collective-permute-start(bf16[160,256]{1,0:T(8,128)(2,1)S(1)} %own.1.refs_0_), channel_id=1, source_target_pairs={{0,224},{16,816},{32,256},{48,848},{64,288},{80,880},{96,320},{112... | collective-permute-start | bytes 245768 | tf_op jit(solution)/shard_map/ppermute | solution.py:31
  56.9 16.0 %collective-permute-start.3 = (bf16[160,256]{1,0:T(8,128)(2,1)S(1)}, bf16[160,256]{1,0:T(8,128)(2,1)S(1)}, u32[]{:S(2)}, u32[]{:S(2)}) collective-permute-start(bf16[160,256]{1,0:T(8,128)(2,1)S(1)} %collective-permute-done.1.refs_1_), channel_id=1, source_target_pairs={{0,224},{16,816},{32,256},{48,848},{64,288},{80,880},{96,320},{112... | collective-permute-start | bytes 245768 | tf_op jit(solution)/shard_map/ppermute | solution.py:31
  68.8 14.0 %collective-permute-start.4 = (bf16[160,256]{1,0:T(8,128)(2,1)S(1)}, bf16[160,256]{1,0:T(8,128)(2,1)S(1)}, u32[]{:S(2)}, u32[]{:S(2)}) collective-permute-start(bf16[160,256]{1,0:T(8,128)(2,1)S(1)} %collective-permute-done.2.refs_2_), channel_id=1, source_target_pairs={{0,800},{16,240},{32,832},{48,272},{64,864},{80,304},{96,896},{112... | collective-permute-start | bytes 245768 | tf_op jit(solution)/shard_map/ppermute | solution.py:31
  82.9 11.1 %collective-permute-start.5 = (bf16[672,256]{1,0:T(8,128)(2,1)S(1)}, bf16[672,256]{1,0:T(8,128)(2,1)S(1)}, u32[]{:S(2)}, u32[]{:S(2)}) collective-permute-start(bf16[672,256]{1,0:T(8,128)(2,1)S(1)} %get-tuple-element.29.refs_0_), channel_id=1, source_target_pairs={{0,32},{16,1008},{32,64},{48,16},{64,96},{80,48},{96,128},{112,80}... | collective-permute-start | bytes 1032200 | tf_op jit(solution)/shard_map/ppermute | solution.py:31
  85.5 8.5 %collective-permute-start.6 = (bf16[544,256]{1,0:T(8,128)(2,1)S(1)}, bf16[544,256]{1,0:T(8,128)(2,1)S(1)}, u32[]{:S(2)}, u32[]{:S(2)}) collective-permute-start(bf16[544,256]{1,0:T(8,128)(2,1)S(1)} %get-tuple-element.30), channel_id=1, source_target_pairs={{0,992},{16,48},{32,0},{48,80},{64,32},{80,112},{96,64},{112,144},... | collective-permute-start | bytes 835592 | tf_op jit(solution)/shard_map/ppermute | solution.py:31
  89.7 1.6 %copy-start.2 = (s32[64,64,128]{2,1,0:T(8,128)S(1)}, s32[64,64,128]{2,1,0:T(8,128)}, u32[]{:S(2)}) copy-start(s32[64,64,128]{2,1,0:T(8,128)} %counts_ref.1) | copy-start | bytes 6291460
  94.0 13.4 %collective-permute-start.7 = (bf16[672,256]{1,0:T(8,128)(2,1)S(1)}, bf16[672,256]{1,0:T(8,128)(2,1)S(1)}, u32[]{:S(2)}, u32[]{:S(2)}) collective-permute-start(bf16[672,256]{1,0:T(8,128)(2,1)S(1)} %collective-permute-done.5.refs_1_), channel_id=1, source_target_pairs={{0,32},{16,1008},{32,64},{48,16},{64,96},{80,48},{96,128},{112,80}... | collective-permute-start | bytes 1032200 | tf_op jit(solution)/shard_map/ppermute | solution.py:31
  98.2 0.7 copy-start.5
  98.9 8.5 %collective-permute-start.8 = (bf16[544,256]{1,0:T(8,128)(2,1)S(1)}, bf16[544,256]{1,0:T(8,128)(2,1)S(1)}, u32[]{:S(2)}, u32[]{:S(2)}) collective-permute-start(bf16[544,256]{1,0:T(8,128)(2,1)S(1)} %collective-permute-done.6.refs_4_), channel_id=1, source_target_pairs={{0,992},{16,48},{32,0},{48,80},{64,32},{80,112},{96,64},{112,144},... | collective-permute-start | bytes 835592 | tf_op jit(solution)/shard_map/ppermute | solution.py:31
  100.8 0.7 copy-start.7
  107.4 11.4 %collective-permute-start.9 = (bf16[672,256]{1,0:T(8,128)(2,1)S(1)}, bf16[672,256]{1,0:T(8,128)(2,1)S(1)}, u32[]{:S(2)}, u32[]{:S(2)}) collective-permute-start(bf16[672,256]{1,0:T(8,128)(2,1)S(1)} %collective-permute-done.7.refs_2_), channel_id=1, source_target_pairs={{0,32},{16,1008},{32,64},{48,16},{64,96},{80,48},{96,128},{112,80}... | collective-permute-start | bytes 1032200 | tf_op jit(solution)/shard_map/ppermute | solution.py:31
  110.1 8.8 %collective-permute-start.10 = (bf16[544,256]{1,0:T(8,128)(2,1)S(1)}, bf16[544,256]{1,0:T(8,128)(2,1)S(1)}, u32[]{:S(2)}, u32[]{:S(2)}) collective-permute-start(bf16[544,256]{1,0:T(8,128)(2,1)S(1)} %collective-permute-done.8.refs_5_), channel_id=1, source_target_pairs={{0,992},{16,48},{32,0},{48,80},{64,32},{80,112},{96,64},{112,144},... | collective-permute-start | bytes 835592 | tf_op jit(solution)/shard_map/ppermute | solution.py:31
  118.9 1.0 copy-start.6
  119.8 1.0 copy-start.8
  120.9 6.4 %collective-permute-start.11 = (bf16[4096,256]{1,0:T(8,128)(2,1)S(1)}, bf16[4096,256]{1,0:T(8,128)(2,1)}, u32[]{:S(2)}, u32[]{:S(2)}) collective-permute-start(bf16[4096,256]{1,0:T(8,128)(2,1)S(1)} %join.1.refs_0_), channel_id=1, source_target_pairs={{0,16},{16,0},{32,48},{48,32},{64,80},{80,64},{96,112},{112,96},{1... | collective-permute-start | bytes 6291464 | tf_op jit(solution)/shard_map/ppermute | solution.py:36
  123.1 0.7 copy-start.9
  123.8 12.0 %all-to-all-start.1 = ((f32[16,16,256]{2,1,0:T(8,128)}), f32[16,16,256]{2,1,0:T(8,128)S(1)}, u32[]{:S(2)}, u32[]{:S(2)}) async-start(f32[16,16,256]{2,1,0:T(8,128)} %copy-done.9), calls=%async_computation.1 | async-start | bytes 524288 | tf_op jit(solution)/shard_map/all_to_all | solution.py:320
  127.4 1.0 copy-start
  131.9 1.3 copy-start.3
  133.3 0.8 copy-start.10
  135.9 1.0 copy-start.1
  136.9 1.6 %copy-start.4 = (bf16[4096,256]{1,0:T(8,128)(2,1)S(1)}, bf16[4096,256]{1,0:T(8,128)(2,1)}, u32[]{:S(2)}) copy-start(bf16[4096,256]{1,0:T(8,128)(2,1)} %copy-done.3) | copy-start | bytes 6291460
  138.5 1.0 copy-start.11

commit v4 on v3

--- a/solution.py
+++ b/solution.py
@@ -82,6 +82,11 @@
 
 SCALAR = pl.BlockSpec(memory_space=pltpu.SMEM)
 VECTOR = pl.BlockSpec(memory_space=pltpu.VMEM)
+OUTER = pl.BlockSpec(memory_space=pltpu.HBM)
+
+
+def outer(value):
+    return pltpu.with_memory_space_constraint(value, pltpu.HBM)
 
 
 def small_call(kernel, outs, name, *args):
@@ -123,20 +128,38 @@
     return total
 
 
-def first_kernel(places_ref, *refs):
-    gathered, (weight_ref, items_ref, rows_ref, residue_ref, pool_ref) = refs[:-5], refs[-5:]
-    filled = 0
-    for part in gathered:
-        pool_ref[filled : filled + part.shape[0], :] = part[...]
-        filled += part.shape[0]
+def first_kernel(
+    places_ref, near_ref, other_ref, weight_in_ref, items_in_ref, rows_out_ref, started_out_ref, rows_ref, weight_ref,
+    items_ref, started_ref, sems,
+):
+    near_blocks = near_ref.shape[0] // UROWS
+    bring_weight = pltpu.make_async_copy(weight_in_ref, weight_ref, sems.at[0])
+    bring_items = pltpu.make_async_copy(items_in_ref, items_ref, sems.at[1])
+    bring_weight.start()
+    bring_items.start()
 
     def fetch(tile, carry):
-        to = pl.ds(pl.multiple_of(tile * UROWS, UROWS), UROWS)
-        at = pl.ds(pl.multiple_of(places_ref[tile] * UROWS, UROWS), UROWS)
-        rows_ref[to, :] = pool_ref[at, :]
+        place = places_ref[tile]
+        to = rows_ref.at[pl.ds(pl.multiple_of(tile * UROWS, UROWS), UROWS), :]
+
+        @pl.when(place < near_blocks)
+        def _():
+            at = pl.ds(pl.multiple_of(place * UROWS, UROWS), UROWS)
+            pltpu.make_async_copy(near_ref.at[at, :], to, sems.at[2]).start()
+
+        @pl.when(place >= near_blocks)
+        def _():
+            at = pl.ds(pl.multiple_of((place - near_blocks) * UROWS, UROWS), UROWS)
+            pltpu.make_async_copy(other_ref.at[at, :], to, sems.at[2]).start()
+
         return carry
 
-    lax.fori_loop(0, places_ref.shape[0], fetch, 0, unroll=4)
+    lax.fori_loop(0, places_ref.shape[0], fetch, 0)
+    bring_weight.wait()
+    bring_items.wait()
+    pltpu.make_async_copy(rows_ref, rows_ref, sems.at[2]).wait()
+    keep_rows = pltpu.make_async_copy(rows_ref, rows_out_ref, sems.at[3])
+    keep_rows.start()
     blocks, _, depth = weight_ref.shape
     for block in range(blocks):
         guess = items_ref[item_rows(block), :]
@@ -146,31 +169,42 @@
             confidence = weight + jnp.where(weight > 0, 1.0, 0.0).astype(jnp.bfloat16)
             target = target + dot(confidence, rows_ref[block * depth + start : block * depth + start + CHUNK, :])
         part = tile_part(jnp.zeros_like(guess), guess.astype(jnp.bfloat16), block, rows_ref, weight_ref)
-        residue_ref[item_rows(block), :] = target - part
-
-
-def first_residue(places, gathered, weight, items):
+        started_ref[item_rows(block), :] = target - part
+    keep_started = pltpu.make_async_copy(started_ref, started_out_ref, sems.at[4])
+    keep_started.start()
+    keep_started.wait()
+    keep_rows.wait()
+
+
+def first_residue(places, near, other, weight, items):
     blocks, _, depth = weight.shape
-    features = items.shape[1]
-    pool_rows = sum(part.shape[0] for part in gathered)
+    rows = (blocks * depth, items.shape[1])
     return pl.pallas_call(
         first_kernel,
-        out_shape=(
-            jax.ShapeDtypeStruct((blocks * depth, features), jnp.bfloat16),
-            jax.ShapeDtypeStruct(items.shape, jnp.float32),
-        ),
-        in_specs=[SCALAR] + [VECTOR] * (len(gathered) + 2),
-        out_specs=(VECTOR, VECTOR),
-        scratch_shapes=[pltpu.VMEM((pool_rows, features), jnp.bfloat16)],
-        compiler_params=pltpu.CompilerParams(vmem_limit_bytes=20 * MIB),
+        out_shape=(pltpu.HBM(rows, jnp.bfloat16), pltpu.HBM(items.shape, jnp.float32)),
+        in_specs=[SCALAR, OUTER, pl.BlockSpec(memory_space=pl.ANY), OUTER, OUTER],
+        out_specs=(OUTER, OUTER),
+        scratch_shapes=[
+            pltpu.VMEM(rows, jnp.bfloat16),
+            pltpu.VMEM(weight.shape, jnp.bfloat16),
+            pltpu.VMEM(items.shape, jnp.float32),
+            pltpu.VMEM(items.shape, jnp.float32),
+            pltpu.SemaphoreType.DMA((5,)),
+        ],
+        compiler_params=pltpu.CompilerParams(vmem_limit_bytes=12 * MIB),
         name="first_residue",
-    )(places, *gathered, weight, items)
+    )(places, outer(near), other, outer(weight), outer(items))
 
 
 def steps_kernel(
-    rows_ref, weight_ref, items_ref, started_ref, gram_ref, guess_ref, high_ref, low_ref, residue_ref, direction_ref,
-    applied_ref,
+    rows_in_ref, weight_in_ref, items_ref, started_ref, gram_ref, guess_ref, rows_ref, weight_ref, high_ref, low_ref,
+    residue_ref, direction_ref, applied_ref, sems,
 ):
+    sources = (items_ref, started_ref, weight_in_ref, rows_in_ref)
+    places = (guess_ref, residue_ref, weight_ref, rows_ref)
+    copies = [pltpu.make_async_copy(*pair, sems.at[at]) for at, pair in enumerate(zip(sources, places))]
+    for copy in copies:
+        copy.start()
     blocks = weight_ref.shape[0]
     high_ref[...], low_ref[...] = high_low(gram_ref[...])
 
@@ -178,11 +212,13 @@
         high, low = high_low(vector)
         return dot(high, high_ref[...]) + (dot(high, low_ref[...]) + dot(low, high_ref[...]))
 
-    guess = items_ref[...]
-    guess_ref[...] = guess
-    residue = started_ref[...] - gram_part(guess)
+    copies[0].wait()
+    copies[1].wait()
+    residue = residue_ref[...] - gram_part(guess_ref[...])
     residue_ref[...] = residue
     direction_ref[...] = residue
+    copies[2].wait()
+    copies[3].wait()
 
     def step(iteration, current):
         vector = direction_ref[...]
@@ -211,12 +247,21 @@
     return pl.pallas_call(
         steps_kernel,
         out_shape=jax.ShapeDtypeStruct(items.shape, jnp.float32),
-        in_specs=[VECTOR] * 5,
+        in_specs=[OUTER] * 4 + [VECTOR],
         out_specs=VECTOR,
-        scratch_shapes=[square, square, state, state, state],
-        compiler_params=pltpu.CompilerParams(vmem_limit_bytes=16 * MIB),
+        scratch_shapes=[
+            pltpu.VMEM(rows.shape, jnp.bfloat16),
+            pltpu.VMEM(weight.shape, jnp.bfloat16),
+            square,
+            square,
+            state,
+            state,
+            state,
+            pltpu.SemaphoreType.DMA((4,)),
+        ],
+        compiler_params=pltpu.CompilerParams(vmem_limit_bytes=14 * MIB),
         name="solve_steps",
-    )(rows, weight, items, started, gram)
+    )(*map(outer, (rows, weight, items, started)), gram)
 
 
 def put_parts(ref, start, value):
@@ -244,24 +289,53 @@
     put_parts(up_ref, len(parts) * rows, total)
 
 
-def join_kernel(counts, *refs):
-    filled = 0
-    for count, part in zip(counts, refs[:-1]):
-        refs[-1][filled : filled + count, :] = part[:count, :]
-        filled += count
-
-
-def join(parts, counts):
-    out = jax.ShapeDtypeStruct((sum(counts), parts[0].shape[1]), parts[0].dtype)
-    return small_call(functools.partial(join_kernel, counts), out, "join", *parts)
-
-
-def spread_kernel(*refs):
-    parts, out_ref = refs[:-1], refs[-1]
-    copies, share, _ = out_ref.shape
+def collect_kernel(rows, places, share, *refs):
+    parts, (near_ref, total_ref, sems) = refs[: len(rows)], refs[-3:]
+    copies = []
+    for at, part in enumerate(parts):
+        to = near_ref.at[places[at] : places[at] + rows[at], :]
+        copies.append(pltpu.make_async_copy(part.at[: rows[at], :], to, sems.at[at]))
+        copies[-1].start()
     total = functools.reduce(jnp.add, [merge(part[-2 * share :, :]) for part in parts])
-    for copy in range(copies):
-        out_ref[copy] = total
+    total_ref[...] = total if len(refs) == len(rows) + 3 else refs[len(rows) + 1][...] + total
+    for copy in copies:
+        copy.wait()
+
+
+def collect(name, parts, rows, places, near_shape, share, *earlier):
+    count = len(parts)
+    return pl.pallas_call(
+        functools.partial(collect_kernel, rows, places, share),
+        out_shape=(near_shape, jax.ShapeDtypeStruct((share, near_shape.shape[1]), jnp.float32)),
+        in_specs=[VECTOR] * count + [OUTER, VECTOR][: len(earlier)],
+        out_specs=(OUTER, VECTOR),
+        scratch_shapes=[pltpu.SemaphoreType.DMA((count,))],
+        input_output_aliases={count: 0} if earlier else {},
+        compiler_params=pltpu.CompilerParams(vmem_limit_bytes=4 * MIB),
+        name=name,
+    )(*parts, *map(outer, earlier[:1]), *earlier[1:])
+
+
+def spread_kernel(total_ref, out_ref, copies_ref, sem):
+    total = total_ref[...]
+    for copy in range(copies_ref.shape[0]):
+        copies_ref[copy] = total
+    write = pltpu.make_async_copy(copies_ref, out_ref, sem)
+    write.start()
+    write.wait()
+
+
+def spread(total, replicas):
+    shape = (replicas,) + total.shape
+    return pl.pallas_call(
+        spread_kernel,
+        out_shape=pltpu.HBM(shape, jnp.float32),
+        in_specs=[VECTOR],
+        out_specs=OUTER,
+        scratch_shapes=[pltpu.VMEM(shape, jnp.float32), pltpu.SemaphoreType.DMA],
+        compiler_params=pltpu.CompilerParams(vmem_limit_bytes=4 * MIB),
+        name="spread",
+    )(total)
 
 
 def on_device(user_factors, item_factors, tile_users, tile_counts):
@@ -295,7 +369,6 @@
         far_below,
         far_above,
     )
-    ups, downs = [up], []
     weight = small_call(
         weight_kernel,
         jax.ShapeDtypeStruct((blocks, IBLK, tile_counts.shape[0] * UROWS // blocks), jnp.bfloat16),
@@ -303,22 +376,21 @@
         tile_counts,
     )
     places = pool_places(tile_users, chips, replicas, owned_rows // UROWS)
-    for hop in range(HOPS):
+    up_rows, down_rows = 5 * owned_rows, 4 * owned_rows
+    near_shape = pltpu.HBM((chips * owned_rows, features), jnp.bfloat16)
+    near, total = collect("collect_0", [up], [up_rows], [0], near_shape, share)
+    for hop in range(1, HOPS + 1):
         up, down = shift(up, distance=1), shift(down, distance=-1)
-        if hop == 0:
-            up, down, weight, places = bar((up, down, weight, places))
+        if hop == 1:
+            up, down, near, total, weight, places = bar((up, down, near, total, weight, places))
         else:
-            up, down = bar((up, down))
-        ups.append(up)
-        downs.append(down)
-
-    near = join(ups + downs, [5 * owned_rows] * (HOPS + 1) + [4 * owned_rows] * HOPS)
+            up, down, near, total = bar((up, down, near, total))
+        at = [hop * up_rows, (HOPS + 1) * up_rows + (hop - 1) * down_rows]
+        near, total = collect("collect_" + str(hop), [up, down], [up_rows, down_rows], at, near_shape, share, near, total)
+
     other = core_swap(near, chips)
-    spread = small_call(
-        spread_kernel, jax.ShapeDtypeStruct((replicas, share, features), jnp.float32), "spread", *ups, *downs
-    )
-    gram = lax.all_to_all(spread.reshape(features, features), "rep", 0, 0, tiled=True)
-    rows, started = first_residue(places, [near, other], weight, item_factors)
+    gram = lax.all_to_all(spread(total, replicas).reshape(features, features), "rep", 0, 0, tiled=True)
+    rows, started = first_residue(places, near, other, weight, item_factors)
     return solve_steps(rows, weight, item_factors, started, gram)
 
 

time: 146 us -> 146 us (level)
  local copies, waits for them, and re-layouts: 13.4 us -> 3.47 us
  Pallas kernels: 10.4 us -> 18.2 us
  starting transfers between devices: 64.5 us -> 69.8 us
  waiting for transfers between devices: 40.6 us -> 37.5 us
    unnamed x28 -> x8, local copies, waits for them, and re-layouts: 13.4 us -> 3.47 us
    pallas_call x1 -> x6, Pallas kernels: 3.52 us -> 9.55 us  [the longest x1 5.55 us: first_residue(): pl.pallas_call(first_kernel, out_shape=(pltpu.HBM(rows, jnp.bfloat16), pl...]
    ppermute x10, waiting for transfers between devices: 38 us -> 33.8 us  [chip_shift(): return lax.ppermute(value, 'grp', pairs)]
    ppermute x10, starting transfers between devices: 46.4 us -> 49.4 us  [chip_shift(): return lax.ppermute(value, 'grp', pairs)]
    ppermute x2, starting transfers between devices: 14.6 us -> 16.9 us  [core_swap(): return lax.ppermute(value, 'grp', pairs)]
    pallas_call x1, Pallas kernels: 6.06 us -> 7.96 us  [solve_steps(): pl.pallas_call(steps_kernel, out_shape=jax.ShapeDtypeStruct(items.shape,...]
  transfers between devices with their start and end apart: 13 -> 13, of which waited for: 9 -> 8; matrix products, arithmetic and copies ran while one was open for 1% -> 1% of each run, Pallas kernels for 3% -> 6%
where the time goes in v4:
time: 146 us
  starting transfers between devices  69.8 us (48%)
  waiting for transfers between devices  37.5 us (26%)
  Pallas kernels  18.2 us (12%)
  blocking collectives  14.9 us (10%)
  local copies, waits for them, and re-layouts  3.47 us (2%)
  other arithmetic  1.47 us (1%)
    ppermute x10, starting transfers between devices, chip_shift(): return lax.ppermute(value, 'grp', pairs)  49.4 us
    ppermute x10, waiting for transfers between devices, chip_shift(): return lax.ppermute(value, 'grp', pairs)  33.8 us
    ppermute x2, starting transfers between devices, core_swap(): return lax.ppermute(value, 'grp', pairs)  16.9 us
    all_to_all x1, blocking collectives, on_device(): pieces = lax.all_to_all(gram, 'rep', 0, 0, tiled=True)  14.9 us
    pallas_call x1, Pallas kernels, solve_steps(): pl.pallas_call(steps_kernel, out_shape=jax.ShapeDtypeStruct(items.shape,...  7.96 us
    pallas_call x1, Pallas kernels, first_residue(): pl.pallas_call(first_kernel, out_shape=(pltpu.HBM(rows, jnp.bfloat16), pl...  5.55 us
    all_to_all x1, starting transfers between devices, on_device(): lax.all_to_all(spread(total, replicas).reshape(features, features), 'rep'...  3.55 us
    unnamed x8, local copies, waits for them, and re-layouts  3.47 us
  transfers between devices with their start and end apart: 13, of which 8 were waited for; matrix products, arithmetic and copies ran while one was open for 1% of the time, Pallas kernels for 6%

profile of v4, /device:TPU:1, one launch (start us, length us, event | category | flops | bytes accessed | tf_op | source)
XLA Modules:
  0.0 145.7 jit_solution(5475121540347731692)
XLA Ops:
  0.0 0.0 copy-start.2
  0.0 0.9 copy-done.2
  0.9 0.3 local_gram.1
  1.2 14.9 %all_to_all.17 = f32[16,16,256]{2,1,0:T(8,128)S(1)} all-to-all(f32[16,16,256]{2,1,0:T(8,128)S(1)} %bitcast.3), channel_id=1, replica_groups=mesh['grp'=64,'rep'=16] {'rep'}, dimensions={0} | all-to-all | bytes 524288 | tf_op jit(solution)/shard_map/all_to_all | solution.py:356
  16.1 0.0 copy-start.3
  16.2 12.4 %collective-permute-start = (f32[16,256]{1,0:T(8,128)S(1)}, f32[16,256]{1,0:T(8,128)S(1)}, u32[]{:S(2)}, u32[]{:S(2)}) collective-permute-start(f32[16,256]{1,0:T(8,128)S(1)} %reduce_sum.18.mine_ref), channel_id=1, source_target_pairs={{0,16},{16,0},{32,48},{48,32},{64,80},{80,64},{96,112},{112,96},{1... | collective-permute-start | bytes 49160 | tf_op jit(solution)/shard_map/ppermute | solution.py:36
  28.6 0.8 collective-permute-done.other_ref
  29.4 13.9 %collective-permute-start.1 = (bf16[160,256]{1,0:T(8,128)(2,1)S(1)}, bf16[160,256]{1,0:T(8,128)(2,1)S(1)}, u32[]{:S(2)}, u32[]{:S(2)}) collective-permute-start(bf16[160,256]{1,0:T(8,128)(2,1)S(1)} %own.1.refs_0_), channel_id=1, source_target_pairs={{0,224},{16,816},{32,256},{48,848},{64,288},{80,880},{96,320},{112... | collective-permute-start | bytes 245768 | tf_op jit(solution)/shard_map/ppermute | solution.py:31
  43.3 1.9 %collective-permute-start.2 = (bf16[160,256]{1,0:T(8,128)(2,1)S(1)}, bf16[160,256]{1,0:T(8,128)(2,1)S(1)}, u32[]{:S(2)}, u32[]{:S(2)}) collective-permute-start(bf16[160,256]{1,0:T(8,128)(2,1)S(1)} %own.1.refs_0_), channel_id=1, source_target_pairs={{0,800},{16,240},{32,832},{48,272},{64,864},{80,304},{96,896},{112... | collective-permute-start | bytes 245768 | tf_op jit(solution)/shard_map/ppermute | solution.py:31
  45.2 10.5 %collective-permute-done.1.refs_1_ = bf16[160,256]{1,0:T(8,128)(2,1)S(1)} collective-permute-done((bf16[160,256]{1,0:T(8,128)(2,1)S(1)}, bf16[160,256]{1,0:T(8,128)(2,1)S(1)}, u32[]{:S(2)}, u32[]{:S(2)}) %collective-permute-start.1) | collective-permute-done | bytes 81952 | tf_op jit(solution)/shard_map/ppermute | solution.py:31
  55.7 1.5 %collective-permute-done.2.refs_2_ = bf16[160,256]{1,0:T(8,128)(2,1)S(1)} collective-permute-done((bf16[160,256]{1,0:T(8,128)(2,1)S(1)}, bf16[160,256]{1,0:T(8,128)(2,1)S(1)}, u32[]{:S(2)}, u32[]{:S(2)}) %collective-permute-start.2) | collective-permute-done | bytes 81952 | tf_op jit(solution)/shard_map/ppermute | solution.py:31
  57.2 10.6 %collective-permute-start.3 = (bf16[160,256]{1,0:T(8,128)(2,1)S(1)}, bf16[160,256]{1,0:T(8,128)(2,1)S(1)}, u32[]{:S(2)}, u32[]{:S(2)}) collective-permute-start(bf16[160,256]{1,0:T(8,128)(2,1)S(1)} %collective-permute-done.1.refs_1_), channel_id=1, source_target_pairs={{0,224},{16,816},{32,256},{48,848},{64,288},{80,880},{96,320},{112... | collective-permute-start | bytes 245768 | tf_op jit(solution)/shard_map/ppermute | solution.py:31
  67.8 1.9 %collective-permute-start.4 = (bf16[160,256]{1,0:T(8,128)(2,1)S(1)}, bf16[160,256]{1,0:T(8,128)(2,1)S(1)}, u32[]{:S(2)}, u32[]{:S(2)}) collective-permute-start(bf16[160,256]{1,0:T(8,128)(2,1)S(1)} %collective-permute-done.2.refs_2_), channel_id=1, source_target_pairs={{0,800},{16,240},{32,832},{48,272},{64,864},{80,304},{96,896},{112... | collective-permute-start | bytes 245768 | tf_op jit(solution)/shard_map/ppermute | solution.py:31
  69.7 0.3 collective-permute-done.3.refs_3_
  70.0 11.2 %collective-permute-done.4.refs_4_ = bf16[160,256]{1,0:T(8,128)(2,1)S(1)} collective-permute-done((bf16[160,256]{1,0:T(8,128)(2,1)S(1)}, bf16[160,256]{1,0:T(8,128)(2,1)S(1)}, u32[]{:S(2)}, u32[]{:S(2)}) %collective-permute-start.4) | collective-permute-done | bytes 81952 | tf_op jit(solution)/shard_map/ppermute | solution.py:31
  81.2 1.9 %collective-permute-start.5 = (bf16[672,256]{1,0:T(8,128)(2,1)S(1)}, bf16[672,256]{1,0:T(8,128)(2,1)S(1)}, u32[]{:S(2)}, u32[]{:S(2)}) collective-permute-start(bf16[672,256]{1,0:T(8,128)(2,1)S(1)} %get-tuple-element.43.refs_0_), channel_id=1, source_target_pairs={{0,32},{16,1008},{32,64},{48,16},{64,96},{80,48},{96,128},{112,80}... | collective-permute-start | bytes 1032200 | tf_op jit(solution)/shard_map/ppermute | solution.py:31
  83.2 0.7 and_select_fusion.1
  83.8 5.7 %collective-permute-start.6 = (bf16[544,256]{1,0:T(8,128)(2,1)S(1)}, bf16[544,256]{1,0:T(8,128)(2,1)S(1)}, u32[]{:S(2)}, u32[]{:S(2)}) collective-permute-start(bf16[544,256]{1,0:T(8,128)(2,1)S(1)} %get-tuple-element.44), channel_id=1, source_target_pairs={{0,992},{16,48},{32,0},{48,80},{64,32},{80,112},{96,64},{112,144},... | collective-permute-start | bytes 835592 | tf_op jit(solution)/shard_map/ppermute | solution.py:31
  89.5 0.7 select_reduce_fusion
  90.3 0.0 copy-start.1
  90.3 1.6 %copy-done.1 = s32[64,64,128]{2,1,0:T(8,128)S(1)} copy-done((s32[64,64,128]{2,1,0:T(8,128)S(1)}, s32[64,64,128]{2,1,0:T(8,128)}, u32[]{:S(2)}) %copy-start.1) | copy-done | bytes 2097176
  91.9 0.4 item_weights.1.weight_in_ref
  92.3 0.0 copy-start
  92.3 1.0 copy-done
  93.2 0.0 copy-done.3
  93.3 0.7 collect_0.1
  94.0 0.0 collective-permute-done.6.refs_1_
  94.0 0.0 collective-permute-done.5.refs_0_
  94.0 3.1 %collective-permute-start.7 = (bf16[672,256]{1,0:T(8,128)(2,1)S(1)}, bf16[672,256]{1,0:T(8,128)(2,1)S(1)}, u32[]{:S(2)}, u32[]{:S(2)}) collective-permute-start(bf16[672,256]{1,0:T(8,128)(2,1)S(1)} %collective-permute-done.5.refs_0_), channel_id=1, source_target_pairs={{0,32},{16,1008},{32,64},{48,16},{64,96},{80,48},{96,128},{112,80}... | collective-permute-start | bytes 1032200 | tf_op jit(solution)/shard_map/ppermute | solution.py:31
  97.1 3.8 %collective-permute-start.8 = (bf16[544,256]{1,0:T(8,128)(2,1)S(1)}, bf16[544,256]{1,0:T(8,128)(2,1)S(1)}, u32[]{:S(2)}, u32[]{:S(2)}) collective-permute-start(bf16[544,256]{1,0:T(8,128)(2,1)S(1)} %collective-permute-done.6.refs_1_), channel_id=1, source_target_pairs={{0,992},{16,48},{32,0},{48,80},{64,32},{80,112},{96,64},{112,144},... | collective-permute-start | bytes 835592 | tf_op jit(solution)/shard_map/ppermute | solution.py:31
  100.9 0.8 collect_1.1
  101.8 5.0 %collective-permute-done.8.refs_1_ = bf16[544,256]{1,0:T(8,128)(2,1)S(1)} collective-permute-done((bf16[544,256]{1,0:T(8,128)(2,1)S(1)}, bf16[544,256]{1,0:T(8,128)(2,1)S(1)}, u32[]{:S(2)}, u32[]{:S(2)}) %collective-permute-start.8) | collective-permute-done | bytes 278560 | tf_op jit(solution)/shard_map/ppermute | solution.py:31
  106.8 0.0 collective-permute-done.7.refs_0_
  106.8 1.9 %collective-permute-start.9 = (bf16[672,256]{1,0:T(8,128)(2,1)S(1)}, bf16[672,256]{1,0:T(8,128)(2,1)S(1)}, u32[]{:S(2)}, u32[]{:S(2)}) collective-permute-start(bf16[672,256]{1,0:T(8,128)(2,1)S(1)} %collective-permute-done.7.refs_0_), channel_id=1, source_target_pairs={{0,32},{16,1008},{32,64},{48,16},{64,96},{80,48},{96,128},{112,80}... | collective-permute-start | bytes 1032200 | tf_op jit(solution)/shard_map/ppermute | solution.py:31
  108.7 4.7 %collective-permute-start.10 = (bf16[544,256]{1,0:T(8,128)(2,1)S(1)}, bf16[544,256]{1,0:T(8,128)(2,1)S(1)}, u32[]{:S(2)}, u32[]{:S(2)}) collective-permute-start(bf16[544,256]{1,0:T(8,128)(2,1)S(1)} %collective-permute-done.8.refs_1_), channel_id=1, source_target_pairs={{0,992},{16,48},{32,0},{48,80},{64,32},{80,112},{96,64},{112,144},... | collective-permute-start | bytes 835592 | tf_op jit(solution)/shard_map/ppermute | solution.py:31
  113.4 0.9 collect_2.1
  114.3 5.3 %collective-permute-done.10.refs_1_ = bf16[544,256]{1,0:T(8,128)(2,1)S(1)} collective-permute-done((bf16[544,256]{1,0:T(8,128)(2,1)S(1)}, bf16[544,256]{1,0:T(8,128)(2,1)S(1)}, u32[]{:S(2)}, u32[]{:S(2)}) %collective-permute-start.10) | collective-permute-done | bytes 278560 | tf_op jit(solution)/shard_map/ppermute | solution.py:31
  119.6 0.0 collective-permute-done.9.refs_0_
  119.6 0.8 collect_3.1
  120.4 4.4 %collective-permute-start.11 = (bf16[4096,256]{1,0:T(8,128)(2,1)}, bf16[4096,256]{1,0:T(8,128)(2,1)S(1)}, u32[]{:S(2)}, u32[]{:S(2)}) collective-permute-start(bf16[4096,256]{1,0:T(8,128)(2,1)} %get-tuple-element.64.near_ref), channel_id=1, source_target_pairs={{0,16},{16,0},{32,48},{48,32},{64,80},{80,64},{96,112},{112,96},{1... | collective-permute-start | bytes 6291464 | tf_op jit(solution)/shard_map/ppermute | solution.py:36
  124.9 0.7 spread.1
  125.6 3.5 %all-to-all-start.1 = ((f32[16,16,256]{2,1,0:T(8,128)}), f32[16,16,256]{2,1,0:T(8,128)S(1)}, u32[]{:S(2)}, u32[]{:S(2)}) async-start(f32[16,16,256]{2,1,0:T(8,128)} %spread.1), calls=%async_computation.1 | async-start | bytes 524288 | tf_op jit(solution)/shard_map/all_to_all | solution.py:392
  129.2 0.0 collective-permute-done.11.other_ref
  129.2 5.6 %first_residue.1 = (bf16[4096,256]{1,0:T(8,128)(2,1)}, f32[512,256]{1,0:T(8,128)}) custom-call(s32[64]{0:T(128)S(1)} %fusion.places_ref, bf16[4096,256]{1,0:T(8,128)(2,1)} %get-tuple-element.64.near_ref, bf16[4096,256]{1,0:T(8,128)(2,1)S(1)} %collective-permute-done.11.other_ref, bf16[4,128,1024]{2,1,0:T(8,128)(2,1)} %copy-done, f32[512,256]{1,0:T(8,128)} %items_ref.1), custom_call_target="tpu_custom_call" | custom-call | tf_op jit(solution)/shard_map/first_residue/pallas_call | solution.py:182
  134.8 2.9 %all-to-all-done.1 = f32[16,16,256]{2,1,0:T(8,128)S(1)} async-done(((f32[16,16,256]{2,1,0:T(8,128)}), f32[16,16,256]{2,1,0:T(8,128)S(1)}, u32[]{:S(2)}, u32[]{:S(2)}) %all-to-all-start.1) | async-done | bytes 262176 | tf_op jit(solution)/shard_map/all_to_all | solution.py:392
  137.7 8.0 %solve_steps.1 = f32[512,256]{1,0:T(8,128)} custom-call(bf16[4096,256]{1,0:T(8,128)(2,1)} %get-tuple-element.66.rows_in_ref, bf16[4,128,1024]{2,1,0:T(8,128)(2,1)} %copy-done, f32[512,256]{1,0:T(8,128)} %items_ref.1, f32[512,256]{1,0:T(8,128)} %get-tuple-element.67.started_ref, f32[256,256]{1,0:T(8,128)S(1)} %bitcast.2), custom_call_target="tpu_custom_call" | custom-call | tf_op jit(solution)/shard_map/solve_steps/pallas_call | solution.py:247
  (4 shorter events, 0.1 us)
Async XLA Ops:
  0.0 0.9 copy-start.2
  16.1 77.1 %copy-start.3 = (s32[64]{0:T(128)S(1)}, s32[64]{0:T(128)}, u32[]{:S(2)}) copy-start(s32[64]{0:T(128)} %param.8) | copy-start | bytes 772
  16.2 13.2 %collective-permute-start = (f32[16,256]{1,0:T(8,128)S(1)}, f32[16,256]{1,0:T(8,128)S(1)}, u32[]{:S(2)}, u32[]{:S(2)}) collective-permute-start(f32[16,256]{1,0:T(8,128)S(1)} %reduce_sum.18.mine_ref), channel_id=1, source_target_pairs={{0,16},{16,0},{32,48},{48,32},{64,80},{80,64},{96,112},{112,96},{1... | collective-permute-start | bytes 49160 | tf_op jit(solution)/shard_map/ppermute | solution.py:36
  29.4 26.3 %collective-permute-start.1 = (bf16[160,256]{1,0:T(8,128)(2,1)S(1)}, bf16[160,256]{1,0:T(8,128)(2,1)S(1)}, u32[]{:S(2)}, u32[]{:S(2)}) collective-permute-start(bf16[160,256]{1,0:T(8,128)(2,1)S(1)} %own.1.refs_0_), channel_id=1, source_target_pairs={{0,224},{16,816},{32,256},{48,848},{64,288},{80,880},{96,320},{112... | collective-permute-start | bytes 245768 | tf_op jit(solution)/shard_map/ppermute | solution.py:31
  43.3 13.9 %collective-permute-start.2 = (bf16[160,256]{1,0:T(8,128)(2,1)S(1)}, bf16[160,256]{1,0:T(8,128)(2,1)S(1)}, u32[]{:S(2)}, u32[]{:S(2)}) collective-permute-start(bf16[160,256]{1,0:T(8,128)(2,1)S(1)} %own.1.refs_0_), channel_id=1, source_target_pairs={{0,800},{16,240},{32,832},{48,272},{64,864},{80,304},{96,896},{112... | collective-permute-start | bytes 245768 | tf_op jit(solution)/shard_map/ppermute | solution.py:31
  57.2 12.8 %collective-permute-start.3 = (bf16[160,256]{1,0:T(8,128)(2,1)S(1)}, bf16[160,256]{1,0:T(8,128)(2,1)S(1)}, u32[]{:S(2)}, u32[]{:S(2)}) collective-permute-start(bf16[160,256]{1,0:T(8,128)(2,1)S(1)} %collective-permute-done.1.refs_1_), channel_id=1, source_target_pairs={{0,224},{16,816},{32,256},{48,848},{64,288},{80,880},{96,320},{112... | collective-permute-start | bytes 245768 | tf_op jit(solution)/shard_map/ppermute | solution.py:31
  67.8 13.4 %collective-permute-start.4 = (bf16[160,256]{1,0:T(8,128)(2,1)S(1)}, bf16[160,256]{1,0:T(8,128)(2,1)S(1)}, u32[]{:S(2)}, u32[]{:S(2)}) collective-permute-start(bf16[160,256]{1,0:T(8,128)(2,1)S(1)} %collective-permute-done.2.refs_2_), channel_id=1, source_target_pairs={{0,800},{16,240},{32,832},{48,272},{64,864},{80,304},{96,896},{112... | collective-permute-start | bytes 245768 | tf_op jit(solution)/shard_map/ppermute | solution.py:31
  81.2 12.8 %collective-permute-start.5 = (bf16[672,256]{1,0:T(8,128)(2,1)S(1)}, bf16[672,256]{1,0:T(8,128)(2,1)S(1)}, u32[]{:S(2)}, u32[]{:S(2)}) collective-permute-start(bf16[672,256]{1,0:T(8,128)(2,1)S(1)} %get-tuple-element.43.refs_0_), channel_id=1, source_target_pairs={{0,32},{16,1008},{32,64},{48,16},{64,96},{80,48},{96,128},{112,80}... | collective-permute-start | bytes 1032200 | tf_op jit(solution)/shard_map/ppermute | solution.py:31
  83.8 10.2 %collective-permute-start.6 = (bf16[544,256]{1,0:T(8,128)(2,1)S(1)}, bf16[544,256]{1,0:T(8,128)(2,1)S(1)}, u32[]{:S(2)}, u32[]{:S(2)}) collective-permute-start(bf16[544,256]{1,0:T(8,128)(2,1)S(1)} %get-tuple-element.44), channel_id=1, source_target_pairs={{0,992},{16,48},{32,0},{48,80},{64,32},{80,112},{96,64},{112,144},... | collective-permute-start | bytes 835592 | tf_op jit(solution)/shard_map/ppermute | solution.py:31
  90.3 1.6 %copy-start.1 = (s32[64,64,128]{2,1,0:T(8,128)S(1)}, s32[64,64,128]{2,1,0:T(8,128)}, u32[]{:S(2)}) copy-start(s32[64,64,128]{2,1,0:T(8,128)} %counts_ref.1) | copy-start | bytes 6291460
  92.3 1.0 copy-start
  94.0 12.8 %collective-permute-start.7 = (bf16[672,256]{1,0:T(8,128)(2,1)S(1)}, bf16[672,256]{1,0:T(8,128)(2,1)S(1)}, u32[]{:S(2)}, u32[]{:S(2)}) collective-permute-start(bf16[672,256]{1,0:T(8,128)(2,1)S(1)} %collective-permute-done.5.refs_0_), channel_id=1, source_target_pairs={{0,32},{16,1008},{32,64},{48,16},{64,96},{80,48},{96,128},{112,80}... | collective-permute-start | bytes 1032200 | tf_op jit(solution)/shard_map/ppermute | solution.py:31
  97.1 9.7 %collective-permute-start.8 = (bf16[544,256]{1,0:T(8,128)(2,1)S(1)}, bf16[544,256]{1,0:T(8,128)(2,1)S(1)}, u32[]{:S(2)}, u32[]{:S(2)}) collective-permute-start(bf16[544,256]{1,0:T(8,128)(2,1)S(1)} %collective-permute-done.6.refs_1_), channel_id=1, source_target_pairs={{0,992},{16,48},{32,0},{48,80},{64,32},{80,112},{96,64},{112,144},... | collective-permute-start | bytes 835592 | tf_op jit(solution)/shard_map/ppermute | solution.py:31
  106.8 12.8 %collective-permute-start.9 = (bf16[672,256]{1,0:T(8,128)(2,1)S(1)}, bf16[672,256]{1,0:T(8,128)(2,1)S(1)}, u32[]{:S(2)}, u32[]{:S(2)}) collective-permute-start(bf16[672,256]{1,0:T(8,128)(2,1)S(1)} %collective-permute-done.7.refs_0_), channel_id=1, source_target_pairs={{0,32},{16,1008},{32,64},{48,16},{64,96},{80,48},{96,128},{112,80}... | collective-permute-start | bytes 1032200 | tf_op jit(solution)/shard_map/ppermute | solution.py:31
  108.7 10.9 %collective-permute-start.10 = (bf16[544,256]{1,0:T(8,128)(2,1)S(1)}, bf16[544,256]{1,0:T(8,128)(2,1)S(1)}, u32[]{:S(2)}, u32[]{:S(2)}) collective-permute-start(bf16[544,256]{1,0:T(8,128)(2,1)S(1)} %collective-permute-done.8.refs_1_), channel_id=1, source_target_pairs={{0,992},{16,48},{32,0},{48,80},{64,32},{80,112},{96,64},{112,144},... | collective-permute-start | bytes 835592 | tf_op jit(solution)/shard_map/ppermute | solution.py:31
  120.4 8.8 %collective-permute-start.11 = (bf16[4096,256]{1,0:T(8,128)(2,1)}, bf16[4096,256]{1,0:T(8,128)(2,1)S(1)}, u32[]{:S(2)}, u32[]{:S(2)}) collective-permute-start(bf16[4096,256]{1,0:T(8,128)(2,1)} %get-tuple-element.64.near_ref), channel_id=1, source_target_pairs={{0,16},{16,0},{32,48},{48,32},{64,80},{80,64},{96,112},{112,96},{1... | collective-permute-start | bytes 6291464 | tf_op jit(solution)/shard_map/ppermute | solution.py:36
  125.6 12.1 %all-to-all-start.1 = ((f32[16,16,256]{2,1,0:T(8,128)}), f32[16,16,256]{2,1,0:T(8,128)S(1)}, u32[]{:S(2)}, u32[]{:S(2)}) async-start(f32[16,16,256]{2,1,0:T(8,128)} %spread.1), calls=%async_computation.1 | async-start | bytes 524288 | tf_op jit(solution)/shard_map/all_to_all | solution.py:392

commit v5 on v4

--- a/solution.py
+++ b/solution.py
@@ -89,6 +89,10 @@
     return pltpu.with_memory_space_constraint(value, pltpu.HBM)
 
 
+def inner(value):
+    return pltpu.with_memory_space_constraint(value, pltpu.VMEM)
+
+
 def small_call(kernel, outs, name, *args):
     return pl.pallas_call(
         kernel,
@@ -129,39 +133,39 @@
 
 
 def first_kernel(
-    places_ref, near_ref, other_ref, weight_in_ref, items_in_ref, rows_out_ref, started_out_ref, rows_ref, weight_ref,
-    items_ref, started_ref, sems,
+    places_ref, near_ref, other_ref, weight_ref, items_in_ref, open_rows_ref, rows_ref, started_out_ref, items_ref,
+    started_ref, items_sem, sems, started_sems,
 ):
+    del open_rows_ref
     near_blocks = near_ref.shape[0] // UROWS
-    bring_weight = pltpu.make_async_copy(weight_in_ref, weight_ref, sems.at[0])
-    bring_items = pltpu.make_async_copy(items_in_ref, items_ref, sems.at[1])
-    bring_weight.start()
+    blocks, _, depth = weight_ref.shape
+    per_block = depth // UROWS
+    bring_items = pltpu.make_async_copy(items_in_ref, items_ref, items_sem)
     bring_items.start()
 
-    def fetch(tile, carry):
+    def fetch(tile, block):
         place = places_ref[tile]
         to = rows_ref.at[pl.ds(pl.multiple_of(tile * UROWS, UROWS), UROWS), :]
 
         @pl.when(place < near_blocks)
         def _():
             at = pl.ds(pl.multiple_of(place * UROWS, UROWS), UROWS)
-            pltpu.make_async_copy(near_ref.at[at, :], to, sems.at[2]).start()
+            pltpu.make_async_copy(near_ref.at[at, :], to, sems.at[block]).start()
 
         @pl.when(place >= near_blocks)
         def _():
             at = pl.ds(pl.multiple_of((place - near_blocks) * UROWS, UROWS), UROWS)
-            pltpu.make_async_copy(other_ref.at[at, :], to, sems.at[2]).start()
-
-        return carry
-
-    lax.fori_loop(0, places_ref.shape[0], fetch, 0)
-    bring_weight.wait()
+            pltpu.make_async_copy(other_ref.at[at, :], to, sems.at[block]).start()
+
+        return block
+
+    for block in range(blocks):
+        lax.fori_loop(block * per_block, (block + 1) * per_block, fetch, block)
     bring_items.wait()
-    pltpu.make_async_copy(rows_ref, rows_ref, sems.at[2]).wait()
-    keep_rows = pltpu.make_async_copy(rows_ref, rows_out_ref, sems.at[3])
-    keep_rows.start()
-    blocks, _, depth = weight_ref.shape
+    kept = []
     for block in range(blocks):
+        mine = rows_ref.at[block * depth : (block + 1) * depth, :]
+        pltpu.make_async_copy(mine, mine, sems.at[block]).wait()
         guess = items_ref[item_rows(block), :]
         target = -LAMBDA * guess
         for start in range(0, depth, CHUNK):
@@ -170,41 +174,43 @@
             target = target + dot(confidence, rows_ref[block * depth + start : block * depth + start + CHUNK, :])
         part = tile_part(jnp.zeros_like(guess), guess.astype(jnp.bfloat16), block, rows_ref, weight_ref)
         started_ref[item_rows(block), :] = target - part
-    keep_started = pltpu.make_async_copy(started_ref, started_out_ref, sems.at[4])
-    keep_started.start()
-    keep_started.wait()
-    keep_rows.wait()
-
-
-def first_residue(places, near, other, weight, items):
-    blocks, _, depth = weight.shape
-    rows = (blocks * depth, items.shape[1])
+        span = item_rows(block)
+        kept.append(
+            pltpu.make_async_copy(started_ref.at[span, :], started_out_ref.at[span, :], started_sems.at[block])
+        )
+        kept[-1].start()
+    for copy in kept:
+        copy.wait()
+
+
+def first_residue(places, near, other, weight, items, rows):
+    blocks = weight.shape[0]
     return pl.pallas_call(
         first_kernel,
-        out_shape=(pltpu.HBM(rows, jnp.bfloat16), pltpu.HBM(items.shape, jnp.float32)),
-        in_specs=[SCALAR, OUTER, pl.BlockSpec(memory_space=pl.ANY), OUTER, OUTER],
-        out_specs=(OUTER, OUTER),
+        out_shape=(pltpu.VMEM(rows.shape, rows.dtype), pltpu.HBM(items.shape, jnp.float32)),
+        in_specs=[SCALAR, OUTER, pl.BlockSpec(memory_space=pl.ANY), VECTOR, OUTER, VECTOR],
+        out_specs=(VECTOR, OUTER),
         scratch_shapes=[
-            pltpu.VMEM(rows, jnp.bfloat16),
-            pltpu.VMEM(weight.shape, jnp.bfloat16),
             pltpu.VMEM(items.shape, jnp.float32),
             pltpu.VMEM(items.shape, jnp.float32),
-            pltpu.SemaphoreType.DMA((5,)),
+            pltpu.SemaphoreType.DMA,
+            pltpu.SemaphoreType.DMA((blocks,)),
+            pltpu.SemaphoreType.DMA((blocks,)),
         ],
-        compiler_params=pltpu.CompilerParams(vmem_limit_bytes=12 * MIB),
+        compiler_params=pltpu.CompilerParams(vmem_limit_bytes=8 * MIB),
+        input_output_aliases={5: 0},
         name="first_residue",
-    )(places, outer(near), other, outer(weight), outer(items))
+    )(places, outer(near), other, inner(weight), outer(items), inner(rows))
 
 
 def steps_kernel(
-    rows_in_ref, weight_in_ref, items_ref, started_ref, gram_ref, guess_ref, rows_ref, weight_ref, high_ref, low_ref,
-    residue_ref, direction_ref, applied_ref, sems,
+    rows_ref, weight_ref, items_ref, started_ref, gram_ref, guess_ref, high_ref, low_ref, residue_ref, direction_ref,
+    applied_ref, sems,
 ):
-    sources = (items_ref, started_ref, weight_in_ref, rows_in_ref)
-    places = (guess_ref, residue_ref, weight_ref, rows_ref)
-    copies = [pltpu.make_async_copy(*pair, sems.at[at]) for at, pair in enumerate(zip(sources, places))]
-    for copy in copies:
-        copy.start()
+    bring_items = pltpu.make_async_copy(items_ref, guess_ref, sems.at[0])
+    bring_items.start()
+    bring_started = pltpu.make_async_copy(started_ref, residue_ref, sems.at[1])
+    bring_started.start()
     blocks = weight_ref.shape[0]
     high_ref[...], low_ref[...] = high_low(gram_ref[...])
 
@@ -212,13 +218,12 @@
         high, low = high_low(vector)
         return dot(high, high_ref[...]) + (dot(high, low_ref[...]) + dot(low, high_ref[...]))
 
-    copies[0].wait()
-    copies[1].wait()
-    residue = residue_ref[...] - gram_part(guess_ref[...])
+    bring_items.wait()
+    first = gram_part(guess_ref[...])
+    bring_started.wait()
+    residue = residue_ref[...] - first
     residue_ref[...] = residue
     direction_ref[...] = residue
-    copies[2].wait()
-    copies[3].wait()
 
     def step(iteration, current):
         vector = direction_ref[...]
@@ -247,21 +252,12 @@
     return pl.pallas_call(
         steps_kernel,
         out_shape=jax.ShapeDtypeStruct(items.shape, jnp.float32),
-        in_specs=[OUTER] * 4 + [VECTOR],
+        in_specs=[VECTOR, VECTOR, OUTER, OUTER, VECTOR],
         out_specs=VECTOR,
-        scratch_shapes=[
-            pltpu.VMEM(rows.shape, jnp.bfloat16),
-            pltpu.VMEM(weight.shape, jnp.bfloat16),
-            square,
-            square,
-            state,
-            state,
-            state,
-            pltpu.SemaphoreType.DMA((4,)),
-        ],
-        compiler_params=pltpu.CompilerParams(vmem_limit_bytes=14 * MIB),
+        scratch_shapes=[square, square, state, state, state, pltpu.SemaphoreType.DMA((2,))],
+        compiler_params=pltpu.CompilerParams(vmem_limit_bytes=10 * MIB),
         name="solve_steps",
-    )(*map(outer, (rows, weight, items, started)), gram)
+    )(inner(rows), inner(weight), outer(items), outer(started), gram)
 
 
 def put_parts(ref, start, value):
@@ -316,7 +312,8 @@
     )(*parts, *map(outer, earlier[:1]), *earlier[1:])
 
 
-def spread_kernel(total_ref, out_ref, copies_ref, sem):
+def spread_kernel(total_ref, out_ref, rows_ref, copies_ref, sem):
+    del rows_ref
     total = total_ref[...]
     for copy in range(copies_ref.shape[0]):
         copies_ref[copy] = total
@@ -325,13 +322,13 @@
     write.wait()
 
 
-def spread(total, replicas):
+def spread(total, replicas, rows_shape):
     shape = (replicas,) + total.shape
     return pl.pallas_call(
         spread_kernel,
-        out_shape=pltpu.HBM(shape, jnp.float32),
+        out_shape=(pltpu.HBM(shape, jnp.float32), pltpu.VMEM(rows_shape, jnp.bfloat16)),
         in_specs=[VECTOR],
-        out_specs=OUTER,
+        out_specs=(OUTER, VECTOR),
         scratch_shapes=[pltpu.VMEM(shape, jnp.float32), pltpu.SemaphoreType.DMA],
         compiler_params=pltpu.CompilerParams(vmem_limit_bytes=4 * MIB),
         name="spread",
@@ -357,8 +354,8 @@
     gram = jnp.sum(pieces.reshape(replicas, share, features), axis=0)
     own = small_call(own_kernel, half_rows(owned_rows + parts), "own", own, gram, core_swap(gram, chips))
 
-    below, above = bar((shift(own, distance=STRIDE), shift(own, distance=-STRIDE)))
-    far_below, far_above = bar((shift(below, distance=STRIDE), shift(above, distance=-STRIDE)))
+    below, above = shift(own, distance=STRIDE), shift(own, distance=-STRIDE)
+    far_below, far_above = shift(below, distance=STRIDE), shift(above, distance=-STRIDE)
     up, down = small_call(
         functools.partial(pack_kernel, owned_rows),
         (half_rows(5 * owned_rows + parts), half_rows(4 * owned_rows + parts)),
@@ -371,7 +368,7 @@
     )
     weight = small_call(
         weight_kernel,
-        jax.ShapeDtypeStruct((blocks, IBLK, tile_counts.shape[0] * UROWS // blocks), jnp.bfloat16),
+        pltpu.VMEM((blocks, IBLK, tile_counts.shape[0] * UROWS // blocks), jnp.bfloat16),
         "item_weights",
         tile_counts,
     )
@@ -382,15 +379,17 @@
     for hop in range(1, HOPS + 1):
         up, down = shift(up, distance=1), shift(down, distance=-1)
         if hop == 1:
-            up, down, near, total, weight, places = bar((up, down, near, total, weight, places))
+            up, near, total, weight, places = bar((up, near, total, weight, places))
         else:
-            up, down, near, total = bar((up, down, near, total))
+            up, near, total = bar((up, near, total))
         at = [hop * up_rows, (HOPS + 1) * up_rows + (hop - 1) * down_rows]
         near, total = collect("collect_" + str(hop), [up, down], [up_rows, down_rows], at, near_shape, share, near, total)
 
     other = core_swap(near, chips)
-    gram = lax.all_to_all(spread(total, replicas).reshape(features, features), "rep", 0, 0, tiled=True)
-    rows, started = first_residue(places, near, other, weight, item_factors)
+    rows_shape = (tile_counts.shape[0] * UROWS, features)
+    copies, rows = spread(total, replicas, rows_shape)
+    gram = lax.all_to_all(copies.reshape(features, features), "rep", 0, 0, tiled=True)
+    rows, started = first_residue(places, near, other, weight, item_factors, rows)
     return solve_steps(rows, weight, item_factors, started, gram)
 
 

time: 146 us -> 141 us (0.966)
  waiting for transfers between devices: 37.5 us -> 24.9 us
  starting transfers between devices: 69.8 us -> 80.2 us
    ppermute x10, waiting for transfers between devices: 33.8 us -> 20.4 us  [chip_shift(): return lax.ppermute(value, 'grp', pairs)]
    ppermute x2, starting transfers between devices: 16.9 us -> 24.4 us  [core_swap(): return lax.ppermute(value, 'grp', pairs)]
    ppermute x10, starting transfers between devices: 49.4 us -> 52.2 us  [chip_shift(): return lax.ppermute(value, 'grp', pairs)]
  transfers between devices with their start and end apart: 13 -> 13, of which waited for: 8 -> 10; matrix products, arithmetic and copies ran while one was open for 1% -> 1% of each run, Pallas kernels for 6% -> 6%
where the time goes in v5:
time: 141 us; the launch traced here: 140 us
  starting transfers between devices  80.2 us (57%)
  waiting for transfers between devices  24.9 us (18%)
  Pallas kernels  16.9 us (12%)
  blocking collectives  14.9 us (11%)
  local copies, waits for them, and re-layouts  2.5 us (2%)
    ppermute x10, starting transfers between devices, chip_shift(): return lax.ppermute(value, 'grp', pairs)  52.2 us
    ppermute x2, starting transfers between devices, core_swap(): return lax.ppermute(value, 'grp', pairs)  24.4 us
    ppermute x10, waiting for transfers between devices, chip_shift(): return lax.ppermute(value, 'grp', pairs)  20.4 us
    all_to_all x1, blocking collectives, on_device(): pieces = lax.all_to_all(gram, 'rep', 0, 0, tiled=True)  14.9 us
    pallas_call x1, Pallas kernels, solve_steps(): pl.pallas_call(steps_kernel, out_shape=jax.ShapeDtypeStruct(items.shape,...  7.36 us
    pallas_call x1, Pallas kernels, first_residue(): pl.pallas_call(first_kernel, out_shape=(pltpu.VMEM(rows.shape, rows.dtype...  4.84 us
    all_to_all x1, waiting for transfers between devices, on_device(): lax.all_to_all(copies.reshape(features, features), 'rep', 0, 0, tiled=True)  3.65 us
    all_to_all x1, starting transfers between devices, on_device(): lax.all_to_all(copies.reshape(features, features), 'rep', 0, 0, tiled=True)  3.55 us
  transfers between devices with their start and end apart: 13, of which 10 were waited for; matrix products, arithmetic and copies ran while one was open for 1% of the time, Pallas kernels for 6%

profile of v5, /device:TPU:1, one launch (start us, length us, event | category | flops | bytes accessed | tf_op | source)
XLA Modules:
  0.0 140.4 jit_solution(10420646157435627250)
XLA Ops:
  0.0 0.0 copy-start.1
  0.0 0.9 copy-done.1
  0.9 0.3 local_gram.1
  1.2 14.9 %all_to_all.17 = f32[16,16,256]{2,1,0:T(8,128)S(1)} all-to-all(f32[16,16,256]{2,1,0:T(8,128)S(1)} %bitcast.3), channel_id=1, replica_groups=mesh['grp'=64,'rep'=16] {'rep'}, dimensions={0} | all-to-all | bytes 524288 | tf_op jit(solution)/shard_map/all_to_all | solution.py:353
  16.1 0.0 copy-start.3
  16.1 0.0 copy-start.2
  16.2 12.4 %collective-permute-start = (f32[16,256]{1,0:T(8,128)S(1)}, f32[16,256]{1,0:T(8,128)S(1)}, u32[]{:S(2)}, u32[]{:S(2)}) collective-permute-start(f32[16,256]{1,0:T(8,128)S(1)} %reduce_sum.18.mine_ref), channel_id=1, source_target_pairs={{0,16},{16,0},{32,48},{48,32},{64,80},{80,64},{96,112},{112,96},{1... | collective-permute-start | bytes 49160 | tf_op jit(solution)/shard_map/ppermute | solution.py:36
  28.6 0.8 collective-permute-done.other_ref
  29.4 4.5 %collective-permute-start.2 = (bf16[160,256]{1,0:T(8,128)(2,1)S(1)}, bf16[160,256]{1,0:T(8,128)(2,1)S(1)}, u32[]{:S(2)}, u32[]{:S(2)}) collective-permute-start(bf16[160,256]{1,0:T(8,128)(2,1)S(1)} %own.1.refs_0_), channel_id=1, source_target_pairs={{0,800},{16,240},{32,832},{48,272},{64,864},{80,304},{96,896},{112... | collective-permute-start | bytes 245768 | tf_op jit(solution)/shard_map/ppermute | solution.py:31
  33.9 11.3 %collective-permute-start.1 = (bf16[160,256]{1,0:T(8,128)(2,1)S(1)}, bf16[160,256]{1,0:T(8,128)(2,1)S(1)}, u32[]{:S(2)}, u32[]{:S(2)}) collective-permute-start(bf16[160,256]{1,0:T(8,128)(2,1)S(1)} %own.1.refs_0_), channel_id=1, source_target_pairs={{0,224},{16,816},{32,256},{48,848},{64,288},{80,880},{96,320},{112... | collective-permute-start | bytes 245768 | tf_op jit(solution)/shard_map/ppermute | solution.py:31
  45.2 0.1 collective-permute-done.2.refs_2_
  45.4 7.2 %collective-permute-start.4 = (bf16[160,256]{1,0:T(8,128)(2,1)S(1)}, bf16[160,256]{1,0:T(8,128)(2,1)S(1)}, u32[]{:S(2)}, u32[]{:S(2)}) collective-permute-start(bf16[160,256]{1,0:T(8,128)(2,1)S(1)} %collective-permute-done.2.refs_2_), channel_id=1, source_target_pairs={{0,800},{16,240},{32,832},{48,272},{64,864},{80,304},{96,896},{112... | collective-permute-start | bytes 245768 | tf_op jit(solution)/shard_map/ppermute | solution.py:31
  52.5 4.4 %collective-permute-done.1.refs_1_ = bf16[160,256]{1,0:T(8,128)(2,1)S(1)} collective-permute-done((bf16[160,256]{1,0:T(8,128)(2,1)S(1)}, bf16[160,256]{1,0:T(8,128)(2,1)S(1)}, u32[]{:S(2)}, u32[]{:S(2)}) %collective-permute-start.1) | collective-permute-done | bytes 81952 | tf_op jit(solution)/shard_map/ppermute | solution.py:31
  56.9 11.9 %collective-permute-start.3 = (bf16[160,256]{1,0:T(8,128)(2,1)S(1)}, bf16[160,256]{1,0:T(8,128)(2,1)S(1)}, u32[]{:S(2)}, u32[]{:S(2)}) collective-permute-start(bf16[160,256]{1,0:T(8,128)(2,1)S(1)} %collective-permute-done.1.refs_1_), channel_id=1, source_target_pairs={{0,224},{16,816},{32,256},{48,848},{64,288},{80,880},{96,320},{112... | collective-permute-start | bytes 245768 | tf_op jit(solution)/shard_map/ppermute | solution.py:31
  68.8 0.0 collective-permute-done.4.refs_4_
  68.8 7.0 %collective-permute-done.3.refs_3_ = bf16[160,256]{1,0:T(8,128)(2,1)S(1)} collective-permute-done((bf16[160,256]{1,0:T(8,128)(2,1)S(1)}, bf16[160,256]{1,0:T(8,128)(2,1)S(1)}, u32[]{:S(2)}, u32[]{:S(2)}) %collective-permute-start.3) | collective-permute-done | bytes 81952 | tf_op jit(solution)/shard_map/ppermute | solution.py:31
  75.9 1.9 %collective-permute-start.5 = (bf16[672,256]{1,0:T(8,128)(2,1)S(1)}, bf16[672,256]{1,0:T(8,128)(2,1)S(1)}, u32[]{:S(2)}, u32[]{:S(2)}) collective-permute-start(bf16[672,256]{1,0:T(8,128)(2,1)S(1)} %get-tuple-element.34.refs_0_), channel_id=1, source_target_pairs={{0,32},{16,1008},{32,64},{48,16},{64,96},{80,48},{96,128},{112,80}... | collective-permute-start | bytes 1032200 | tf_op jit(solution)/shard_map/ppermute | solution.py:31
  77.8 0.7 and_select_fusion.1
  78.5 0.0 copy-start
  78.6 1.6 %copy-done = s32[64,64,128]{2,1,0:T(8,128)S(1)} copy-done((s32[64,64,128]{2,1,0:T(8,128)S(1)}, s32[64,64,128]{2,1,0:T(8,128)}, u32[]{:S(2)}) %copy-start) | copy-done | bytes 2097176
  80.1 0.4 item_weights.1.weight_ref
  80.5 0.0 copy-done.3
  80.5 0.1 select_reduce_fusion
  80.6 3.4 %collective-permute-start.7 = (bf16[544,256]{1,0:T(8,128)(2,1)S(1)}, bf16[544,256]{1,0:T(8,128)(2,1)S(1)}, u32[]{:S(2)}, u32[]{:S(2)}) collective-permute-start(bf16[544,256]{1,0:T(8,128)(2,1)S(1)} %get-tuple-element.39), channel_id=1, source_target_pairs={{0,992},{16,48},{32,0},{48,80},{64,32},{80,112},{96,64},{112,144},... | collective-permute-start | bytes 835592 | tf_op jit(solution)/shard_map/ppermute | solution.py:31
  84.0 0.0 copy-done.2
  84.0 0.7 collect_0.1
  84.7 0.0 collective-permute-done.5.refs_0_
  84.7 3.1 %collective-permute-start.6 = (bf16[672,256]{1,0:T(8,128)(2,1)S(1)}, bf16[672,256]{1,0:T(8,128)(2,1)S(1)}, u32[]{:S(2)}, u32[]{:S(2)}) collective-permute-start(bf16[672,256]{1,0:T(8,128)(2,1)S(1)} %collective-permute-done.5.refs_0_), channel_id=1, source_target_pairs={{0,32},{16,1008},{32,64},{48,16},{64,96},{80,48},{96,128},{112,80}... | collective-permute-start | bytes 1032200 | tf_op jit(solution)/shard_map/ppermute | solution.py:31
  87.9 1.2 collective-permute-done.7.refs_1_
  89.1 3.0 %collective-permute-start.9 = (bf16[544,256]{1,0:T(8,128)(2,1)S(1)}, bf16[544,256]{1,0:T(8,128)(2,1)S(1)}, u32[]{:S(2)}, u32[]{:S(2)}) collective-permute-start(bf16[544,256]{1,0:T(8,128)(2,1)S(1)} %collective-permute-done.7.refs_1_), channel_id=1, source_target_pairs={{0,992},{16,48},{32,0},{48,80},{64,32},{80,112},{96,64},{112,144},... | collective-permute-start | bytes 835592 | tf_op jit(solution)/shard_map/ppermute | solution.py:31
  92.1 0.8 collect_1.1
  93.0 0.1 collective-permute-done.6.refs_0_
  93.0 4.0 %collective-permute-start.8 = (bf16[672,256]{1,0:T(8,128)(2,1)S(1)}, bf16[672,256]{1,0:T(8,128)(2,1)S(1)}, u32[]{:S(2)}, u32[]{:S(2)}) collective-permute-start(bf16[672,256]{1,0:T(8,128)(2,1)S(1)} %collective-permute-done.6.refs_0_), channel_id=1, source_target_pairs={{0,32},{16,1008},{32,64},{48,16},{64,96},{80,48},{96,128},{112,80}... | collective-permute-start | bytes 1032200 | tf_op jit(solution)/shard_map/ppermute | solution.py:31
  97.1 0.5 collective-permute-done.9.refs_1_
  97.6 1.9 %collective-permute-start.10 = (bf16[544,256]{1,0:T(8,128)(2,1)S(1)}, bf16[544,256]{1,0:T(8,128)(2,1)S(1)}, u32[]{:S(2)}, u32[]{:S(2)}) collective-permute-start(bf16[544,256]{1,0:T(8,128)(2,1)S(1)} %collective-permute-done.9.refs_1_), channel_id=1, source_target_pairs={{0,992},{16,48},{32,0},{48,80},{64,32},{80,112},{96,64},{112,144},... | collective-permute-start | bytes 835592 | tf_op jit(solution)/shard_map/ppermute | solution.py:31
  99.5 0.8 collect_2.1
  100.4 1.0 collective-permute-done.8.refs_0_
  101.3 6.1 %collective-permute-done.10.refs_1_ = bf16[544,256]{1,0:T(8,128)(2,1)S(1)} collective-permute-done((bf16[544,256]{1,0:T(8,128)(2,1)S(1)}, bf16[544,256]{1,0:T(8,128)(2,1)S(1)}, u32[]{:S(2)}, u32[]{:S(2)}) %collective-permute-start.10) | collective-permute-done | bytes 278560 | tf_op jit(solution)/shard_map/ppermute | solution.py:31
  107.4 0.8 collect_3.1
  108.3 12.0 %collective-permute-start.11 = (bf16[4096,256]{1,0:T(8,128)(2,1)}, bf16[4096,256]{1,0:T(8,128)(2,1)}, u32[]{:S(2)}, u32[]{:S(2)}) collective-permute-start(bf16[4096,256]{1,0:T(8,128)(2,1)} %get-tuple-element.52.near_ref), channel_id=1, source_target_pairs={{0,16},{16,0},{32,48},{48,32},{64,80},{80,64},{96,112},{112,96},{1... | collective-permute-start | bytes 6291464 | tf_op jit(solution)/shard_map/ppermute | solution.py:36
  120.3 0.7 spread.1
  121.0 3.5 %all-to-all-start.1 = ((f32[16,16,256]{2,1,0:T(8,128)}), f32[16,16,256]{2,1,0:T(8,128)S(1)}, u32[]{:S(2)}, u32[]{:S(2)}) async-start(f32[16,16,256]{2,1,0:T(8,128)} %get-tuple-element.58), calls=%async_computation.1 | async-start | bytes 524288 | tf_op jit(solution)/shard_map/all_to_all | solution.py:391
  124.6 0.0 collective-permute-done.11.other_ref
  124.6 4.8 %first_residue.1 = (bf16[4096,256]{1,0:T(8,128)(2,1)S(1)}, f32[512,256]{1,0:T(8,128)}) custom-call(s32[64]{0:T(128)S(1)} %fusion.places_ref, bf16[4096,256]{1,0:T(8,128)(2,1)} %get-tuple-element.52.near_ref, bf16[4096,256]{1,0:T(8,128)(2,1)} %collective-permute-done.11.other_ref, ...), custom_call_target="tpu_custom_call", output_to_operand_aliasing={{0}: (5, {})} | custom-call | tf_op jit(solution)/shard_map/first_residue/pallas_call | solution.py:188
  129.4 3.6 %all-to-all-done.1 = f32[16,16,256]{2,1,0:T(8,128)S(1)} async-done(((f32[16,16,256]{2,1,0:T(8,128)}), f32[16,16,256]{2,1,0:T(8,128)S(1)}, u32[]{:S(2)}, u32[]{:S(2)}) %all-to-all-start.1) | async-done | bytes 262176 | tf_op jit(solution)/shard_map/all_to_all | solution.py:391
  133.1 7.4 %solve_steps.1 = f32[512,256]{1,0:T(8,128)} custom-call(bf16[4096,256]{1,0:T(8,128)(2,1)S(1)} %get-tuple-element.56.rows_ref, bf16[4,128,1024]{2,1,0:T(8,128)(2,1)S(1)} %item_weights.1.weight_ref, f32[512,256]{1,0:T(8,128)} %items_ref.1, f32[512,256]{1,0:T(8,128)} %get-tuple-element.57.started_ref, f32[256,256]{1,0:T(8,128)S(1)} %bitcast.2), custom_call_target="tpu_custom_call" | custom-call | tf_op jit(solution)/shard_map/solve_steps/pallas_call | solution.py:252
  (4 shorter events, 0.1 us)
Async XLA Ops:
  0.0 0.9 copy-start.1
  16.1 64.4 %copy-start.3 = (s32[32]{0:T(128)S(1)}, s32[32]{0:T(128)}, u32[]{:S(2)}) copy-start(s32[32]{0:T(128)} %constant.83.clone) | copy-start | bytes 388
  16.1 67.8 %copy-start.2 = (s32[64]{0:T(128)S(1)}, s32[64]{0:T(128)}, u32[]{:S(2)}) copy-start(s32[64]{0:T(128)} %param.8) | copy-start | bytes 772
  16.2 13.2 %collective-permute-start = (f32[16,256]{1,0:T(8,128)S(1)}, f32[16,256]{1,0:T(8,128)S(1)}, u32[]{:S(2)}, u32[]{:S(2)}) collective-permute-start(f32[16,256]{1,0:T(8,128)S(1)} %reduce_sum.18.mine_ref), channel_id=1, source_target_pairs={{0,16},{16,0},{32,48},{48,32},{64,80},{80,64},{96,112},{112,96},{1... | collective-permute-start | bytes 49160 | tf_op jit(solution)/shard_map/ppermute | solution.py:36
  29.4 15.9 %collective-permute-start.2 = (bf16[160,256]{1,0:T(8,128)(2,1)S(1)}, bf16[160,256]{1,0:T(8,128)(2,1)S(1)}, u32[]{:S(2)}, u32[]{:S(2)}) collective-permute-start(bf16[160,256]{1,0:T(8,128)(2,1)S(1)} %own.1.refs_0_), channel_id=1, source_target_pairs={{0,800},{16,240},{32,832},{48,272},{64,864},{80,304},{96,896},{112... | collective-permute-start | bytes 245768 | tf_op jit(solution)/shard_map/ppermute | solution.py:31
  33.9 23.0 %collective-permute-start.1 = (bf16[160,256]{1,0:T(8,128)(2,1)S(1)}, bf16[160,256]{1,0:T(8,128)(2,1)S(1)}, u32[]{:S(2)}, u32[]{:S(2)}) collective-permute-start(bf16[160,256]{1,0:T(8,128)(2,1)S(1)} %own.1.refs_0_), channel_id=1, source_target_pairs={{0,224},{16,816},{32,256},{48,848},{64,288},{80,880},{96,320},{112... | collective-permute-start | bytes 245768 | tf_op jit(solution)/shard_map/ppermute | solution.py:31
  45.4 23.5 %collective-permute-start.4 = (bf16[160,256]{1,0:T(8,128)(2,1)S(1)}, bf16[160,256]{1,0:T(8,128)(2,1)S(1)}, u32[]{:S(2)}, u32[]{:S(2)}) collective-permute-start(bf16[160,256]{1,0:T(8,128)(2,1)S(1)} %collective-permute-done.2.refs_2_), channel_id=1, source_target_pairs={{0,800},{16,240},{32,832},{48,272},{64,864},{80,304},{96,896},{112... | collective-permute-start | bytes 245768 | tf_op jit(solution)/shard_map/ppermute | solution.py:31
  56.9 19.0 %collective-permute-start.3 = (bf16[160,256]{1,0:T(8,128)(2,1)S(1)}, bf16[160,256]{1,0:T(8,128)(2,1)S(1)}, u32[]{:S(2)}, u32[]{:S(2)}) collective-permute-start(bf16[160,256]{1,0:T(8,128)(2,1)S(1)} %collective-permute-done.1.refs_1_), channel_id=1, source_target_pairs={{0,224},{16,816},{32,256},{48,848},{64,288},{80,880},{96,320},{112... | collective-permute-start | bytes 245768 | tf_op jit(solution)/shard_map/ppermute | solution.py:31
  75.9 8.8 %collective-permute-start.5 = (bf16[672,256]{1,0:T(8,128)(2,1)S(1)}, bf16[672,256]{1,0:T(8,128)(2,1)S(1)}, u32[]{:S(2)}, u32[]{:S(2)}) collective-permute-start(bf16[672,256]{1,0:T(8,128)(2,1)S(1)} %get-tuple-element.34.refs_0_), channel_id=1, source_target_pairs={{0,32},{16,1008},{32,64},{48,16},{64,96},{80,48},{96,128},{112,80}... | collective-permute-start | bytes 1032200 | tf_op jit(solution)/shard_map/ppermute | solution.py:31
  78.5 1.6 %copy-start = (s32[64,64,128]{2,1,0:T(8,128)S(1)}, s32[64,64,128]{2,1,0:T(8,128)}, u32[]{:S(2)}) copy-start(s32[64,64,128]{2,1,0:T(8,128)} %counts_ref.1) | copy-start | bytes 6291460
  80.6 8.5 %collective-permute-start.7 = (bf16[544,256]{1,0:T(8,128)(2,1)S(1)}, bf16[544,256]{1,0:T(8,128)(2,1)S(1)}, u32[]{:S(2)}, u32[]{:S(2)}) collective-permute-start(bf16[544,256]{1,0:T(8,128)(2,1)S(1)} %get-tuple-element.39), channel_id=1, source_target_pairs={{0,992},{16,48},{32,0},{48,80},{64,32},{80,112},{96,64},{112,144},... | collective-permute-start | bytes 835592 | tf_op jit(solution)/shard_map/ppermute | solution.py:31
  84.7 8.3 %collective-permute-start.6 = (bf16[672,256]{1,0:T(8,128)(2,1)S(1)}, bf16[672,256]{1,0:T(8,128)(2,1)S(1)}, u32[]{:S(2)}, u32[]{:S(2)}) collective-permute-start(bf16[672,256]{1,0:T(8,128)(2,1)S(1)} %collective-permute-done.5.refs_0_), channel_id=1, source_target_pairs={{0,32},{16,1008},{32,64},{48,16},{64,96},{80,48},{96,128},{112,80}... | collective-permute-start | bytes 1032200 | tf_op jit(solution)/shard_map/ppermute | solution.py:31
  89.1 8.5 %collective-permute-start.9 = (bf16[544,256]{1,0:T(8,128)(2,1)S(1)}, bf16[544,256]{1,0:T(8,128)(2,1)S(1)}, u32[]{:S(2)}, u32[]{:S(2)}) collective-permute-start(bf16[544,256]{1,0:T(8,128)(2,1)S(1)} %collective-permute-done.7.refs_1_), channel_id=1, source_target_pairs={{0,992},{16,48},{32,0},{48,80},{64,32},{80,112},{96,64},{112,144},... | collective-permute-start | bytes 835592 | tf_op jit(solution)/shard_map/ppermute | solution.py:31
  93.0 8.3 %collective-permute-start.8 = (bf16[672,256]{1,0:T(8,128)(2,1)S(1)}, bf16[672,256]{1,0:T(8,128)(2,1)S(1)}, u32[]{:S(2)}, u32[]{:S(2)}) collective-permute-start(bf16[672,256]{1,0:T(8,128)(2,1)S(1)} %collective-permute-done.6.refs_0_), channel_id=1, source_target_pairs={{0,32},{16,1008},{32,64},{48,16},{64,96},{80,48},{96,128},{112,80}... | collective-permute-start | bytes 1032200 | tf_op jit(solution)/shard_map/ppermute | solution.py:31
  97.6 9.8 %collective-permute-start.10 = (bf16[544,256]{1,0:T(8,128)(2,1)S(1)}, bf16[544,256]{1,0:T(8,128)(2,1)S(1)}, u32[]{:S(2)}, u32[]{:S(2)}) collective-permute-start(bf16[544,256]{1,0:T(8,128)(2,1)S(1)} %collective-permute-done.9.refs_1_), channel_id=1, source_target_pairs={{0,992},{16,48},{32,0},{48,80},{64,32},{80,112},{96,64},{112,144},... | collective-permute-start | bytes 835592 | tf_op jit(solution)/shard_map/ppermute | solution.py:31
  108.3 16.3 %collective-permute-start.11 = (bf16[4096,256]{1,0:T(8,128)(2,1)}, bf16[4096,256]{1,0:T(8,128)(2,1)}, u32[]{:S(2)}, u32[]{:S(2)}) collective-permute-start(bf16[4096,256]{1,0:T(8,128)(2,1)} %get-tuple-element.52.near_ref), channel_id=1, source_target_pairs={{0,16},{16,0},{32,48},{48,32},{64,80},{80,64},{96,112},{112,96},{1... | collective-permute-start | bytes 6291464 | tf_op jit(solution)/shard_map/ppermute | solution.py:36
  121.0 12.1 %all-to-all-start.1 = ((f32[16,16,256]{2,1,0:T(8,128)}), f32[16,16,256]{2,1,0:T(8,128)S(1)}, u32[]{:S(2)}, u32[]{:S(2)}) async-start(f32[16,16,256]{2,1,0:T(8,128)} %get-tuple-element.58), calls=%async_computation.1 | async-start | bytes 524288 | tf_op jit(solution)/shard_map/all_to_all | solution.py:391

commit v6 on v5

--- a/solution.py
+++ b/solution.py
@@ -312,27 +312,39 @@
     )(*parts, *map(outer, earlier[:1]), *earlier[1:])
 
 
-def spread_kernel(total_ref, out_ref, rows_ref, copies_ref, sem):
-    del rows_ref
-    total = total_ref[...]
+def finish_kernel(rows, places, share, up_ref, down_ref, near_in_ref, total_ref, near_ref, out_ref, rows_ref, copies_ref, sems):
+    del near_in_ref, rows_ref
+    copies = []
+    for at, part in enumerate((up_ref, down_ref)):
+        to = near_ref.at[places[at] : places[at] + rows[at], :]
+        copies.append(pltpu.make_async_copy(part.at[: rows[at], :], to, sems.at[at]))
+        copies[-1].start()
+    total = total_ref[...] + (merge(up_ref[-2 * share :, :]) + merge(down_ref[-2 * share :, :]))
     for copy in range(copies_ref.shape[0]):
         copies_ref[copy] = total
-    write = pltpu.make_async_copy(copies_ref, out_ref, sem)
-    write.start()
-    write.wait()
-
-
-def spread(total, replicas, rows_shape):
+    copies.append(pltpu.make_async_copy(copies_ref, out_ref, sems.at[2]))
+    copies[-1].start()
+    for copy in copies:
+        copy.wait()
+
+
+def finish(parts, rows, places, near, total, replicas, rows_shape):
+    share = total.shape[0]
     shape = (replicas,) + total.shape
     return pl.pallas_call(
-        spread_kernel,
-        out_shape=(pltpu.HBM(shape, jnp.float32), pltpu.VMEM(rows_shape, jnp.bfloat16)),
-        in_specs=[VECTOR],
-        out_specs=(OUTER, VECTOR),
-        scratch_shapes=[pltpu.VMEM(shape, jnp.float32), pltpu.SemaphoreType.DMA],
+        functools.partial(finish_kernel, rows, places, share),
+        out_shape=(
+            pltpu.HBM(near.shape, near.dtype),
+            pltpu.HBM(shape, jnp.float32),
+            pltpu.VMEM(rows_shape, jnp.bfloat16),
+        ),
+        in_specs=[VECTOR, VECTOR, OUTER, VECTOR],
+        out_specs=(OUTER, OUTER, VECTOR),
+        scratch_shapes=[pltpu.VMEM(shape, jnp.float32), pltpu.SemaphoreType.DMA((3,))],
+        input_output_aliases={2: 0},
         compiler_params=pltpu.CompilerParams(vmem_limit_bytes=4 * MIB),
-        name="spread",
-    )(total)
+        name="finish",
+    )(*parts, outer(near), total)
 
 
 def on_device(user_factors, item_factors, tile_users, tile_counts):
@@ -356,6 +368,13 @@
 
     below, above = shift(own, distance=STRIDE), shift(own, distance=-STRIDE)
     far_below, far_above = shift(below, distance=STRIDE), shift(above, distance=-STRIDE)
+    weight = small_call(
+        weight_kernel,
+        pltpu.VMEM((blocks, IBLK, tile_counts.shape[0] * UROWS // blocks), jnp.bfloat16),
+        "item_weights",
+        tile_counts,
+    )
+    far_above, weight = bar((far_above, weight))
     up, down = small_call(
         functools.partial(pack_kernel, owned_rows),
         (half_rows(5 * owned_rows + parts), half_rows(4 * owned_rows + parts)),
@@ -366,28 +385,21 @@
         far_below,
         far_above,
     )
-    weight = small_call(
-        weight_kernel,
-        pltpu.VMEM((blocks, IBLK, tile_counts.shape[0] * UROWS // blocks), jnp.bfloat16),
-        "item_weights",
-        tile_counts,
-    )
-    places = pool_places(tile_users, chips, replicas, owned_rows // UROWS)
     up_rows, down_rows = 5 * owned_rows, 4 * owned_rows
     near_shape = pltpu.HBM((chips * owned_rows, features), jnp.bfloat16)
     near, total = collect("collect_0", [up], [up_rows], [0], near_shape, share)
+    places = pool_places(tile_users, chips, replicas, owned_rows // UROWS)
     for hop in range(1, HOPS + 1):
         up, down = shift(up, distance=1), shift(down, distance=-1)
-        if hop == 1:
-            up, near, total, weight, places = bar((up, near, total, weight, places))
-        else:
-            up, near, total = bar((up, near, total))
+        down, near, total, places = bar((down, near, total, places))
         at = [hop * up_rows, (HOPS + 1) * up_rows + (hop - 1) * down_rows]
-        near, total = collect("collect_" + str(hop), [up, down], [up_rows, down_rows], at, near_shape, share, near, total)
-
+        if hop < HOPS:
+            name = "collect_" + str(hop)
+            near, total = collect(name, [up, down], [up_rows, down_rows], at, near_shape, share, near, total)
+
+    rows_shape = (tile_counts.shape[0] * UROWS, features)
+    near, copies, rows = finish([up, down], [up_rows, down_rows], at, near, total, replicas, rows_shape)
     other = core_swap(near, chips)
-    rows_shape = (tile_counts.shape[0] * UROWS, features)
-    copies, rows = spread(total, replicas, rows_shape)
     gram = lax.all_to_all(copies.reshape(features, features), "rep", 0, 0, tiled=True)
     rows, started = first_residue(places, near, other, weight, item_factors, rows)
     return solve_steps(rows, weight, item_factors, started, gram)

time: 141 us -> 142 us (level)
  waiting for transfers between devices: 24.9 us -> 27.3 us
    ppermute x10, waiting for transfers between devices: 20.4 us -> 22.8 us  [chip_shift(): return lax.ppermute(value, 'grp', pairs)]
    ppermute x2, starting transfers between devices: 24.4 us -> 26 us  [core_swap(): return lax.ppermute(value, 'grp', pairs)]
    ppermute x10, starting transfers between devices: 52.2 us -> 50.7 us  [chip_shift(): return lax.ppermute(value, 'grp', pairs)]
    pallas_call x4 -> x3, Pallas kernels: 3.23 us -> 2.44 us  [collect(): pl.pallas_call(functools.partial(collect_kernel, rows, places, share), ou...]
  transfers between devices with their start and end apart: 13 -> 13, of which waited for: 10 -> 9; matrix products, arithmetic and copies ran while one was open for 1% -> 0% of each run, Pallas kernels for 6% -> 5%
where the time goes in v6:
time: 142 us; the launch traced here: 141 us
  starting transfers between devices  80.2 us (56%)
  waiting for transfers between devices  27.3 us (19%)
  Pallas kernels  16 us (11%)
  blocking collectives  14.9 us (10%)
  local copies, waits for them, and re-layouts  2.5 us (2%)
    ppermute x10, starting transfers between devices, chip_shift(): return lax.ppermute(value, 'grp', pairs)  50.7 us
    ppermute x2, starting transfers between devices, core_swap(): return lax.ppermute(value, 'grp', pairs)  26 us
    ppermute x10, waiting for transfers between devices, chip_shift(): return lax.ppermute(value, 'grp', pairs)  22.8 us
    all_to_all x1, blocking collectives, on_device(): pieces = lax.all_to_all(gram, 'rep', 0, 0, tiled=True)  14.9 us
    pallas_call x1, Pallas kernels, solve_steps(): pl.pallas_call(steps_kernel, out_shape=jax.ShapeDtypeStruct(items.shape,...  7.17 us
    pallas_call x1, Pallas kernels, first_residue(): pl.pallas_call(first_kernel, out_shape=(pltpu.VMEM(rows.shape, rows.dtype...  4.8 us
    all_to_all x1, starting transfers between devices, on_device(): lax.all_to_all(copies.reshape(features, features), 'rep', 0, 0, tiled=True)  3.55 us
    all_to_all x1, waiting for transfers between devices, on_device(): lax.all_to_all(copies.reshape(features, features), 'rep', 0, 0, tiled=True)  3.14 us
  transfers between devices with their start and end apart: 13, of which 9 were waited for; matrix products, arithmetic and copies ran while one was open for 0% of the time, Pallas kernels for 5%

profile of v6, /device:TPU:1, one launch (start us, length us, event | category | flops | bytes accessed | tf_op | source)
XLA Modules:
  0.0 141.5 jit_solution(15623489993783216073)
XLA Ops:
  0.0 0.0 copy-start.1
  0.0 0.9 copy-done.1
  0.9 0.3 local_gram.1
  1.2 14.9 %all_to_all.17 = f32[16,16,256]{2,1,0:T(8,128)S(1)} all-to-all(f32[16,16,256]{2,1,0:T(8,128)S(1)} %bitcast.3), channel_id=1, replica_groups=mesh['grp'=64,'rep'=16] {'rep'}, dimensions={0} | all-to-all | bytes 524288 | tf_op jit(solution)/shard_map/all_to_all | solution.py:365
  16.1 0.0 copy-start.2
  16.1 0.0 copy-start.3
  16.2 12.4 %collective-permute-start = (f32[16,256]{1,0:T(8,128)S(1)}, f32[16,256]{1,0:T(8,128)S(1)}, u32[]{:S(2)}, u32[]{:S(2)}) collective-permute-start(f32[16,256]{1,0:T(8,128)S(1)} %reduce_sum.18.mine_ref), channel_id=1, source_target_pairs={{0,16},{16,0},{32,48},{48,32},{64,80},{80,64},{96,112},{112,96},{1... | collective-permute-start | bytes 49160 | tf_op jit(solution)/shard_map/ppermute | solution.py:36
  28.6 0.8 collective-permute-done.other_ref
  29.4 4.5 %collective-permute-start.2 = (bf16[160,256]{1,0:T(8,128)(2,1)S(1)}, bf16[160,256]{1,0:T(8,128)(2,1)S(1)}, u32[]{:S(2)}, u32[]{:S(2)}) collective-permute-start(bf16[160,256]{1,0:T(8,128)(2,1)S(1)} %own.1.refs_0_), channel_id=1, source_target_pairs={{0,800},{16,240},{32,832},{48,272},{64,864},{80,304},{96,896},{112... | collective-permute-start | bytes 245768 | tf_op jit(solution)/shard_map/ppermute | solution.py:31
  33.9 11.3 %collective-permute-start.1 = (bf16[160,256]{1,0:T(8,128)(2,1)S(1)}, bf16[160,256]{1,0:T(8,128)(2,1)S(1)}, u32[]{:S(2)}, u32[]{:S(2)}) collective-permute-start(bf16[160,256]{1,0:T(8,128)(2,1)S(1)} %own.1.refs_0_), channel_id=1, source_target_pairs={{0,224},{16,816},{32,256},{48,848},{64,288},{80,880},{96,320},{112... | collective-permute-start | bytes 245768 | tf_op jit(solution)/shard_map/ppermute | solution.py:31
  45.2 0.1 collective-permute-done.2.refs_2_
  45.4 7.2 %collective-permute-start.4 = (bf16[160,256]{1,0:T(8,128)(2,1)S(1)}, bf16[160,256]{1,0:T(8,128)(2,1)S(1)}, u32[]{:S(2)}, u32[]{:S(2)}) collective-permute-start(bf16[160,256]{1,0:T(8,128)(2,1)S(1)} %collective-permute-done.2.refs_2_), channel_id=1, source_target_pairs={{0,800},{16,240},{32,832},{48,272},{64,864},{80,304},{96,896},{112... | collective-permute-start | bytes 245768 | tf_op jit(solution)/shard_map/ppermute | solution.py:31
  52.5 4.4 %collective-permute-done.1.refs_1_ = bf16[160,256]{1,0:T(8,128)(2,1)S(1)} collective-permute-done((bf16[160,256]{1,0:T(8,128)(2,1)S(1)}, bf16[160,256]{1,0:T(8,128)(2,1)S(1)}, u32[]{:S(2)}, u32[]{:S(2)}) %collective-permute-start.1) | collective-permute-done | bytes 81952 | tf_op jit(solution)/shard_map/ppermute | solution.py:31
  56.9 11.9 %collective-permute-start.3 = (bf16[160,256]{1,0:T(8,128)(2,1)S(1)}, bf16[160,256]{1,0:T(8,128)(2,1)S(1)}, u32[]{:S(2)}, u32[]{:S(2)}) collective-permute-start(bf16[160,256]{1,0:T(8,128)(2,1)S(1)} %collective-permute-done.1.refs_1_), channel_id=1, source_target_pairs={{0,224},{16,816},{32,256},{48,848},{64,288},{80,880},{96,320},{112... | collective-permute-start | bytes 245768 | tf_op jit(solution)/shard_map/ppermute | solution.py:31
  68.8 0.0 copy-start
  68.8 1.6 %copy-done = s32[64,64,128]{2,1,0:T(8,128)S(1)} copy-done((s32[64,64,128]{2,1,0:T(8,128)S(1)}, s32[64,64,128]{2,1,0:T(8,128)}, u32[]{:S(2)}) %copy-start) | copy-done | bytes 2097176
  70.4 0.4 item_weights.1.weight_ref
  70.8 0.0 collective-permute-done.4.refs_4_
  70.8 5.1 %collective-permute-done.3.refs_3_ = bf16[160,256]{1,0:T(8,128)(2,1)S(1)} collective-permute-done((bf16[160,256]{1,0:T(8,128)(2,1)S(1)}, bf16[160,256]{1,0:T(8,128)(2,1)S(1)}, u32[]{:S(2)}, u32[]{:S(2)}) %collective-permute-start.3) | collective-permute-done | bytes 81952 | tf_op jit(solution)/shard_map/ppermute | solution.py:31
  75.9 1.9 %collective-permute-start.7 = (bf16[672,256]{1,0:T(8,128)(2,1)S(1)}, bf16[672,256]{1,0:T(8,128)(2,1)S(1)}, u32[]{:S(2)}, u32[]{:S(2)}) collective-permute-start(bf16[672,256]{1,0:T(8,128)(2,1)S(1)} %get-tuple-element.38.refs_0_), channel_id=1, source_target_pairs={{0,32},{16,1008},{32,64},{48,16},{64,96},{80,48},{96,128},{112,80}... | collective-permute-start | bytes 1032200 | tf_op jit(solution)/shard_map/ppermute | solution.py:31
  77.9 0.0 copy-done.2
  77.9 3.4 %collective-permute-start.5 = (bf16[544,256]{1,0:T(8,128)(2,1)S(1)}, bf16[544,256]{1,0:T(8,128)(2,1)S(1)}, u32[]{:S(2)}, u32[]{:S(2)}) collective-permute-start(bf16[544,256]{1,0:T(8,128)(2,1)S(1)} %get-tuple-element.37), channel_id=1, source_target_pairs={{0,992},{16,48},{32,0},{48,80},{64,32},{80,112},{96,64},{112,144},... | collective-permute-start | bytes 835592 | tf_op jit(solution)/shard_map/ppermute | solution.py:31
  81.3 0.0 copy-done.3
  81.3 0.1 select_reduce_fusion
  81.4 2.5 %collective-permute-done.7.refs_0_ = bf16[672,256]{1,0:T(8,128)(2,1)S(1)} collective-permute-done((bf16[672,256]{1,0:T(8,128)(2,1)S(1)}, bf16[672,256]{1,0:T(8,128)(2,1)S(1)}, u32[]{:S(2)}, u32[]{:S(2)}) %collective-permute-start.7) | collective-permute-done | bytes 344096 | tf_op jit(solution)/shard_map/ppermute | solution.py:31
  83.9 3.1 %collective-permute-start.9 = (bf16[672,256]{1,0:T(8,128)(2,1)S(1)}, bf16[672,256]{1,0:T(8,128)(2,1)S(1)}, u32[]{:S(2)}, u32[]{:S(2)}) collective-permute-start(bf16[672,256]{1,0:T(8,128)(2,1)S(1)} %collective-permute-done.7.refs_0_), channel_id=1, source_target_pairs={{0,32},{16,1008},{32,64},{48,16},{64,96},{80,48},{96,128},{112,80}... | collective-permute-start | bytes 1032200 | tf_op jit(solution)/shard_map/ppermute | solution.py:31
  87.1 0.7 collect_0.1
  87.8 0.0 collective-permute-done.5.refs_1_
  87.8 2.2 %collective-permute-start.6 = (bf16[544,256]{1,0:T(8,128)(2,1)S(1)}, bf16[544,256]{1,0:T(8,128)(2,1)S(1)}, u32[]{:S(2)}, u32[]{:S(2)}) collective-permute-start(bf16[544,256]{1,0:T(8,128)(2,1)S(1)} %collective-permute-done.5.refs_1_), channel_id=1, source_target_pairs={{0,992},{16,48},{32,0},{48,80},{64,32},{80,112},{96,64},{112,144},... | collective-permute-start | bytes 835592 | tf_op jit(solution)/shard_map/ppermute | solution.py:31
  90.0 3.1 %collective-permute-done.9.refs_0_ = bf16[672,256]{1,0:T(8,128)(2,1)S(1)} collective-permute-done((bf16[672,256]{1,0:T(8,128)(2,1)S(1)}, bf16[672,256]{1,0:T(8,128)(2,1)S(1)}, u32[]{:S(2)}, u32[]{:S(2)}) %collective-permute-start.9) | collective-permute-done | bytes 344096 | tf_op jit(solution)/shard_map/ppermute | solution.py:31
  93.1 3.2 %collective-permute-start.10 = (bf16[672,256]{1,0:T(8,128)(2,1)S(1)}, bf16[672,256]{1,0:T(8,128)(2,1)S(1)}, u32[]{:S(2)}, u32[]{:S(2)}) collective-permute-start(bf16[672,256]{1,0:T(8,128)(2,1)S(1)} %collective-permute-done.9.refs_0_), channel_id=1, source_target_pairs={{0,32},{16,1008},{32,64},{48,16},{64,96},{80,48},{96,128},{112,80}... | collective-permute-start | bytes 1032200 | tf_op jit(solution)/shard_map/ppermute | solution.py:31
  96.2 0.8 collect_1.1
  97.1 0.0 collective-permute-done.6.refs_1_
  97.1 2.1 %collective-permute-start.8 = (bf16[544,256]{1,0:T(8,128)(2,1)S(1)}, bf16[544,256]{1,0:T(8,128)(2,1)S(1)}, u32[]{:S(2)}, u32[]{:S(2)}) collective-permute-start(bf16[544,256]{1,0:T(8,128)(2,1)S(1)} %collective-permute-done.6.refs_1_), channel_id=1, source_target_pairs={{0,992},{16,48},{32,0},{48,80},{64,32},{80,112},{96,64},{112,144},... | collective-permute-start | bytes 835592 | tf_op jit(solution)/shard_map/ppermute | solution.py:31
  99.2 0.9 collect_2.1
  100.1 7.6 %collective-permute-done.8.down_ref = bf16[544,256]{1,0:T(8,128)(2,1)S(1)} collective-permute-done((bf16[544,256]{1,0:T(8,128)(2,1)S(1)}, bf16[544,256]{1,0:T(8,128)(2,1)S(1)}, u32[]{:S(2)}, u32[]{:S(2)}) %collective-permute-start.8) | collective-permute-done | bytes 278560 | tf_op jit(solution)/shard_map/ppermute | solution.py:31
  107.7 0.0 collective-permute-done.10.up_ref
  107.7 0.9 finish.1
  108.6 13.6 %collective-permute-start.11 = (bf16[4096,256]{1,0:T(8,128)(2,1)}, bf16[4096,256]{1,0:T(8,128)(2,1)}, u32[]{:S(2)}, u32[]{:S(2)}) collective-permute-start(bf16[4096,256]{1,0:T(8,128)(2,1)} %get-tuple-element.57.near_ref), channel_id=1, source_target_pairs={{0,16},{16,0},{32,48},{48,32},{64,80},{80,64},{96,112},{112,96},{1... | collective-permute-start | bytes 6291464 | tf_op jit(solution)/shard_map/ppermute | solution.py:36
  122.2 3.5 %all-to-all-start.1 = ((f32[16,16,256]{2,1,0:T(8,128)}), f32[16,16,256]{2,1,0:T(8,128)S(1)}, u32[]{:S(2)}, u32[]{:S(2)}) async-start(f32[16,16,256]{2,1,0:T(8,128)} %get-tuple-element.62), calls=%async_computation.1 | async-start | bytes 524288 | tf_op jit(solution)/shard_map/all_to_all | solution.py:403
  125.8 0.6 collective-permute-done.11.other_ref
  126.3 4.8 %first_residue.1 = (bf16[4096,256]{1,0:T(8,128)(2,1)S(1)}, f32[512,256]{1,0:T(8,128)}) custom-call(s32[64]{0:T(128)S(1)} %fusion.places_ref, bf16[4096,256]{1,0:T(8,128)(2,1)} %get-tuple-element.57.near_ref, bf16[4096,256]{1,0:T(8,128)(2,1)} %collective-permute-done.11.other_ref, ...), custom_call_target="tpu_custom_call", output_to_operand_aliasing={{0}: (5, {})} | custom-call | tf_op jit(solution)/shard_map/first_residue/pallas_call | solution.py:188
  131.1 3.1 %all-to-all-done.1 = f32[16,16,256]{2,1,0:T(8,128)S(1)} async-done(((f32[16,16,256]{2,1,0:T(8,128)}), f32[16,16,256]{2,1,0:T(8,128)S(1)}, u32[]{:S(2)}, u32[]{:S(2)}) %all-to-all-start.1) | async-done | bytes 262176 | tf_op jit(solution)/shard_map/all_to_all | solution.py:403
  134.3 7.2 %solve_steps.1 = f32[512,256]{1,0:T(8,128)} custom-call(bf16[4096,256]{1,0:T(8,128)(2,1)S(1)} %get-tuple-element.60.rows_ref, bf16[4,128,1024]{2,1,0:T(8,128)(2,1)S(1)} %item_weights.1.weight_ref, f32[512,256]{1,0:T(8,128)} %items_ref.1, f32[512,256]{1,0:T(8,128)} %get-tuple-element.61.started_ref, f32[256,256]{1,0:T(8,128)S(1)} %bitcast.2), custom_call_target="tpu_custom_call" | custom-call | tf_op jit(solution)/shard_map/solve_steps/pallas_call | solution.py:252
  (5 shorter events, 0.1 us)
Async XLA Ops:
  0.0 0.9 copy-start.1
  16.1 61.7 %copy-start.2 = (s32[64]{0:T(128)S(1)}, s32[64]{0:T(128)}, u32[]{:S(2)}) copy-start(s32[64]{0:T(128)} %param.8) | copy-start | bytes 772
  16.1 65.1 %copy-start.3 = (s32[32]{0:T(128)S(1)}, s32[32]{0:T(128)}, u32[]{:S(2)}) copy-start(s32[32]{0:T(128)} %constant.83.clone) | copy-start | bytes 388
  16.2 13.2 %collective-permute-start = (f32[16,256]{1,0:T(8,128)S(1)}, f32[16,256]{1,0:T(8,128)S(1)}, u32[]{:S(2)}, u32[]{:S(2)}) collective-permute-start(f32[16,256]{1,0:T(8,128)S(1)} %reduce_sum.18.mine_ref), channel_id=1, source_target_pairs={{0,16},{16,0},{32,48},{48,32},{64,80},{80,64},{96,112},{112,96},{1... | collective-permute-start | bytes 49160 | tf_op jit(solution)/shard_map/ppermute | solution.py:36
  29.4 15.9 %collective-permute-start.2 = (bf16[160,256]{1,0:T(8,128)(2,1)S(1)}, bf16[160,256]{1,0:T(8,128)(2,1)S(1)}, u32[]{:S(2)}, u32[]{:S(2)}) collective-permute-start(bf16[160,256]{1,0:T(8,128)(2,1)S(1)} %own.1.refs_0_), channel_id=1, source_target_pairs={{0,800},{16,240},{32,832},{48,272},{64,864},{80,304},{96,896},{112... | collective-permute-start | bytes 245768 | tf_op jit(solution)/shard_map/ppermute | solution.py:31
  33.9 23.0 %collective-permute-start.1 = (bf16[160,256]{1,0:T(8,128)(2,1)S(1)}, bf16[160,256]{1,0:T(8,128)(2,1)S(1)}, u32[]{:S(2)}, u32[]{:S(2)}) collective-permute-start(bf16[160,256]{1,0:T(8,128)(2,1)S(1)} %own.1.refs_0_), channel_id=1, source_target_pairs={{0,224},{16,816},{32,256},{48,848},{64,288},{80,880},{96,320},{112... | collective-permute-start | bytes 245768 | tf_op jit(solution)/shard_map/ppermute | solution.py:31
  45.4 25.4 %collective-permute-start.4 = (bf16[160,256]{1,0:T(8,128)(2,1)S(1)}, bf16[160,256]{1,0:T(8,128)(2,1)S(1)}, u32[]{:S(2)}, u32[]{:S(2)}) collective-permute-start(bf16[160,256]{1,0:T(8,128)(2,1)S(1)} %collective-permute-done.2.refs_2_), channel_id=1, source_target_pairs={{0,800},{16,240},{32,832},{48,272},{64,864},{80,304},{96,896},{112... | collective-permute-start | bytes 245768 | tf_op jit(solution)/shard_map/ppermute | solution.py:31
  56.9 19.0 %collective-permute-start.3 = (bf16[160,256]{1,0:T(8,128)(2,1)S(1)}, bf16[160,256]{1,0:T(8,128)(2,1)S(1)}, u32[]{:S(2)}, u32[]{:S(2)}) collective-permute-start(bf16[160,256]{1,0:T(8,128)(2,1)S(1)} %collective-permute-done.1.refs_1_), channel_id=1, source_target_pairs={{0,224},{16,816},{32,256},{48,848},{64,288},{80,880},{96,320},{112... | collective-permute-start | bytes 245768 | tf_op jit(solution)/shard_map/ppermute | solution.py:31
  68.8 1.6 %copy-start = (s32[64,64,128]{2,1,0:T(8,128)S(1)}, s32[64,64,128]{2,1,0:T(8,128)}, u32[]{:S(2)}) copy-start(s32[64,64,128]{2,1,0:T(8,128)} %counts_ref.1) | copy-start | bytes 6291460
  75.9 8.0 %collective-permute-start.7 = (bf16[672,256]{1,0:T(8,128)(2,1)S(1)}, bf16[672,256]{1,0:T(8,128)(2,1)S(1)}, u32[]{:S(2)}, u32[]{:S(2)}) collective-permute-start(bf16[672,256]{1,0:T(8,128)(2,1)S(1)} %get-tuple-element.38.refs_0_), channel_id=1, source_target_pairs={{0,32},{16,1008},{32,64},{48,16},{64,96},{80,48},{96,128},{112,80}... | collective-permute-start | bytes 1032200 | tf_op jit(solution)/shard_map/ppermute | solution.py:31
  77.9 9.9 %collective-permute-start.5 = (bf16[544,256]{1,0:T(8,128)(2,1)S(1)}, bf16[544,256]{1,0:T(8,128)(2,1)S(1)}, u32[]{:S(2)}, u32[]{:S(2)}) collective-permute-start(bf16[544,256]{1,0:T(8,128)(2,1)S(1)} %get-tuple-element.37), channel_id=1, source_target_pairs={{0,992},{16,48},{32,0},{48,80},{64,32},{80,112},{96,64},{112,144},... | collective-permute-start | bytes 835592 | tf_op jit(solution)/shard_map/ppermute | solution.py:31
  83.9 9.1 %collective-permute-start.9 = (bf16[672,256]{1,0:T(8,128)(2,1)S(1)}, bf16[672,256]{1,0:T(8,128)(2,1)S(1)}, u32[]{:S(2)}, u32[]{:S(2)}) collective-permute-start(bf16[672,256]{1,0:T(8,128)(2,1)S(1)} %collective-permute-done.7.refs_0_), channel_id=1, source_target_pairs={{0,32},{16,1008},{32,64},{48,16},{64,96},{80,48},{96,128},{112,80}... | collective-permute-start | bytes 1032200 | tf_op jit(solution)/shard_map/ppermute | solution.py:31
  87.8 9.3 %collective-permute-start.6 = (bf16[544,256]{1,0:T(8,128)(2,1)S(1)}, bf16[544,256]{1,0:T(8,128)(2,1)S(1)}, u32[]{:S(2)}, u32[]{:S(2)}) collective-permute-start(bf16[544,256]{1,0:T(8,128)(2,1)S(1)} %collective-permute-done.5.refs_1_), channel_id=1, source_target_pairs={{0,992},{16,48},{32,0},{48,80},{64,32},{80,112},{96,64},{112,144},... | collective-permute-start | bytes 835592 | tf_op jit(solution)/shard_map/ppermute | solution.py:31
  93.1 14.6 %collective-permute-start.10 = (bf16[672,256]{1,0:T(8,128)(2,1)S(1)}, bf16[672,256]{1,0:T(8,128)(2,1)S(1)}, u32[]{:S(2)}, u32[]{:S(2)}) collective-permute-start(bf16[672,256]{1,0:T(8,128)(2,1)S(1)} %collective-permute-done.9.refs_0_), channel_id=1, source_target_pairs={{0,32},{16,1008},{32,64},{48,16},{64,96},{80,48},{96,128},{112,80}... | collective-permute-start | bytes 1032200 | tf_op jit(solution)/shard_map/ppermute | solution.py:31
  97.1 10.6 %collective-permute-start.8 = (bf16[544,256]{1,0:T(8,128)(2,1)S(1)}, bf16[544,256]{1,0:T(8,128)(2,1)S(1)}, u32[]{:S(2)}, u32[]{:S(2)}) collective-permute-start(bf16[544,256]{1,0:T(8,128)(2,1)S(1)} %collective-permute-done.6.refs_1_), channel_id=1, source_target_pairs={{0,992},{16,48},{32,0},{48,80},{64,32},{80,112},{96,64},{112,144},... | collective-permute-start | bytes 835592 | tf_op jit(solution)/shard_map/ppermute | solution.py:31
  108.6 17.7 %collective-permute-start.11 = (bf16[4096,256]{1,0:T(8,128)(2,1)}, bf16[4096,256]{1,0:T(8,128)(2,1)}, u32[]{:S(2)}, u32[]{:S(2)}) collective-permute-start(bf16[4096,256]{1,0:T(8,128)(2,1)} %get-tuple-element.57.near_ref), channel_id=1, source_target_pairs={{0,16},{16,0},{32,48},{48,32},{64,80},{80,64},{96,112},{112,96},{1... | collective-permute-start | bytes 6291464 | tf_op jit(solution)/shard_map/ppermute | solution.py:36
  122.2 12.1 %all-to-all-start.1 = ((f32[16,16,256]{2,1,0:T(8,128)}), f32[16,16,256]{2,1,0:T(8,128)S(1)}, u32[]{:S(2)}, u32[]{:S(2)}) async-start(f32[16,16,256]{2,1,0:T(8,128)} %get-tuple-element.62), calls=%async_computation.1 | async-start | bytes 524288 | tf_op jit(solution)/shard_map/all_to_all | solution.py:403

commit v7 on v6

--- a/solution.py
+++ b/solution.py
@@ -265,14 +265,22 @@
     ref[start : start + count, :], ref[start + count : start + 2 * count, :] = high_low(value)
 
 
-def own_kernel(own_ref, mine_ref, other_ref, out_ref):
+def own_kernel(own_ref, gram_ref, out_ref):
     rows = own_ref.shape[0]
     out_ref[:rows, :] = own_ref[...]
-    put_parts(out_ref, rows, mine_ref[...] + other_ref[...])
+    put_parts(out_ref, rows, gram_ref[...])
+
+
+def pair_kernel(mine_ref, other_ref, out_ref):
+    rows = out_ref.shape[0] - mine_ref.shape[0]
+    out_ref[:rows, :] = mine_ref[:rows, :]
+    out_ref[rows : 2 * rows, :] = other_ref[:rows, :]
+    put_parts(out_ref, 2 * rows, merge(mine_ref[rows:, :]) + merge(other_ref[rows:, :]))
 
 
 def pack_kernel(rows, *refs):
     parts, (up_ref, down_ref) = refs[:-2], refs[-2:]
+    parts_rows = up_ref.shape[0] - len(parts) * rows
     total = None
     for place, part in enumerate(parts):
         up_ref[place * rows : (place + 1) * rows, :] = part[:rows, :]
@@ -280,7 +288,7 @@
             down_ref[place * rows : (place + 1) * rows, :] = part[:rows, :]
         else:
             put_parts(down_ref, place * rows, total)
-        piece = merge(part[rows:, :])
+        piece = merge(part[-parts_rows:, :])
         total = piece if total is None else total + piece
     put_parts(up_ref, len(parts) * rows, total)
 
@@ -364,17 +372,20 @@
     gram, own = small_call(gram_kernel, (square, half_rows(owned_rows)), "local_gram", user_factors)
     pieces = lax.all_to_all(gram, "rep", 0, 0, tiled=True)
     gram = jnp.sum(pieces.reshape(replicas, share, features), axis=0)
-    own = small_call(own_kernel, half_rows(owned_rows + parts), "own", own, gram, core_swap(gram, chips))
-
-    below, above = shift(own, distance=STRIDE), shift(own, distance=-STRIDE)
-    far_below, far_above = shift(below, distance=STRIDE), shift(above, distance=-STRIDE)
+    mine = small_call(own_kernel, half_rows(owned_rows + parts), "own", own, gram)
+    own = small_call(pair_kernel, half_rows(2 * owned_rows + parts), "pair", mine, core_swap(mine, chips))
+
+    below = shift(own, distance=STRIDE)
+    far_below = shift(below, distance=STRIDE)
+    above = core_swap(below[owned_rows:], chips)
     weight = small_call(
         weight_kernel,
         pltpu.VMEM((blocks, IBLK, tile_counts.shape[0] * UROWS // blocks), jnp.bfloat16),
         "item_weights",
         tile_counts,
     )
-    far_above, weight = bar((far_above, weight))
+    far_below, above, weight = bar((far_below, above, weight))
+    far_above = core_swap(far_below[owned_rows:], chips)
     up, down = small_call(
         functools.partial(pack_kernel, owned_rows),
         (half_rows(5 * owned_rows + parts), half_rows(4 * owned_rows + parts)),

time: 142 us -> 141 us (level)
  starting transfers between devices: 80.2 us -> 77.7 us
    ppermute x10 -> x8, starting transfers between devices: 50.7 us -> 46.7 us  [chip_shift(): return lax.ppermute(value, 'grp', pairs)]
    ppermute x2 -> x4, starting transfers between devices: 26 us -> 27.5 us  [core_swap(): return lax.ppermute(value, 'grp', pairs)]
    ppermute x10 -> x8, waiting for transfers between devices: 22.8 us -> 22.9 us  [chip_shift(): return lax.ppermute(value, 'grp', pairs)]
  transfers between devices with their start and end apart: 13 -> 13, of which waited for: 9 -> 11; matrix products, arithmetic and copies ran while one was open for 0% -> 0% of each run, Pallas kernels for 5% -> 5%
where the time goes in v7:
time: 141 us; the launch traced here: 140 us
  starting transfers between devices  77.7 us (55%)
  waiting for transfers between devices  28.4 us (20%)
  Pallas kernels  16.1 us (11%)
  blocking collectives  14.9 us (11%)
  local copies, waits for them, and re-layouts  2.52 us (2%)
    ppermute x8, starting transfers between devices, chip_shift(): return lax.ppermute(value, 'grp', pairs)  46.7 us
    ppermute x4, starting transfers between devices, core_swap(): return lax.ppermute(value, 'grp', pairs)  27.5 us
    ppermute x8, waiting for transfers between devices, chip_shift(): return lax.ppermute(value, 'grp', pairs)  22.9 us
    all_to_all x1, blocking collectives, on_device(): pieces = lax.all_to_all(gram, 'rep', 0, 0, tiled=True)  14.9 us
    pallas_call x1, Pallas kernels, solve_steps(): pl.pallas_call(steps_kernel, out_shape=jax.ShapeDtypeStruct(items.shape,...  7.17 us
    pallas_call x1, Pallas kernels, first_residue(): pl.pallas_call(first_kernel, out_shape=(pltpu.VMEM(rows.shape, rows.dtype...  4.8 us
    all_to_all x1, starting transfers between devices, on_device(): lax.all_to_all(copies.reshape(features, features), 'rep', 0, 0, tiled=True)  3.55 us
    all_to_all x1, waiting for transfers between devices, on_device(): lax.all_to_all(copies.reshape(features, features), 'rep', 0, 0, tiled=True)  3.15 us
  transfers between devices with their start and end apart: 13, of which 11 were waited for; matrix products, arithmetic and copies ran while one was open for 0% of the time, Pallas kernels for 5%

profile of v7, /device:TPU:1, one launch (start us, length us, event | category | flops | bytes accessed | tf_op | source)
XLA Modules:
  0.0 140.0 jit_solution(17581555584009052679)
XLA Ops:
  0.0 0.0 copy-start.1
  0.0 0.9 copy-done.1
  0.9 0.3 local_gram.1
  1.2 14.9 %all_to_all.17 = f32[16,16,256]{2,1,0:T(8,128)S(1)} all-to-all(f32[16,16,256]{2,1,0:T(8,128)S(1)} %bitcast.3), channel_id=1, replica_groups=mesh['grp'=64,'rep'=16] {'rep'}, dimensions={0} | all-to-all | bytes 524288 | tf_op jit(solution)/shard_map/all_to_all | solution.py:373
  16.2 12.4 %collective-permute-start = (bf16[160,256]{1,0:T(8,128)(2,1)S(1)}, bf16[160,256]{1,0:T(8,128)(2,1)S(1)}, u32[]{:S(2)}, u32[]{:S(2)}) collective-permute-start(bf16[160,256]{1,0:T(8,128)(2,1)S(1)} %own.1.mine_ref), channel_id=1, source_target_pairs={{0,16},{16,0},{32,48},{48,32},{64,80},{80,64},{96,112},{112,96},{1... | collective-permute-start | bytes 245768 | tf_op jit(solution)/shard_map/ppermute | solution.py:36
  28.6 0.9 collective-permute-done.other_ref
  29.5 0.0 copy-start.2
  29.5 0.0 copy-start.3
  29.5 13.9 %collective-permute-start.1 = (bf16[288,256]{1,0:T(8,128)(2,1)S(1)}, bf16[288,256]{1,0:T(8,128)(2,1)S(1)}, u32[]{:S(2)}, u32[]{:S(2)}) collective-permute-start(bf16[288,256]{1,0:T(8,128)(2,1)S(1)} %pair.1.refs_0_), channel_id=1, source_target_pairs={{0,224},{16,816},{32,256},{48,848},{64,288},{80,880},{96,320},{112... | collective-permute-start | bytes 442376 | tf_op jit(solution)/shard_map/ppermute | solution.py:31
  43.4 5.2 %collective-permute-done.1.refs_1_ = bf16[288,256]{1,0:T(8,128)(2,1)S(1)} collective-permute-done((bf16[288,256]{1,0:T(8,128)(2,1)S(1)}, bf16[288,256]{1,0:T(8,128)(2,1)S(1)}, u32[]{:S(2)}, u32[]{:S(2)}) %collective-permute-start.1) | collective-permute-done | bytes 147488 | tf_op jit(solution)/shard_map/ppermute | solution.py:31
  48.7 17.9 %collective-permute-start.2 = (bf16[288,256]{1,0:T(8,128)(2,1)S(1)}, bf16[288,256]{1,0:T(8,128)(2,1)S(1)}, u32[]{:S(2)}, u32[]{:S(2)}) collective-permute-start(bf16[288,256]{1,0:T(8,128)(2,1)S(1)} %collective-permute-done.1.refs_1_), channel_id=1, source_target_pairs={{0,224},{16,816},{32,256},{48,848},{64,288},{80,880},{96,320},{112... | collective-permute-start | bytes 442376 | tf_op jit(solution)/shard_map/ppermute | solution.py:31
  66.6 1.9 %collective-permute-start.3 = (bf16[160,256]{1,0:T(8,128)(2,1)S(1)}, bf16[160,256]{1,0:T(8,128)(2,1)S(1)}, u32[]{:S(2)}, u32[]{:S(2)}) collective-permute-start(bf16[160,256]{1,0:T(8,128)(2,1)S(1)} %slice.8), channel_id=1, source_target_pairs={{0,16},{16,0},{32,48},{48,32},{64,80},{80,64},{96,112},{112,96},{1... | collective-permute-start | bytes 245768 | tf_op jit(solution)/shard_map/ppermute | solution.py:36
  68.5 0.0 copy-start
  68.5 1.6 %copy-done = s32[64,64,128]{2,1,0:T(8,128)S(1)} copy-done((s32[64,64,128]{2,1,0:T(8,128)S(1)}, s32[64,64,128]{2,1,0:T(8,128)}, u32[]{:S(2)}) %copy-start) | copy-done | bytes 2097176
  70.1 0.4 item_weights.1.weight_ref
  70.5 0.0 collective-permute-done.3.refs_2_
  70.5 1.6 %collective-permute-done.2.refs_3_ = bf16[288,256]{1,0:T(8,128)(2,1)S(1)} collective-permute-done((bf16[288,256]{1,0:T(8,128)(2,1)S(1)}, bf16[288,256]{1,0:T(8,128)(2,1)S(1)}, u32[]{:S(2)}, u32[]{:S(2)}) %collective-permute-start.2) | collective-permute-done | bytes 147488 | tf_op jit(solution)/shard_map/ppermute | solution.py:31
  72.1 7.1 %collective-permute-start.4 = (bf16[160,256]{1,0:T(8,128)(2,1)S(1)}, bf16[160,256]{1,0:T(8,128)(2,1)S(1)}, u32[]{:S(2)}, u32[]{:S(2)}) collective-permute-start(bf16[160,256]{1,0:T(8,128)(2,1)S(1)} %slice.7), channel_id=1, source_target_pairs={{0,16},{16,0},{32,48},{48,32},{64,80},{80,64},{96,112},{112,96},{1... | collective-permute-start | bytes 245768 | tf_op jit(solution)/shard_map/ppermute | solution.py:36
  79.1 0.9 collective-permute-done.4.refs_4_
  80.1 1.9 %collective-permute-start.7 = (bf16[672,256]{1,0:T(8,128)(2,1)S(1)}, bf16[672,256]{1,0:T(8,128)(2,1)S(1)}, u32[]{:S(2)}, u32[]{:S(2)}) collective-permute-start(bf16[672,256]{1,0:T(8,128)(2,1)S(1)} %get-tuple-element.40.refs_0_), channel_id=1, source_target_pairs={{0,32},{16,1008},{32,64},{48,16},{64,96},{80,48},{96,128},{112,80}... | collective-permute-start | bytes 1032200 | tf_op jit(solution)/shard_map/ppermute | solution.py:31
  82.0 0.0 copy-done.2
  82.1 3.4 %collective-permute-start.5 = (bf16[544,256]{1,0:T(8,128)(2,1)S(1)}, bf16[544,256]{1,0:T(8,128)(2,1)S(1)}, u32[]{:S(2)}, u32[]{:S(2)}) collective-permute-start(bf16[544,256]{1,0:T(8,128)(2,1)S(1)} %get-tuple-element.39), channel_id=1, source_target_pairs={{0,992},{16,48},{32,0},{48,80},{64,32},{80,112},{96,64},{112,144},... | collective-permute-start | bytes 835592 | tf_op jit(solution)/shard_map/ppermute | solution.py:31
  85.4 0.0 copy-done.3
  85.5 0.1 select_reduce_fusion
  85.5 3.7 %collective-permute-done.7.refs_0_ = bf16[672,256]{1,0:T(8,128)(2,1)S(1)} collective-permute-done((bf16[672,256]{1,0:T(8,128)(2,1)S(1)}, bf16[672,256]{1,0:T(8,128)(2,1)S(1)}, u32[]{:S(2)}, u32[]{:S(2)}) %collective-permute-start.7) | collective-permute-done | bytes 344096 | tf_op jit(solution)/shard_map/ppermute | solution.py:31
  89.2 2.0 %collective-permute-start.9 = (bf16[672,256]{1,0:T(8,128)(2,1)S(1)}, bf16[672,256]{1,0:T(8,128)(2,1)S(1)}, u32[]{:S(2)}, u32[]{:S(2)}) collective-permute-start(bf16[672,256]{1,0:T(8,128)(2,1)S(1)} %collective-permute-done.7.refs_0_), channel_id=1, source_target_pairs={{0,32},{16,1008},{32,64},{48,16},{64,96},{80,48},{96,128},{112,80}... | collective-permute-start | bytes 1032200 | tf_op jit(solution)/shard_map/ppermute | solution.py:31
  91.2 0.7 collect_0.1
  92.0 1.1 collective-permute-done.5.refs_1_
  93.1 2.2 %collective-permute-start.6 = (bf16[544,256]{1,0:T(8,128)(2,1)S(1)}, bf16[544,256]{1,0:T(8,128)(2,1)S(1)}, u32[]{:S(2)}, u32[]{:S(2)}) collective-permute-start(bf16[544,256]{1,0:T(8,128)(2,1)S(1)} %collective-permute-done.5.refs_1_), channel_id=1, source_target_pairs={{0,992},{16,48},{32,0},{48,80},{64,32},{80,112},{96,64},{112,144},... | collective-permute-start | bytes 835592 | tf_op jit(solution)/shard_map/ppermute | solution.py:31
  95.3 1.9 %collective-permute-done.9.refs_0_ = bf16[672,256]{1,0:T(8,128)(2,1)S(1)} collective-permute-done((bf16[672,256]{1,0:T(8,128)(2,1)S(1)}, bf16[672,256]{1,0:T(8,128)(2,1)S(1)}, u32[]{:S(2)}, u32[]{:S(2)}) %collective-permute-start.9) | collective-permute-done | bytes 344096 | tf_op jit(solution)/shard_map/ppermute | solution.py:31
  97.2 3.6 %collective-permute-start.10 = (bf16[672,256]{1,0:T(8,128)(2,1)S(1)}, bf16[672,256]{1,0:T(8,128)(2,1)S(1)}, u32[]{:S(2)}, u32[]{:S(2)}) collective-permute-start(bf16[672,256]{1,0:T(8,128)(2,1)S(1)} %collective-permute-done.9.refs_0_), channel_id=1, source_target_pairs={{0,32},{16,1008},{32,64},{48,16},{64,96},{80,48},{96,128},{112,80}... | collective-permute-start | bytes 1032200 | tf_op jit(solution)/shard_map/ppermute | solution.py:31
  100.8 0.8 collect_1.1
  101.6 2.6 %collective-permute-done.6.refs_1_ = bf16[544,256]{1,0:T(8,128)(2,1)S(1)} collective-permute-done((bf16[544,256]{1,0:T(8,128)(2,1)S(1)}, bf16[544,256]{1,0:T(8,128)(2,1)S(1)}, u32[]{:S(2)}, u32[]{:S(2)}) %collective-permute-start.6) | collective-permute-done | bytes 278560 | tf_op jit(solution)/shard_map/ppermute | solution.py:31
  104.3 1.9 %collective-permute-start.8 = (bf16[544,256]{1,0:T(8,128)(2,1)S(1)}, bf16[544,256]{1,0:T(8,128)(2,1)S(1)}, u32[]{:S(2)}, u32[]{:S(2)}) collective-permute-start(bf16[544,256]{1,0:T(8,128)(2,1)S(1)} %collective-permute-done.6.refs_1_), channel_id=1, source_target_pairs={{0,992},{16,48},{32,0},{48,80},{64,32},{80,112},{96,64},{112,144},... | collective-permute-start | bytes 835592 | tf_op jit(solution)/shard_map/ppermute | solution.py:31
  106.2 0.9 collect_2.1
  107.0 6.7 %collective-permute-done.8.down_ref = bf16[544,256]{1,0:T(8,128)(2,1)S(1)} collective-permute-done((bf16[544,256]{1,0:T(8,128)(2,1)S(1)}, bf16[544,256]{1,0:T(8,128)(2,1)S(1)}, u32[]{:S(2)}, u32[]{:S(2)}) %collective-permute-start.8) | collective-permute-done | bytes 278560 | tf_op jit(solution)/shard_map/ppermute | solution.py:31
  113.8 0.0 collective-permute-done.10.up_ref
  113.8 0.9 finish.1
  114.7 6.0 %collective-permute-start.11 = (bf16[4096,256]{1,0:T(8,128)(2,1)}, bf16[4096,256]{1,0:T(8,128)(2,1)}, u32[]{:S(2)}, u32[]{:S(2)}) collective-permute-start(bf16[4096,256]{1,0:T(8,128)(2,1)} %get-tuple-element.59.near_ref), channel_id=1, source_target_pairs={{0,16},{16,0},{32,48},{48,32},{64,80},{80,64},{96,112},{112,96},{1... | collective-permute-start | bytes 6291464 | tf_op jit(solution)/shard_map/ppermute | solution.py:36
  120.8 3.5 %all-to-all-start.1 = ((f32[16,16,256]{2,1,0:T(8,128)}), f32[16,16,256]{2,1,0:T(8,128)S(1)}, u32[]{:S(2)}, u32[]{:S(2)}) async-start(f32[16,16,256]{2,1,0:T(8,128)} %get-tuple-element.64), calls=%async_computation.1 | async-start | bytes 524288 | tf_op jit(solution)/shard_map/all_to_all | solution.py:414
  124.3 0.6 collective-permute-done.11.other_ref
  124.9 4.8 %first_residue.1 = (bf16[4096,256]{1,0:T(8,128)(2,1)S(1)}, f32[512,256]{1,0:T(8,128)}) custom-call(s32[64]{0:T(128)S(1)} %fusion.places_ref, bf16[4096,256]{1,0:T(8,128)(2,1)} %get-tuple-element.59.near_ref, bf16[4096,256]{1,0:T(8,128)(2,1)} %collective-permute-done.11.other_ref, ...), custom_call_target="tpu_custom_call", output_to_operand_aliasing={{0}: (5, {})} | custom-call | tf_op jit(solution)/shard_map/first_residue/pallas_call | solution.py:188
  129.7 3.1 %all-to-all-done.1 = f32[16,16,256]{2,1,0:T(8,128)S(1)} async-done(((f32[16,16,256]{2,1,0:T(8,128)}), f32[16,16,256]{2,1,0:T(8,128)S(1)}, u32[]{:S(2)}, u32[]{:S(2)}) %all-to-all-start.1) | async-done | bytes 262176 | tf_op jit(solution)/shard_map/all_to_all | solution.py:414
  132.8 7.2 %solve_steps.1 = f32[512,256]{1,0:T(8,128)} custom-call(bf16[4096,256]{1,0:T(8,128)(2,1)S(1)} %get-tuple-element.62.rows_ref, bf16[4,128,1024]{2,1,0:T(8,128)(2,1)S(1)} %item_weights.1.weight_ref, f32[512,256]{1,0:T(8,128)} %items_ref.1, f32[512,256]{1,0:T(8,128)} %get-tuple-element.63.started_ref, f32[256,256]{1,0:T(8,128)S(1)} %bitcast.2), custom_call_target="tpu_custom_call" | custom-call | tf_op jit(solution)/shard_map/solve_steps/pallas_call | solution.py:252
  (8 shorter events, 0.2 us)
Async XLA Ops:
  0.0 0.9 copy-start.1
  16.2 13.3 %collective-permute-start = (bf16[160,256]{1,0:T(8,128)(2,1)S(1)}, bf16[160,256]{1,0:T(8,128)(2,1)S(1)}, u32[]{:S(2)}, u32[]{:S(2)}) collective-permute-start(bf16[160,256]{1,0:T(8,128)(2,1)S(1)} %own.1.mine_ref), channel_id=1, source_target_pairs={{0,16},{16,0},{32,48},{48,32},{64,80},{80,64},{96,112},{112,96},{1... | collective-permute-start | bytes 245768 | tf_op jit(solution)/shard_map/ppermute | solution.py:36
  29.5 52.5 %copy-start.2 = (s32[64]{0:T(128)S(1)}, s32[64]{0:T(128)}, u32[]{:S(2)}) copy-start(s32[64]{0:T(128)} %param.8) | copy-start | bytes 772
  29.5 55.9 %copy-start.3 = (s32[32]{0:T(128)S(1)}, s32[32]{0:T(128)}, u32[]{:S(2)}) copy-start(s32[32]{0:T(128)} %constant.83.clone) | copy-start | bytes 388
  29.5 19.1 %collective-permute-start.1 = (bf16[288,256]{1,0:T(8,128)(2,1)S(1)}, bf16[288,256]{1,0:T(8,128)(2,1)S(1)}, u32[]{:S(2)}, u32[]{:S(2)}) collective-permute-start(bf16[288,256]{1,0:T(8,128)(2,1)S(1)} %pair.1.refs_0_), channel_id=1, source_target_pairs={{0,224},{16,816},{32,256},{48,848},{64,288},{80,880},{96,320},{112... | collective-permute-start | bytes 442376 | tf_op jit(solution)/shard_map/ppermute | solution.py:31
  48.7 23.4 %collective-permute-start.2 = (bf16[288,256]{1,0:T(8,128)(2,1)S(1)}, bf16[288,256]{1,0:T(8,128)(2,1)S(1)}, u32[]{:S(2)}, u32[]{:S(2)}) collective-permute-start(bf16[288,256]{1,0:T(8,128)(2,1)S(1)} %collective-permute-done.1.refs_1_), channel_id=1, source_target_pairs={{0,224},{16,816},{32,256},{48,848},{64,288},{80,880},{96,320},{112... | collective-permute-start | bytes 442376 | tf_op jit(solution)/shard_map/ppermute | solution.py:31
  66.6 3.9 %collective-permute-start.3 = (bf16[160,256]{1,0:T(8,128)(2,1)S(1)}, bf16[160,256]{1,0:T(8,128)(2,1)S(1)}, u32[]{:S(2)}, u32[]{:S(2)}) collective-permute-start(bf16[160,256]{1,0:T(8,128)(2,1)S(1)} %slice.8), channel_id=1, source_target_pairs={{0,16},{16,0},{32,48},{48,32},{64,80},{80,64},{96,112},{112,96},{1... | collective-permute-start | bytes 245768 | tf_op jit(solution)/shard_map/ppermute | solution.py:36
  68.5 1.6 %copy-start = (s32[64,64,128]{2,1,0:T(8,128)S(1)}, s32[64,64,128]{2,1,0:T(8,128)}, u32[]{:S(2)}) copy-start(s32[64,64,128]{2,1,0:T(8,128)} %counts_ref.1) | copy-start | bytes 6291460
  72.1 8.0 %collective-permute-start.4 = (bf16[160,256]{1,0:T(8,128)(2,1)S(1)}, bf16[160,256]{1,0:T(8,128)(2,1)S(1)}, u32[]{:S(2)}, u32[]{:S(2)}) collective-permute-start(bf16[160,256]{1,0:T(8,128)(2,1)S(1)} %slice.7), channel_id=1, source_target_pairs={{0,16},{16,0},{32,48},{48,32},{64,80},{80,64},{96,112},{112,96},{1... | collective-permute-start | bytes 245768 | tf_op jit(solution)/shard_map/ppermute | solution.py:36
  80.1 9.1 %collective-permute-start.7 = (bf16[672,256]{1,0:T(8,128)(2,1)S(1)}, bf16[672,256]{1,0:T(8,128)(2,1)S(1)}, u32[]{:S(2)}, u32[]{:S(2)}) collective-permute-start(bf16[672,256]{1,0:T(8,128)(2,1)S(1)} %get-tuple-element.40.refs_0_), channel_id=1, source_target_pairs={{0,32},{16,1008},{32,64},{48,16},{64,96},{80,48},{96,128},{112,80}... | collective-permute-start | bytes 1032200 | tf_op jit(solution)/shard_map/ppermute | solution.py:31
  82.1 11.0 %collective-permute-start.5 = (bf16[544,256]{1,0:T(8,128)(2,1)S(1)}, bf16[544,256]{1,0:T(8,128)(2,1)S(1)}, u32[]{:S(2)}, u32[]{:S(2)}) collective-permute-start(bf16[544,256]{1,0:T(8,128)(2,1)S(1)} %get-tuple-element.39), channel_id=1, source_target_pairs={{0,992},{16,48},{32,0},{48,80},{64,32},{80,112},{96,64},{112,144},... | collective-permute-start | bytes 835592 | tf_op jit(solution)/shard_map/ppermute | solution.py:31
  89.2 8.0 %collective-permute-start.9 = (bf16[672,256]{1,0:T(8,128)(2,1)S(1)}, bf16[672,256]{1,0:T(8,128)(2,1)S(1)}, u32[]{:S(2)}, u32[]{:S(2)}) collective-permute-start(bf16[672,256]{1,0:T(8,128)(2,1)S(1)} %collective-permute-done.7.refs_0_), channel_id=1, source_target_pairs={{0,32},{16,1008},{32,64},{48,16},{64,96},{80,48},{96,128},{112,80}... | collective-permute-start | bytes 1032200 | tf_op jit(solution)/shard_map/ppermute | solution.py:31
  93.1 11.2 %collective-permute-start.6 = (bf16[544,256]{1,0:T(8,128)(2,1)S(1)}, bf16[544,256]{1,0:T(8,128)(2,1)S(1)}, u32[]{:S(2)}, u32[]{:S(2)}) collective-permute-start(bf16[544,256]{1,0:T(8,128)(2,1)S(1)} %collective-permute-done.5.refs_1_), channel_id=1, source_target_pairs={{0,992},{16,48},{32,0},{48,80},{64,32},{80,112},{96,64},{112,144},... | collective-permute-start | bytes 835592 | tf_op jit(solution)/shard_map/ppermute | solution.py:31
  97.2 16.6 %collective-permute-start.10 = (bf16[672,256]{1,0:T(8,128)(2,1)S(1)}, bf16[672,256]{1,0:T(8,128)(2,1)S(1)}, u32[]{:S(2)}, u32[]{:S(2)}) collective-permute-start(bf16[672,256]{1,0:T(8,128)(2,1)S(1)} %collective-permute-done.9.refs_0_), channel_id=1, source_target_pairs={{0,32},{16,1008},{32,64},{48,16},{64,96},{80,48},{96,128},{112,80}... | collective-permute-start | bytes 1032200 | tf_op jit(solution)/shard_map/ppermute | solution.py:31
  104.3 9.5 %collective-permute-start.8 = (bf16[544,256]{1,0:T(8,128)(2,1)S(1)}, bf16[544,256]{1,0:T(8,128)(2,1)S(1)}, u32[]{:S(2)}, u32[]{:S(2)}) collective-permute-start(bf16[544,256]{1,0:T(8,128)(2,1)S(1)} %collective-permute-done.6.refs_1_), channel_id=1, source_target_pairs={{0,992},{16,48},{32,0},{48,80},{64,32},{80,112},{96,64},{112,144},... | collective-permute-start | bytes 835592 | tf_op jit(solution)/shard_map/ppermute | solution.py:31
  114.7 10.2 %collective-permute-start.11 = (bf16[4096,256]{1,0:T(8,128)(2,1)}, bf16[4096,256]{1,0:T(8,128)(2,1)}, u32[]{:S(2)}, u32[]{:S(2)}) collective-permute-start(bf16[4096,256]{1,0:T(8,128)(2,1)} %get-tuple-element.59.near_ref), channel_id=1, source_target_pairs={{0,16},{16,0},{32,48},{48,32},{64,80},{80,64},{96,112},{112,96},{1... | collective-permute-start | bytes 6291464 | tf_op jit(solution)/shard_map/ppermute | solution.py:36
  120.8 12.1 %all-to-all-start.1 = ((f32[16,16,256]{2,1,0:T(8,128)}), f32[16,16,256]{2,1,0:T(8,128)S(1)}, u32[]{:S(2)}, u32[]{:S(2)}) async-start(f32[16,16,256]{2,1,0:T(8,128)} %get-tuple-element.64), calls=%async_computation.1 | async-start | bytes 524288 | tf_op jit(solution)/shard_map/all_to_all | solution.py:414

commit v8 on v7

--- a/solution.py
+++ b/solution.py
@@ -225,24 +225,31 @@
     residue_ref[...] = residue
     direction_ref[...] = residue
 
-    def step(iteration, current):
+    def operate():
         vector = direction_ref[...]
         applied_ref[...] = vector * LAMBDA + gram_part(vector)
         for block in range(blocks):
             span = item_rows(block)
             high = direction_ref[span, :].astype(jnp.bfloat16)
             applied_ref[span, :] = tile_part(applied_ref[span, :], high, block, rows_ref, weight_ref)
+
+    def step_size(current):
+        return current / (jnp.sum(direction_ref[...] * applied_ref[...], axis=1, keepdims=True) + EPSILON)
+
+    def step(iteration, current):
+        operate()
+        size = step_size(current)
         direction = direction_ref[...]
-        applied = applied_ref[...]
-        size = current / (jnp.sum(direction * applied, axis=1, keepdims=True) + EPSILON)
         guess_ref[...] += size * direction
-        residue = residue_ref[...] - size * applied
+        residue = residue_ref[...] - size * applied_ref[...]
         residue_ref[...] = residue
         following = jnp.sum(residue * residue, axis=1, keepdims=True)
         direction_ref[...] = residue + (following / (current + EPSILON)) * direction
         return following
 
-    lax.fori_loop(0, ITERS, step, jnp.sum(residue * residue, axis=1, keepdims=True))
+    current = lax.fori_loop(0, ITERS - 1, step, jnp.sum(residue * residue, axis=1, keepdims=True))
+    operate()
+    guess_ref[...] += step_size(current) * direction_ref[...]
 
 
 def solve_steps(rows, weight, items, started, gram):

time: 141 us -> 141 us (level)
  no operation moved by 1% of the time
where the time goes in v8:
time: 141 us; the launch traced here: 140 us
  starting transfers between devices  77.7 us (55%)
  waiting for transfers between devices  28.3 us (20%)
  Pallas kernels  16.1 us (11%)
  blocking collectives  14.9 us (11%)
  local copies, waits for them, and re-layouts  2.52 us (2%)
    ppermute x8, starting transfers between devices, chip_shift(): return lax.ppermute(value, 'grp', pairs)  46.7 us
    ppermute x4, starting transfers between devices, core_swap(): return lax.ppermute(value, 'grp', pairs)  27.5 us
    ppermute x8, waiting for transfers between devices, chip_shift(): return lax.ppermute(value, 'grp', pairs)  22.9 us
    all_to_all x1, blocking collectives, on_device(): pieces = lax.all_to_all(gram, 'rep', 0, 0, tiled=True)  14.9 us
    pallas_call x1, Pallas kernels, solve_steps(): pl.pallas_call(steps_kernel, out_shape=jax.ShapeDtypeStruct(items.shape,...  7.14 us
    pallas_call x1, Pallas kernels, first_residue(): pl.pallas_call(first_kernel, out_shape=(pltpu.VMEM(rows.shape, rows.dtype...  4.86 us
    all_to_all x1, starting transfers between devices, on_device(): lax.all_to_all(copies.reshape(features, features), 'rep', 0, 0, tiled=True)  3.55 us
    all_to_all x1, waiting for transfers between devices, on_device(): lax.all_to_all(copies.reshape(features, features), 'rep', 0, 0, tiled=True)  3.09 us
  transfers between devices with their start and end apart: 13, of which 11 were waited for; matrix products, arithmetic and copies ran while one was open for 0% of the time, Pallas kernels for 5%

profile of v8, /device:TPU:1, one launch (start us, length us, event | category | flops | bytes accessed | tf_op | source)
XLA Modules:
  0.0 140.0 jit_solution(17540756299897142509)
XLA Ops:
  0.0 0.0 copy-start.1
  0.0 0.9 copy-done.1
  0.9 0.3 local_gram.1
  1.2 14.9 %all_to_all.17 = f32[16,16,256]{2,1,0:T(8,128)S(1)} all-to-all(f32[16,16,256]{2,1,0:T(8,128)S(1)} %bitcast.3), channel_id=1, replica_groups=mesh['grp'=64,'rep'=16] {'rep'}, dimensions={0} | all-to-all | bytes 524288 | tf_op jit(solution)/shard_map/all_to_all | solution.py:380
  16.2 12.4 %collective-permute-start = (bf16[160,256]{1,0:T(8,128)(2,1)S(1)}, bf16[160,256]{1,0:T(8,128)(2,1)S(1)}, u32[]{:S(2)}, u32[]{:S(2)}) collective-permute-start(bf16[160,256]{1,0:T(8,128)(2,1)S(1)} %own.1.mine_ref), channel_id=1, source_target_pairs={{0,16},{16,0},{32,48},{48,32},{64,80},{80,64},{96,112},{112,96},{1... | collective-permute-start | bytes 245768 | tf_op jit(solution)/shard_map/ppermute | solution.py:36
  28.6 0.9 collective-permute-done.other_ref
  29.5 0.0 copy-start.2
  29.5 0.0 copy-start.3
  29.5 13.9 %collective-permute-start.1 = (bf16[288,256]{1,0:T(8,128)(2,1)S(1)}, bf16[288,256]{1,0:T(8,128)(2,1)S(1)}, u32[]{:S(2)}, u32[]{:S(2)}) collective-permute-start(bf16[288,256]{1,0:T(8,128)(2,1)S(1)} %pair.1.refs_0_), channel_id=1, source_target_pairs={{0,224},{16,816},{32,256},{48,848},{64,288},{80,880},{96,320},{112... | collective-permute-start | bytes 442376 | tf_op jit(solution)/shard_map/ppermute | solution.py:31
  43.4 5.2 %collective-permute-done.1.refs_1_ = bf16[288,256]{1,0:T(8,128)(2,1)S(1)} collective-permute-done((bf16[288,256]{1,0:T(8,128)(2,1)S(1)}, bf16[288,256]{1,0:T(8,128)(2,1)S(1)}, u32[]{:S(2)}, u32[]{:S(2)}) %collective-permute-start.1) | collective-permute-done | bytes 147488 | tf_op jit(solution)/shard_map/ppermute | solution.py:31
  48.7 17.9 %collective-permute-start.2 = (bf16[288,256]{1,0:T(8,128)(2,1)S(1)}, bf16[288,256]{1,0:T(8,128)(2,1)S(1)}, u32[]{:S(2)}, u32[]{:S(2)}) collective-permute-start(bf16[288,256]{1,0:T(8,128)(2,1)S(1)} %collective-permute-done.1.refs_1_), channel_id=1, source_target_pairs={{0,224},{16,816},{32,256},{48,848},{64,288},{80,880},{96,320},{112... | collective-permute-start | bytes 442376 | tf_op jit(solution)/shard_map/ppermute | solution.py:31
  66.6 1.9 %collective-permute-start.3 = (bf16[160,256]{1,0:T(8,128)(2,1)S(1)}, bf16[160,256]{1,0:T(8,128)(2,1)S(1)}, u32[]{:S(2)}, u32[]{:S(2)}) collective-permute-start(bf16[160,256]{1,0:T(8,128)(2,1)S(1)} %slice.8), channel_id=1, source_target_pairs={{0,16},{16,0},{32,48},{48,32},{64,80},{80,64},{96,112},{112,96},{1... | collective-permute-start | bytes 245768 | tf_op jit(solution)/shard_map/ppermute | solution.py:36
  68.5 0.0 copy-start
  68.5 1.6 %copy-done = s32[64,64,128]{2,1,0:T(8,128)S(1)} copy-done((s32[64,64,128]{2,1,0:T(8,128)S(1)}, s32[64,64,128]{2,1,0:T(8,128)}, u32[]{:S(2)}) %copy-start) | copy-done | bytes 2097176
  70.1 0.4 item_weights.1.weight_ref
  70.5 0.0 collective-permute-done.3.refs_2_
  70.5 1.6 %collective-permute-done.2.refs_3_ = bf16[288,256]{1,0:T(8,128)(2,1)S(1)} collective-permute-done((bf16[288,256]{1,0:T(8,128)(2,1)S(1)}, bf16[288,256]{1,0:T(8,128)(2,1)S(1)}, u32[]{:S(2)}, u32[]{:S(2)}) %collective-permute-start.2) | collective-permute-done | bytes 147488 | tf_op jit(solution)/shard_map/ppermute | solution.py:31
  72.1 7.1 %collective-permute-start.4 = (bf16[160,256]{1,0:T(8,128)(2,1)S(1)}, bf16[160,256]{1,0:T(8,128)(2,1)S(1)}, u32[]{:S(2)}, u32[]{:S(2)}) collective-permute-start(bf16[160,256]{1,0:T(8,128)(2,1)S(1)} %slice.7), channel_id=1, source_target_pairs={{0,16},{16,0},{32,48},{48,32},{64,80},{80,64},{96,112},{112,96},{1... | collective-permute-start | bytes 245768 | tf_op jit(solution)/shard_map/ppermute | solution.py:36
  79.1 0.9 collective-permute-done.4.refs_4_
  80.1 1.9 %collective-permute-start.7 = (bf16[672,256]{1,0:T(8,128)(2,1)S(1)}, bf16[672,256]{1,0:T(8,128)(2,1)S(1)}, u32[]{:S(2)}, u32[]{:S(2)}) collective-permute-start(bf16[672,256]{1,0:T(8,128)(2,1)S(1)} %get-tuple-element.40.refs_0_), channel_id=1, source_target_pairs={{0,32},{16,1008},{32,64},{48,16},{64,96},{80,48},{96,128},{112,80}... | collective-permute-start | bytes 1032200 | tf_op jit(solution)/shard_map/ppermute | solution.py:31
  82.0 0.0 copy-done.2
  82.1 3.4 %collective-permute-start.5 = (bf16[544,256]{1,0:T(8,128)(2,1)S(1)}, bf16[544,256]{1,0:T(8,128)(2,1)S(1)}, u32[]{:S(2)}, u32[]{:S(2)}) collective-permute-start(bf16[544,256]{1,0:T(8,128)(2,1)S(1)} %get-tuple-element.39), channel_id=1, source_target_pairs={{0,992},{16,48},{32,0},{48,80},{64,32},{80,112},{96,64},{112,144},... | collective-permute-start | bytes 835592 | tf_op jit(solution)/shard_map/ppermute | solution.py:31
  85.4 0.0 copy-done.3
  85.5 0.1 select_reduce_fusion
  85.5 3.7 %collective-permute-done.7.refs_0_ = bf16[672,256]{1,0:T(8,128)(2,1)S(1)} collective-permute-done((bf16[672,256]{1,0:T(8,128)(2,1)S(1)}, bf16[672,256]{1,0:T(8,128)(2,1)S(1)}, u32[]{:S(2)}, u32[]{:S(2)}) %collective-permute-start.7) | collective-permute-done | bytes 344096 | tf_op jit(solution)/shard_map/ppermute | solution.py:31
  89.2 2.0 %collective-permute-start.9 = (bf16[672,256]{1,0:T(8,128)(2,1)S(1)}, bf16[672,256]{1,0:T(8,128)(2,1)S(1)}, u32[]{:S(2)}, u32[]{:S(2)}) collective-permute-start(bf16[672,256]{1,0:T(8,128)(2,1)S(1)} %collective-permute-done.7.refs_0_), channel_id=1, source_target_pairs={{0,32},{16,1008},{32,64},{48,16},{64,96},{80,48},{96,128},{112,80}... | collective-permute-start | bytes 1032200 | tf_op jit(solution)/shard_map/ppermute | solution.py:31
  91.2 0.7 collect_0.1
  92.0 1.1 collective-permute-done.5.refs_1_
  93.1 2.2 %collective-permute-start.6 = (bf16[544,256]{1,0:T(8,128)(2,1)S(1)}, bf16[544,256]{1,0:T(8,128)(2,1)S(1)}, u32[]{:S(2)}, u32[]{:S(2)}) collective-permute-start(bf16[544,256]{1,0:T(8,128)(2,1)S(1)} %collective-permute-done.5.refs_1_), channel_id=1, source_target_pairs={{0,992},{16,48},{32,0},{48,80},{64,32},{80,112},{96,64},{112,144},... | collective-permute-start | bytes 835592 | tf_op jit(solution)/shard_map/ppermute | solution.py:31
  95.3 1.9 %collective-permute-done.9.refs_0_ = bf16[672,256]{1,0:T(8,128)(2,1)S(1)} collective-permute-done((bf16[672,256]{1,0:T(8,128)(2,1)S(1)}, bf16[672,256]{1,0:T(8,128)(2,1)S(1)}, u32[]{:S(2)}, u32[]{:S(2)}) %collective-permute-start.9) | collective-permute-done | bytes 344096 | tf_op jit(solution)/shard_map/ppermute | solution.py:31
  97.2 3.6 %collective-permute-start.10 = (bf16[672,256]{1,0:T(8,128)(2,1)S(1)}, bf16[672,256]{1,0:T(8,128)(2,1)S(1)}, u32[]{:S(2)}, u32[]{:S(2)}) collective-permute-start(bf16[672,256]{1,0:T(8,128)(2,1)S(1)} %collective-permute-done.9.refs_0_), channel_id=1, source_target_pairs={{0,32},{16,1008},{32,64},{48,16},{64,96},{80,48},{96,128},{112,80}... | collective-permute-start | bytes 1032200 | tf_op jit(solution)/shard_map/ppermute | solution.py:31
  100.8 0.8 collect_1.1
  101.6 2.6 %collective-permute-done.6.refs_1_ = bf16[544,256]{1,0:T(8,128)(2,1)S(1)} collective-permute-done((bf16[544,256]{1,0:T(8,128)(2,1)S(1)}, bf16[544,256]{1,0:T(8,128)(2,1)S(1)}, u32[]{:S(2)}, u32[]{:S(2)}) %collective-permute-start.6) | collective-permute-done | bytes 278560 | tf_op jit(solution)/shard_map/ppermute | solution.py:31
  104.3 1.9 %collective-permute-start.8 = (bf16[544,256]{1,0:T(8,128)(2,1)S(1)}, bf16[544,256]{1,0:T(8,128)(2,1)S(1)}, u32[]{:S(2)}, u32[]{:S(2)}) collective-permute-start(bf16[544,256]{1,0:T(8,128)(2,1)S(1)} %collective-permute-done.6.refs_1_), channel_id=1, source_target_pairs={{0,992},{16,48},{32,0},{48,80},{64,32},{80,112},{96,64},{112,144},... | collective-permute-start | bytes 835592 | tf_op jit(solution)/shard_map/ppermute | solution.py:31
  106.2 0.9 collect_2.1
  107.0 6.7 %collective-permute-done.8.down_ref = bf16[544,256]{1,0:T(8,128)(2,1)S(1)} collective-permute-done((bf16[544,256]{1,0:T(8,128)(2,1)S(1)}, bf16[544,256]{1,0:T(8,128)(2,1)S(1)}, u32[]{:S(2)}, u32[]{:S(2)}) %collective-permute-start.8) | collective-permute-done | bytes 278560 | tf_op jit(solution)/shard_map/ppermute | solution.py:31
  113.8 0.0 collective-permute-done.10.up_ref
  113.8 0.9 finish.1
  114.7 6.0 %collective-permute-start.11 = (bf16[4096,256]{1,0:T(8,128)(2,1)}, bf16[4096,256]{1,0:T(8,128)(2,1)}, u32[]{:S(2)}, u32[]{:S(2)}) collective-permute-start(bf16[4096,256]{1,0:T(8,128)(2,1)} %get-tuple-element.59.near_ref), channel_id=1, source_target_pairs={{0,16},{16,0},{32,48},{48,32},{64,80},{80,64},{96,112},{112,96},{1... | collective-permute-start | bytes 6291464 | tf_op jit(solution)/shard_map/ppermute | solution.py:36
  120.8 3.5 %all-to-all-start.1 = ((f32[16,16,256]{2,1,0:T(8,128)}), f32[16,16,256]{2,1,0:T(8,128)S(1)}, u32[]{:S(2)}, u32[]{:S(2)}) async-start(f32[16,16,256]{2,1,0:T(8,128)} %get-tuple-element.64), calls=%async_computation.1 | async-start | bytes 524288 | tf_op jit(solution)/shard_map/all_to_all | solution.py:421
  124.3 0.6 collective-permute-done.11.other_ref
  124.9 4.9 %first_residue.1 = (bf16[4096,256]{1,0:T(8,128)(2,1)S(1)}, f32[512,256]{1,0:T(8,128)}) custom-call(s32[64]{0:T(128)S(1)} %fusion.places_ref, bf16[4096,256]{1,0:T(8,128)(2,1)} %get-tuple-element.59.near_ref, bf16[4096,256]{1,0:T(8,128)(2,1)} %collective-permute-done.11.other_ref, ...), custom_call_target="tpu_custom_call", output_to_operand_aliasing={{0}: (5, {})} | custom-call | tf_op jit(solution)/shard_map/first_residue/pallas_call | solution.py:188
  129.7 3.1 %all-to-all-done.1 = f32[16,16,256]{2,1,0:T(8,128)S(1)} async-done(((f32[16,16,256]{2,1,0:T(8,128)}), f32[16,16,256]{2,1,0:T(8,128)S(1)}, u32[]{:S(2)}, u32[]{:S(2)}) %all-to-all-start.1) | async-done | bytes 262176 | tf_op jit(solution)/shard_map/all_to_all | solution.py:421
  132.8 7.1 %solve_steps.1 = f32[512,256]{1,0:T(8,128)} custom-call(bf16[4096,256]{1,0:T(8,128)(2,1)S(1)} %get-tuple-element.62.rows_ref, bf16[4,128,1024]{2,1,0:T(8,128)(2,1)S(1)} %item_weights.1.weight_ref, f32[512,256]{1,0:T(8,128)} %items_ref.1, f32[512,256]{1,0:T(8,128)} %get-tuple-element.63.started_ref, f32[256,256]{1,0:T(8,128)S(1)} %bitcast.2), custom_call_target="tpu_custom_call" | custom-call | tf_op jit(solution)/shard_map/solve_steps/pallas_call | solution.py:259
  (8 shorter events, 0.2 us)
Async XLA Ops:
  0.0 0.9 copy-start.1
  16.2 13.3 %collective-permute-start = (bf16[160,256]{1,0:T(8,128)(2,1)S(1)}, bf16[160,256]{1,0:T(8,128)(2,1)S(1)}, u32[]{:S(2)}, u32[]{:S(2)}) collective-permute-start(bf16[160,256]{1,0:T(8,128)(2,1)S(1)} %own.1.mine_ref), channel_id=1, source_target_pairs={{0,16},{16,0},{32,48},{48,32},{64,80},{80,64},{96,112},{112,96},{1... | collective-permute-start | bytes 245768 | tf_op jit(solution)/shard_map/ppermute | solution.py:36
  29.5 52.5 %copy-start.2 = (s32[64]{0:T(128)S(1)}, s32[64]{0:T(128)}, u32[]{:S(2)}) copy-start(s32[64]{0:T(128)} %param.8) | copy-start | bytes 772
  29.5 55.9 %copy-start.3 = (s32[32]{0:T(128)S(1)}, s32[32]{0:T(128)}, u32[]{:S(2)}) copy-start(s32[32]{0:T(128)} %constant.83.clone) | copy-start | bytes 388
  29.5 19.1 %collective-permute-start.1 = (bf16[288,256]{1,0:T(8,128)(2,1)S(1)}, bf16[288,256]{1,0:T(8,128)(2,1)S(1)}, u32[]{:S(2)}, u32[]{:S(2)}) collective-permute-start(bf16[288,256]{1,0:T(8,128)(2,1)S(1)} %pair.1.refs_0_), channel_id=1, source_target_pairs={{0,224},{16,816},{32,256},{48,848},{64,288},{80,880},{96,320},{112... | collective-permute-start | bytes 442376 | tf_op jit(solution)/shard_map/ppermute | solution.py:31
  48.7 23.4 %collective-permute-start.2 = (bf16[288,256]{1,0:T(8,128)(2,1)S(1)}, bf16[288,256]{1,0:T(8,128)(2,1)S(1)}, u32[]{:S(2)}, u32[]{:S(2)}) collective-permute-start(bf16[288,256]{1,0:T(8,128)(2,1)S(1)} %collective-permute-done.1.refs_1_), channel_id=1, source_target_pairs={{0,224},{16,816},{32,256},{48,848},{64,288},{80,880},{96,320},{112... | collective-permute-start | bytes 442376 | tf_op jit(solution)/shard_map/ppermute | solution.py:31
  66.6 3.9 %collective-permute-start.3 = (bf16[160,256]{1,0:T(8,128)(2,1)S(1)}, bf16[160,256]{1,0:T(8,128)(2,1)S(1)}, u32[]{:S(2)}, u32[]{:S(2)}) collective-permute-start(bf16[160,256]{1,0:T(8,128)(2,1)S(1)} %slice.8), channel_id=1, source_target_pairs={{0,16},{16,0},{32,48},{48,32},{64,80},{80,64},{96,112},{112,96},{1... | collective-permute-start | bytes 245768 | tf_op jit(solution)/shard_map/ppermute | solution.py:36
  68.5 1.6 %copy-start = (s32[64,64,128]{2,1,0:T(8,128)S(1)}, s32[64,64,128]{2,1,0:T(8,128)}, u32[]{:S(2)}) copy-start(s32[64,64,128]{2,1,0:T(8,128)} %counts_ref.1) | copy-start | bytes 6291460
  72.1 8.0 %collective-permute-start.4 = (bf16[160,256]{1,0:T(8,128)(2,1)S(1)}, bf16[160,256]{1,0:T(8,128)(2,1)S(1)}, u32[]{:S(2)}, u32[]{:S(2)}) collective-permute-start(bf16[160,256]{1,0:T(8,128)(2,1)S(1)} %slice.7), channel_id=1, source_target_pairs={{0,16},{16,0},{32,48},{48,32},{64,80},{80,64},{96,112},{112,96},{1... | collective-permute-start | bytes 245768 | tf_op jit(solution)/shard_map/ppermute | solution.py:36
  80.1 9.1 %collective-permute-start.7 = (bf16[672,256]{1,0:T(8,128)(2,1)S(1)}, bf16[672,256]{1,0:T(8,128)(2,1)S(1)}, u32[]{:S(2)}, u32[]{:S(2)}) collective-permute-start(bf16[672,256]{1,0:T(8,128)(2,1)S(1)} %get-tuple-element.40.refs_0_), channel_id=1, source_target_pairs={{0,32},{16,1008},{32,64},{48,16},{64,96},{80,48},{96,128},{112,80}... | collective-permute-start | bytes 1032200 | tf_op jit(solution)/shard_map/ppermute | solution.py:31
  82.1 11.0 %collective-permute-start.5 = (bf16[544,256]{1,0:T(8,128)(2,1)S(1)}, bf16[544,256]{1,0:T(8,128)(2,1)S(1)}, u32[]{:S(2)}, u32[]{:S(2)}) collective-permute-start(bf16[544,256]{1,0:T(8,128)(2,1)S(1)} %get-tuple-element.39), channel_id=1, source_target_pairs={{0,992},{16,48},{32,0},{48,80},{64,32},{80,112},{96,64},{112,144},... | collective-permute-start | bytes 835592 | tf_op jit(solution)/shard_map/ppermute | solution.py:31
  89.2 8.0 %collective-permute-start.9 = (bf16[672,256]{1,0:T(8,128)(2,1)S(1)}, bf16[672,256]{1,0:T(8,128)(2,1)S(1)}, u32[]{:S(2)}, u32[]{:S(2)}) collective-permute-start(bf16[672,256]{1,0:T(8,128)(2,1)S(1)} %collective-permute-done.7.refs_0_), channel_id=1, source_target_pairs={{0,32},{16,1008},{32,64},{48,16},{64,96},{80,48},{96,128},{112,80}... | collective-permute-start | bytes 1032200 | tf_op jit(solution)/shard_map/ppermute | solution.py:31
  93.1 11.2 %collective-permute-start.6 = (bf16[544,256]{1,0:T(8,128)(2,1)S(1)}, bf16[544,256]{1,0:T(8,128)(2,1)S(1)}, u32[]{:S(2)}, u32[]{:S(2)}) collective-permute-start(bf16[544,256]{1,0:T(8,128)(2,1)S(1)} %collective-permute-done.5.refs_1_), channel_id=1, source_target_pairs={{0,992},{16,48},{32,0},{48,80},{64,32},{80,112},{96,64},{112,144},... | collective-permute-start | bytes 835592 | tf_op jit(solution)/shard_map/ppermute | solution.py:31
  97.2 16.6 %collective-permute-start.10 = (bf16[672,256]{1,0:T(8,128)(2,1)S(1)}, bf16[672,256]{1,0:T(8,128)(2,1)S(1)}, u32[]{:S(2)}, u32[]{:S(2)}) collective-permute-start(bf16[672,256]{1,0:T(8,128)(2,1)S(1)} %collective-permute-done.9.refs_0_), channel_id=1, source_target_pairs={{0,32},{16,1008},{32,64},{48,16},{64,96},{80,48},{96,128},{112,80}... | collective-permute-start | bytes 1032200 | tf_op jit(solution)/shard_map/ppermute | solution.py:31
  104.3 9.5 %collective-permute-start.8 = (bf16[544,256]{1,0:T(8,128)(2,1)S(1)}, bf16[544,256]{1,0:T(8,128)(2,1)S(1)}, u32[]{:S(2)}, u32[]{:S(2)}) collective-permute-start(bf16[544,256]{1,0:T(8,128)(2,1)S(1)} %collective-permute-done.6.refs_1_), channel_id=1, source_target_pairs={{0,992},{16,48},{32,0},{48,80},{64,32},{80,112},{96,64},{112,144},... | collective-permute-start | bytes 835592 | tf_op jit(solution)/shard_map/ppermute | solution.py:31
  114.7 10.2 %collective-permute-start.11 = (bf16[4096,256]{1,0:T(8,128)(2,1)}, bf16[4096,256]{1,0:T(8,128)(2,1)}, u32[]{:S(2)}, u32[]{:S(2)}) collective-permute-start(bf16[4096,256]{1,0:T(8,128)(2,1)} %get-tuple-element.59.near_ref), channel_id=1, source_target_pairs={{0,16},{16,0},{32,48},{48,32},{64,80},{80,64},{96,112},{112,96},{1... | collective-permute-start | bytes 6291464 | tf_op jit(solution)/shard_map/ppermute | solution.py:36
  120.8 12.1 %all-to-all-start.1 = ((f32[16,16,256]{2,1,0:T(8,128)}), f32[16,16,256]{2,1,0:T(8,128)S(1)}, u32[]{:S(2)}, u32[]{:S(2)}) async-start(f32[16,16,256]{2,1,0:T(8,128)} %get-tuple-element.64), calls=%async_computation.1 | async-start | bytes 524288 | tf_op jit(solution)/shard_map/all_to_all | solution.py:421
